TPU v7x, 128 devices: a whole 4x4x4 slice. The times are simulated.
128 devices in a mesh: dp: 16 (over y_lo, x, core), mp: 8 (over z, y_hi).
Axes of the slice: x: 4, y: 4 (y_hi: 2, y_lo: 2; y = y_hi * 2 + y_lo), z: 4, core: 2. Of those that a mesh axis runs over, the one named last changes fastest.
Arguments:
- hidden: bfloat16 [32768, 1536], P(('dp', 'mp')), may hold values from -6 to 6
- grad_out: bfloat16 [32768, 1536], P(('dp', 'mp')), may hold values from -6 to 6
- norm_gain: float32 [1536], replicated, may hold values from 0.5 to 1.5
- w_zx: bfloat16 [1536, 2, 3072], P('dp', None, 'mp'), may hold values from -0.15625 to 0.15625
- w_bc: bfloat16 [1536, 256], P('dp'), may hold values from -0.15625 to 0.15625
- w_dt: bfloat16 [1536, 48], P('dp', 'mp'), may hold values from -0.15625 to 0.15625
- conv_x: float32 [5, 3072], P(None, 'mp'), may hold values from -3 to 3
- conv_bc: float32 [5, 256], replicated, may hold values from -3 to 3
- a_log: float32 [48], P('mp'), may hold values from -5 to 1
- dt_bias: float32 [48], P('mp'), may hold values from -4 to 0
- d_skip: float32 [48], P('mp'), may hold values from 0.5 to 1.5
- gate_gain: float32 [3072], P('mp'), may hold values from 0.5 to 1.5
- w_out: bfloat16 [3072, 1536], P('mp', 'dp'), may hold values from -0.109375 to 0.109375
Outputs:
- result: bfloat16 [32768, 1536], P(('dp', 'mp'))
- grad_hidden: float32 [32768, 1536], P(('dp', 'mp'))
- grad_norm_gain: float32 [1536], replicated
- grad_w_zx: float32 [1536, 2, 3072], P('dp', None, 'mp')
- grad_w_bc: float32 [1536, 256], P('dp')
- grad_w_dt: float32 [1536, 48], P('dp', 'mp')
- grad_conv_x: float32 [5, 3072], P(None, 'mp')
- grad_conv_bc: float32 [5, 256], replicated
- grad_a_log: float32 [48], P('mp')
- grad_dt_bias: float32 [48], P('mp')
- grad_d_skip: float32 [48], P('mp')
- grad_gate_gain: float32 [3072], P('mp')
- grad_w_out: float32 [3072, 1536], P('mp', 'dp')
All inputs are finite; a program needn't handle non-finite values.
Results may differ from a plain program's by a relative error of at most 0.03.
Values may be sent and summed in bfloat16 or wider, within the bound.
A program may use at most 192 MiB of HBM per device.

v0:
```python
import math

import jax
import jax.numpy as jnp
from jax import lax
from jax.sharding import Mesh
from jax.sharding import PartitionSpec as P

HEAD_DIM = 64
SPAN = 256
LEN = 2048
MP = ("mp_0", "mp_1")
DP_MP = ("dp", "mp_0", "mp_1")


EPS = 1e-05
EXACT = lax.Precision.HIGHEST


def rows_first(arrays, axis, dims):
    turned = [jnp.moveaxis(a, dim, 0) for a, dim in zip(arrays, dims)]
    both = jnp.concatenate([t.reshape(len(t), -1) for t in turned], axis=1)
    result, at, outs = (lax.all_gather(both, axis, axis=0, tiled=True), 0, [])
    for t, dim in zip(turned, dims):
        slab = result[:, at : at + t[0].size].reshape(-1, *t.shape[1:])
        outs.append(jnp.moveaxis(slab, 0, dim))
        at += t[0].size
    return tuple(outs)


def from_everyone(array, axis):
    copies = jnp.broadcast_to(array, (lax.axis_size(axis), *array.shape))
    return lax.all_to_all(copies, axis, split_axis=0, concat_axis=0, tiled=True)


def over_copies(array, axis):
    everything = from_everyone(array, axis)
    return jnp.sum(everything, axis=0)


def in_blocks(array, dim, devices):
    before, after = (array.shape[:dim], array.shape[dim + 1 :])
    return jnp.moveaxis(array.reshape(*before, devices, -1, *after), dim, 0)


def sent_and_summed(array, axis, dim):
    pieces = in_blocks(array, dim, lax.axis_size(axis))
    arrived = lax.all_to_all(pieces, axis, split_axis=0, concat_axis=0, tiled=True)
    return arrived.astype(jnp.float32).sum(axis=0)


def own_rows_2(terms, axes):
    total = terms.astype(jnp.bfloat16)
    for axis in axes:
        total = lax.psum_scatter(total, axis, scatter_dimension=0, tiled=True)
    return total.astype(jnp.float32)


def sent_together(arrays, axis, dim, along):
    widths = [math.prod(a.shape[along:]) for a in arrays]
    both = jnp.concatenate(
        [a.reshape(*a.shape[:along], w) for a, w in zip(arrays, widths)], axis=along
    )
    result = lax.psum_scatter(both, axis, scatter_dimension=dim, tiled=True)
    pieces = jnp.split(result, [sum(widths[:k]) for k in range(1, len(widths))], axis=along)
    return tuple(
        (b.reshape(*result.shape[:along], *a.shape[along:]) for a, b in zip(arrays, pieces))
    )


def in_one(arrays, axis):
    flat, at, outs = (jnp.concatenate([a.reshape(-1) for a in arrays]), 0, [])
    total = over_copies(flat, axis)
    for a in arrays:
        outs.append(total[at : at + a.size].reshape(a.shape))
        at += a.size
    return tuple(outs)


def taken_together(array, axis):
    return from_everyone(array, axis).astype(jnp.float32).sum(axis=0)


def causal_conv(values, taps):
    width = taps.shape[0] - 1
    length = values.shape[1]
    padded = jnp.pad(values, ((0, 0), (width - 1, 0), (0, 0)))
    total = taps[width] + padded[:, 0:length] * taps[0]
    for offset in range(1, width):
        total = total + padded[:, offset : offset + length] * taps[offset]
    return jax.nn.silu(total)


def span_step(state, block):
    u_blk, rate_blk, b_blk, c_blk = block
    size = rate_blk.shape[0]
    cum = jnp.cumsum(rate_blk, axis=0).T
    where_causal = jnp.arange(size)[:, None] >= jnp.arange(size)[None, :]
    diff = cum[:, :, None] - cum[:, None, :]
    decay = jnp.where(where_causal, jnp.exp(jnp.where(where_causal, diff, 0.0)), 0.0)
    gram = jnp.dot(c_blk, b_blk.T, precision=EXACT)
    mixing = decay * gram
    inside = jnp.einsum("hts,shp->thp", mixing, u_blk, precision=EXACT)
    carried = jnp.einsum("tn,hpn->thp", c_blk, state, precision=EXACT) * jnp.exp(cum).T[:, :, None]
    tail = jnp.exp(cum[:, -1:] - cum)
    weighted = u_blk * tail.T[:, :, None]
    new_state = state * jnp.exp(cum[:, -1])[:, None, None] + jnp.einsum(
        "shp,sn->hpn", weighted, b_blk, precision=EXACT
    )
    return (new_state, inside + carried)


def ssd_scan(inputs, log_decay, b_vals, c_vals):
    length, heads, channels = inputs.shape
    count = length // SPAN
    blocks = (
        inputs.reshape(count, SPAN, heads, channels),
        log_decay.reshape(count, SPAN, heads),
        b_vals.reshape(count, SPAN, -1),
        c_vals.reshape(count, SPAN, -1),
    )
    state = jnp.zeros((heads, channels, b_vals.shape[-1]), jnp.float32)
    final, outputs = lax.scan(jax.checkpoint(span_step), state, blocks)
    return outputs.reshape(length, heads, channels)


def shards(
    hidden,
    grad_out,
    norm_gain,
    w_zx,
    w_bc,
    w_dt,
    conv_x,
    conv_bc,
    a_log,
    dt_bias,
    d_skip,
    gate_gain,
    w_out,
):
    row_count, width = hidden.shape
    inner_local = gate_gain.shape[0]
    heads_local = a_log.shape[0]
    state_twice = w_bc.shape[1]
    inner_all = inner_local * lax.axis_size(MP)
    resid = hidden.astype(jnp.float32)
    scale = lax.rsqrt(jnp.mean(resid * resid, axis=1, keepdims=True) + EPS)
    unit = resid * scale
    normed = (unit * norm_gain).astype(jnp.bfloat16)
    gathered = lax.all_gather(normed, MP, axis=0, tiled=True)
    zx_full, bc_full, dt_full, out_full = rows_first((w_zx, w_bc, w_dt, w_out), "dp", (0, 0, 0, 1))
    zx_flat = zx_full.reshape(width, 2 * inner_local)
    group_rows = gathered.shape[0]
    seq_count = group_rows // LEN
    proj_zx = jnp.dot(gathered, zx_flat, preferred_element_type=jnp.float32)
    bc_pre = jnp.dot(gathered, bc_full, preferred_element_type=jnp.float32)
    dt_raw = jnp.dot(gathered, dt_full, preferred_element_type=jnp.float32)
    gate_pre = proj_zx[:, :inner_local]
    x_pre = proj_zx[:, inner_local:]

    def conv_piece(x_in, bc_in, taps_x, taps_bc):
        x_out = causal_conv(x_in.reshape(seq_count, LEN, inner_local), taps_x)
        bc_out = causal_conv(bc_in.reshape(seq_count, LEN, state_twice), taps_bc)
        return (x_out.reshape(group_rows, inner_local), bc_out.reshape(group_rows, state_twice))

    (x_conv, bc_conv), conv_back = jax.vjp(conv_piece, x_pre, bc_pre, conv_x, conv_bc)
    x_round = lax.optimization_barrier(x_conv.astype(jnp.bfloat16)).astype(jnp.float32)
    bc_round = lax.optimization_barrier(bc_conv.astype(jnp.bfloat16)).astype(jnp.float32)

    def ssd_piece(x_in, bc_in, dt_in, log_rate, dt_shift, skip_gain):
        step = jax.nn.softplus(dt_in + dt_shift)
        log_decay = (step * -jnp.exp(log_rate)).reshape(seq_count, LEN, heads_local)
        x_heads = x_in.reshape(seq_count, LEN, heads_local, HEAD_DIM)
        inputs = step.reshape(seq_count, LEN, heads_local)[:, :, :, None] * x_heads
        bc_seq = bc_in.reshape(seq_count, LEN, state_twice)
        half = state_twice // 2
        scanned = jax.vmap(ssd_scan)(inputs, log_decay, bc_seq[:, :, :half], bc_seq[:, :, half:])
        return (scanned + skip_gain[:, None] * x_heads).reshape(group_rows, inner_local)

    scan_out, ssd_back = jax.vjp(ssd_piece, x_round, bc_round, dt_raw, a_log, dt_bias, d_skip)
    gate_act = jax.nn.silu(gate_pre)
    gated = scan_out * gate_act
    total_sq = over_copies(jnp.sum(gated * gated, axis=1), MP)
    gate_scale = lax.rsqrt(total_sq / inner_all + EPS)[:, None]
    gate_unit = gated * gate_scale
    out_in = (gate_unit * gate_gain).astype(jnp.bfloat16)
    piece = out_in
    mixed_part = lax.psum_scatter(
        jnp.dot(piece, out_full, preferred_element_type=jnp.float32).astype(jnp.bfloat16),
        MP,
        scatter_dimension=0,
        tiled=True,
    ).astype(jnp.float32)
    result = (resid + mixed_part).astype(jnp.bfloat16)
    cot_full = lax.all_gather(grad_out, MP, axis=0, tiled=True)
    d_outin = jnp.einsum("gd,id->gi", cot_full, out_full, preferred_element_type=jnp.float32)
    piece = cot_full
    grad_w_out = sent_and_summed(
        jnp.einsum("gd,gi->di", piece, out_in, preferred_element_type=jnp.float32).astype(
            jnp.bfloat16
        ),
        "dp",
        0,
    ).T
    gain_part = jnp.sum(d_outin * gate_unit, axis=0)
    d_unit = d_outin * gate_gain
    total_dot = over_copies(jnp.sum(d_unit * gated, axis=1), MP)
    cube = gate_scale * gate_scale * gate_scale
    d_gated = d_unit * gate_scale - gated * cube * (total_dot[:, None] / inner_all)
    sigma = jax.nn.sigmoid(gate_pre)
    d_scan = d_gated * gate_act
    d_gate = d_gated * scan_out * sigma * (1.0 + gate_pre * (1.0 - sigma))
    grad_xc, grad_bcc, grad_step, grad_rate, grad_shift, grad_skip = ssd_back(d_scan)
    bcc_total = lax.psum(grad_bcc.astype(jnp.bfloat16), MP).astype(jnp.float32)
    grad_xpre, grad_bcpre, grad_taps_x, grad_taps_bc = conv_back((grad_xc, bcc_total))
    d_proj = jnp.concatenate([d_gate, grad_xpre], axis=1).astype(jnp.bfloat16)
    d_steps = grad_step.astype(jnp.bfloat16)
    d_bcpre = grad_bcpre.astype(jnp.bfloat16)
    first = jnp.einsum("gk,dk->gd", d_proj, zx_flat, preferred_element_type=jnp.float32)
    d_normed = own_rows_2(
        first + jnp.einsum("gh,dh->gd", d_steps, dt_full, preferred_element_type=jnp.float32), MP
    )
    own_start = lax.axis_index(MP) * row_count
    bc_own = lax.dynamic_slice_in_dim(d_bcpre, own_start, row_count, 0)
    d_normed = d_normed + jnp.einsum(
        "gk,dk->gd", bc_own, bc_full, preferred_element_type=jnp.float32
    )
    grad_zx_all = jnp.einsum(
        "gd,gk->dk", gathered, d_proj, preferred_element_type=jnp.float32
    ).reshape(width, 2, inner_local)
    grad_dt_all = jnp.einsum("gd,gh->dh", gathered, d_steps, preferred_element_type=jnp.float32)
    grad_bc_part = jnp.einsum("gd,gk->dk", normed, bc_own, preferred_element_type=jnp.float32)
    grad_zx, grad_bc_dp, grad_dt = tuple(
        (
            part.astype(jnp.float32)
            for part in sent_together(
                (
                    grad_zx_all.astype(jnp.bfloat16),
                    grad_bc_part.astype(jnp.bfloat16),
                    grad_dt_all.astype(jnp.bfloat16),
                ),
                "dp",
                0,
                1,
            )
        )
    )
    norm_part = jnp.sum(d_normed * unit, axis=0)
    d_in = d_normed * norm_gain
    grad_hidden = scale * (
        d_in - unit * jnp.mean(d_in * unit, axis=1, keepdims=True)
    ) + grad_out.astype(jnp.float32)
    summed = in_one(
        (gain_part, grad_rate, grad_shift, grad_skip, grad_taps_x, grad_taps_bc, norm_part), "dp"
    )
    grad_gate, rate_sum, shift_sum, skip_sum, taps_x_sum, taps_bc_sum, norm_dp = summed
    grad_bc, grad_norm = (
        taken_together(grad_bc_dp.astype(jnp.bfloat16), MP).astype(jnp.float32),
        taken_together(norm_dp.astype(jnp.bfloat16), MP).astype(jnp.float32),
    )
    return (
        result,
        grad_hidden,
        grad_norm,
        grad_zx,
        grad_bc,
        grad_dt,
        taps_x_sum,
        taps_bc_sum,
        rate_sum,
        shift_sum,
        skip_sum,
        grad_gate,
        grad_w_out,
    )


def solution(mesh):
    finer = Mesh(mesh.devices.reshape(mesh.shape["dp"], 4, 2), ("dp", "mp_0", "mp_1"))
    placed = (
        P(DP_MP, None),
        P(DP_MP, None),
        P(),
        P("dp", None, MP),
        P("dp", None),
        P("dp", MP),
        P(None, MP),
        P(),
        P(MP),
        P(MP),
        P(MP),
        P(MP),
        P(MP, "dp"),
    )
    return jax.shard_map(
        shards,
        mesh=finer,
        in_specs=placed,
        out_specs=(
            P(DP_MP, None),
            P(DP_MP, None),
            P(),
            P("dp", None, MP),
            P("dp", None),
            P("dp", MP),
            P(None, MP),
            P(),
            P(MP),
            P(MP),
            P(MP),
            P(MP),
            P(MP, "dp"),
        ),
        check_vma=False,
    )
```

profile of v0, /device:TPU:0, one launch (start us, length us, event | category | flops | bytes accessed | tf_op | source)
XLA Modules:
  0.0 1106.6 jit_solution(10777186744242466459)
XLA Ops:
  16.2 35.6 %all-gather.6.cloned.1.call-done = bf16[1536,1414]{1,0:T(8,128)(2,1)} async-done(((bf16[96,1414]{1,0:T(8,128)(2,1)}), bf16[1536,1414]{1,0:T(8,128)(2,1)}) %all-gather.6.cloned.1.call-update) | async-done | bytes 4343824 | tf_op jit(solution)/shard_map/all_gather | solution.py:23
  51.8 92.0 %all-gather.4.cloned.1.call-done = bf16[2048,1536]{1,0:T(8,128)(2,1)} async-done(((bf16[256,1536]{1,0:T(8,128)(2,1)}), bf16[2048,1536]{1,0:T(8,128)(2,1)}) %all-gather.4.cloned.1.call-update) | async-done | bytes 6291472 | tf_op jit(solution)/shard_map/all_gather | solution.py:151
  143.8 5.3 compare_select_fusion.2
  156.1 5.1 fusion.118
  179.4 167.2 %while.42 = (s32[]{:T(128)}, f32[1,6,64,128]{3,2,1,0:T(8,128)S(1)}, f32[8,1,256,6,64]{2,0,4,3,1:T(8,128)}, f32[8,1,6,64,128]{4,3,2,1,0:T(8,128)}, f32[8,1,256,6]...) while((s32[]{:T(128)}, f32[1,6,64,128]{3,2,1,0:T(8,128)S(1)}, ...), condition=%wide.region_4.5_spmd.clone.clone, body=%wide.region_1.4_spmd.clone.clone.sunk | while | flops 706956288 | bytes 5784972 | solution.py:123
  190.6 9.9 dynamic_update_slice.74
  211.5 9.9 dynamic_update_slice.74
  232.3 9.9 dynamic_update_slice.74
  253.2 9.9 dynamic_update_slice.74
  274.1 9.9 dynamic_update_slice.74
  295.0 9.9 dynamic_update_slice.74
  315.8 9.9 dynamic_update_slice.74
  336.7 9.9 dynamic_update_slice.74
  353.9 6.3 multiply_reduce_fusion.10
  360.2 10.4 all_to_all.34
  370.7 10.2 fusion.107
  392.8 7.8 multiply_reduce_fusion.7
  412.9 304.6 %while.41 = (s32[]{:T(128)}, f32[1,6,64,128]{3,2,1,0:T(8,128)S(1)}, f32[8,1,256,6,64]{2,0,4,3,1:T(8,128)}, f32[8,1,256,6]{2,0,3,1:T(8,128)}, f32[8,1,256,128]{3,...) while((s32[]{:T(128)}, f32[1,6,64,128]{3,2,1,0:T(8,128)S(1)}, ...), condition=%wide.region_22.23_spmd.clone, body=%wide.region_10.22_spmd.clone.sunk | while | flops 1668447232 | bytes 15877655 | solution.py:123
  430.3 7.6 reduce-window.74
  441.3 9.8 dynamic_update_slice.71
  468.3 7.6 reduce-window.74
  479.4 9.8 dynamic_update_slice.71
  506.4 7.6 reduce-window.74
  517.4 9.8 dynamic_update_slice.71
  544.4 7.6 reduce-window.74
  555.5 9.8 dynamic_update_slice.71
  582.5 7.6 reduce-window.74
  593.5 9.8 dynamic_update_slice.71
  620.5 7.6 reduce-window.74
  631.5 9.8 dynamic_update_slice.71
  658.5 7.6 reduce-window.74
  669.6 9.8 dynamic_update_slice.71
  696.6 7.6 reduce-window.74
  707.6 9.8 dynamic_update_slice.71
  727.5 10.1 multiply_reduce_fusion.6
  756.2 6.6 convolution_convert_fusion.1
  762.8 46.4 %all-reduce.26.cloned.1.call-done = bf16[1,2048,256]{2,1,0:T(8,128)(2,1)} async-done(((bf16[1,2048,256]{2,1,0:T(8,128)(2,1)}), bf16[1,2048,256]{2,1,0:T(8,128)(2,1)}) %all-reduce.26.cloned.1.call-update) | async-done | bytes 1048592 | tf_op jit(solution)/shard_map/psum | solution.py:215
  809.3 5.8 multiply_reduce_fusion.14
  821.9 51.2 %reduce-scatter.9.cloned.1.call-done = bf16[512,1536]{1,0:T(8,128)(2,1)} async-done(((bf16[2048,1536]{1,0:T(8,128)(2,1)}), bf16[512,1536]{1,0:T(8,128)(2,1)}) %reduce-scatter.9.cloned.1.call-update) | async-done | bytes 1572880 | tf_op jit(solution)/shard_map/reduce_scatter | solution.py:55
  873.2 6.9 convolution_convert_fusion
  880.1 6.5 fusion.109
  889.1 5.4 all-to-all-start.5
  894.7 55.1 %reduce-scatter.13.cloned.1.call-done = bf16[96,1030]{1,0:T(8,128)(2,1)} async-done(((bf16[1536,1030]{1,0:T(8,128)(2,1)}), bf16[96,1030]{1,0:T(8,128)(2,1)}) %reduce-scatter.13.cloned.1.call-update) | async-done | bytes 197776
  951.4 5.6 all-to-all-start.4
  960.5 9.6 all-to-all-done.4
  970.8 11.8 %reduce-scatter.11.cloned.1.call-done = bf16[256,1536]{1,0:T(8,128)(2,1)} async-done(((bf16[512,1536]{1,0:T(8,128)(2,1)}), bf16[256,1536]{1,0:T(8,128)(2,1)}) %reduce-scatter.11.cloned.1.call-update) | async-done | bytes 786448 | tf_op jit(solution)/shard_map/reduce_scatter | solution.py:55
  989.2 93.3 %reduce-scatter.7.cloned.1.call-done = bf16[256,1536]{1,0:T(8,128)(2,1)} async-done(((bf16[2048,1536]{1,0:T(8,128)(2,1)}), bf16[256,1536]{1,0:T(8,128)(2,1)}) %reduce-scatter.7.cloned.1.call-update) | async-done | bytes 786448 | tf_op jit(solution)/shard_map/reduce_scatter | solution.py:189
  1093.8 5.1 all-to-all-done.3
  (851 shorter events, 378.8 us)
Async XLA Ops:
  7.2 8.8 copy-start.50
  7.2 8.9 copy-start.47
  7.2 136.5 %copy-start.54 = (f32[6]{0:T(128)S(1)}, f32[6]{0:T(128)}, u32[]{:S(2)}) copy-start(f32[6]{0:T(128)} %param.26) | copy-start | bytes 76
  7.2 44.6 %all-gather.6.cloned.1.call-start = ((), (), s32[]{:S(2)}) async-start(), calls=%async_computation.11 | async-start | bytes 5013504 | tf_op jit(solution)/shard_map/all_gather | solution.py:23
  10.8 133.0 %all-gather.4.cloned.1.call-start = ((), (), s32[]{:S(2)}) async-start(), calls=%async_computation.10 | async-start | bytes 7077888 | tf_op jit(solution)/shard_map/all_gather | solution.py:151
  15.1 355.6 %all-gather.8.cloned.1.call-start = ((), (), s32[]{:S(2)}) async-start(), calls=%async_computation.13 | async-start | bytes 7077888 | tf_op jit(solution)/shard_map/all_gather | solution.py:196
  15.9 133.2 %copy-start.48 = (f32[6]{0:T(128)}, f32[6]{0:T(128)S(1)}, u32[]{:S(2)}) copy-start(f32[6]{0:T(128)S(1)} %exponential_negate_fusion) | copy-start | bytes 76
  16.1 337.8 %copy-start.25 = (f32[384]{0:T(512)}, f32[384]{0:T(512)S(1)}, u32[]{:S(2)}) copy-start(f32[384]{0:T(512)S(1)} %mul.734) | copy-start | bytes 4612
  16.1 135.7 %copy-start.36 = (f32[1,256]{1,0:T(1,128)}, f32[1,256]{1,0:T(1,128)S(1)}, u32[]{:S(2)}) copy-start(f32[1,256]{1,0:T(1,128)S(1)} %get-tuple-element.870) | copy-start | bytes 3076
  16.1 135.7 %copy-start.38 = (f32[1,256]{1,0:T(1,128)}, f32[1,256]{1,0:T(1,128)S(1)}, u32[]{:S(2)}) copy-start(f32[1,256]{1,0:T(1,128)S(1)} %get-tuple-element.871) | copy-start | bytes 3076
  16.1 135.7 %copy-start.40 = (f32[1,256]{1,0:T(1,128)}, f32[1,256]{1,0:T(1,128)S(1)}, u32[]{:S(2)}) copy-start(f32[1,256]{1,0:T(1,128)S(1)} %get-tuple-element.872) | copy-start | bytes 3076
  16.1 135.7 %copy-start.42 = (f32[1,256]{1,0:T(1,128)}, f32[1,256]{1,0:T(1,128)S(1)}, u32[]{:S(2)}) copy-start(f32[1,256]{1,0:T(1,128)S(1)} %get-tuple-element.873) | copy-start | bytes 3076
  16.1 145.3 %copy-start.28 = (f32[384]{0:T(512)}, f32[384]{0:T(512)S(1)}, u32[]{:S(2)}) copy-start(f32[384]{0:T(512)S(1)} %get-tuple-element.776) | copy-start | bytes 4612
  16.2 145.3 %copy-start.30 = (f32[384]{0:T(512)}, f32[384]{0:T(512)S(1)}, u32[]{:S(2)}) copy-start(f32[384]{0:T(512)S(1)} %get-tuple-element.777) | copy-start | bytes 4612
  16.2 145.3 %copy-start.32 = (f32[384]{0:T(512)}, f32[384]{0:T(512)S(1)}, u32[]{:S(2)}) copy-start(f32[384]{0:T(512)S(1)} %get-tuple-element.778) | copy-start | bytes 4612
  16.2 145.3 %copy-start.34 = (f32[384]{0:T(512)}, f32[384]{0:T(512)S(1)}, u32[]{:S(2)}) copy-start(f32[384]{0:T(512)S(1)} %get-tuple-element.779) | copy-start | bytes 4612
  353.9 16.8 %copy-start.51 = (f32[384]{0:T(512)S(1)}, f32[384]{0:T(512)}, u32[]{:S(2)}) copy-start(f32[384]{0:T(512)} %param.28) | copy-start | bytes 4612
  381.5 11.1 %all-to-all-start.1 = ((f32[8,1,2048]{2,1,0:T(1,128)}), f32[8,1,2048]{2,1,0:T(1,128)S(1)}, u32[]{:S(2)}, u32[]{:S(2)}) async-start(f32[8,1,2048]{2,1,0:T(1,128)} %broadcast_in_dim.204), calls=%async_computation.2 | async-start | bytes 131072 | tf_op jit(solution)/shard_map/all_to_all | solution.py:33
  384.9 424.4 %all-reduce.26.cloned.1.call-start = ((), (), s32[]{:S(2)}) async-start(), calls=%async_computation.16 | async-start | bytes 2097152 | tf_op jit(solution)/shard_map/psum | solution.py:215
  429.2 21.9 %copy-start.21 = (f32[8,1,256,6]{2,0,3,1:T(8,128)S(1)}, f32[8,1,256,6]{2,0,3,1:T(8,128)}, u32[]{:S(2)}) copy-start(f32[8,1,256,6]{2,0,3,1:T(8,128)} %copy-done.20) | copy-start | bytes 147460 | tf_op jit(solution)/shard_map/transpose(jvp(vmap()))/while
  467.2 22.0 %copy-start.21 = (f32[8,1,256,6]{2,0,3,1:T(8,128)S(1)}, f32[8,1,256,6]{2,0,3,1:T(8,128)}, u32[]{:S(2)}) copy-start(f32[8,1,256,6]{2,0,3,1:T(8,128)} %copy-done.20) | copy-start | bytes 147460 | tf_op jit(solution)/shard_map/transpose(jvp(vmap()))/while
  505.3 21.9 %copy-start.21 = (f32[8,1,256,6]{2,0,3,1:T(8,128)S(1)}, f32[8,1,256,6]{2,0,3,1:T(8,128)}, u32[]{:S(2)}) copy-start(f32[8,1,256,6]{2,0,3,1:T(8,128)} %copy-done.20) | copy-start | bytes 147460 | tf_op jit(solution)/shard_map/transpose(jvp(vmap()))/while
  543.3 22.0 %copy-start.21 = (f32[8,1,256,6]{2,0,3,1:T(8,128)S(1)}, f32[8,1,256,6]{2,0,3,1:T(8,128)}, u32[]{:S(2)}) copy-start(f32[8,1,256,6]{2,0,3,1:T(8,128)} %copy-done.20) | copy-start | bytes 147460 | tf_op jit(solution)/shard_map/transpose(jvp(vmap()))/while
  581.4 21.9 %copy-start.21 = (f32[8,1,256,6]{2,0,3,1:T(8,128)S(1)}, f32[8,1,256,6]{2,0,3,1:T(8,128)}, u32[]{:S(2)}) copy-start(f32[8,1,256,6]{2,0,3,1:T(8,128)} %copy-done.20) | copy-start | bytes 147460 | tf_op jit(solution)/shard_map/transpose(jvp(vmap()))/while
  619.4 22.0 %copy-start.21 = (f32[8,1,256,6]{2,0,3,1:T(8,128)S(1)}, f32[8,1,256,6]{2,0,3,1:T(8,128)}, u32[]{:S(2)}) copy-start(f32[8,1,256,6]{2,0,3,1:T(8,128)} %copy-done.20) | copy-start | bytes 147460 | tf_op jit(solution)/shard_map/transpose(jvp(vmap()))/while
  657.4 22.0 %copy-start.21 = (f32[8,1,256,6]{2,0,3,1:T(8,128)S(1)}, f32[8,1,256,6]{2,0,3,1:T(8,128)}, u32[]{:S(2)}) copy-start(f32[8,1,256,6]{2,0,3,1:T(8,128)} %copy-done.20) | copy-start | bytes 147460 | tf_op jit(solution)/shard_map/transpose(jvp(vmap()))/while
  695.5 21.9 %copy-start.21 = (f32[8,1,256,6]{2,0,3,1:T(8,128)S(1)}, f32[8,1,256,6]{2,0,3,1:T(8,128)}, u32[]{:S(2)}) copy-start(f32[8,1,256,6]{2,0,3,1:T(8,128)} %copy-done.20) | copy-start | bytes 147460 | tf_op jit(solution)/shard_map/transpose(jvp(vmap()))/while
  720.3 152.8 %reduce-scatter.9.cloned.1.call-start = ((), (), s32[]{:S(2)}) async-start(), calls=%async_computation.14 | async-start | bytes 7864320 | tf_op jit(solution)/shard_map/reduce_scatter | solution.py:55
  727.4 10.1 copy-start.29
  727.4 10.1 copy-start.31
  727.4 10.1 copy-start.33
  727.5 10.1 copy-start.35
  727.5 12.0 %slice-start.3 = ((s8[4718592]{0:T(1024)(128)(4,1)}), s8[4194304]{0:T(1024)(128)(4,1)S(1)}, s32[]{:S(2)}) async-start(s8[4718592]{0:T(1024)(128)(4,1)} %bitcast.576), calls=%async_computation.21 | async-start | bytes 8388608
  750.7 199.1 %reduce-scatter.13.cloned.1.call-start = ((), (), s32[]{:S(2)}) async-start(), calls=%async_computation.17 | async-start | bytes 3760128
  821.8 51.4 %copy-start.10 = (f32[2048,384]{1,0:T(8,128)S(1)}, f32[2048,384]{1,0:T(8,128)}, u32[]{:S(2)}) copy-start(f32[2048,384]{1,0:T(8,128)} %get-tuple-element.833) | copy-start | bytes 9437188
  821.8 51.4 %copy-start.53 = (f32[384]{0:T(512)S(1)}, f32[384]{0:T(512)}, u32[]{:S(2)}) copy-start(f32[384]{0:T(512)} %param.28) | copy-start | bytes 4612
  821.8 160.7 %reduce-scatter.11.cloned.1.call-start = ((), (), s32[]{:S(2)}) async-start(), calls=%async_computation.15 | async-start | bytes 2359296 | tf_op jit(solution)/shard_map/reduce_scatter | solution.py:55
  873.1 209.4 %reduce-scatter.7.cloned.1.call-start = ((), (), s32[]{:S(2)}) async-start(), calls=%async_computation.12 | async-start | bytes 7077888 | tf_op jit(solution)/shard_map/reduce_scatter | solution.py:189
  889.1 93.5 %copy-start.12 = (bf16[256,1536]{1,0:T(8,128)(2,1)S(1)}, bf16[256,1536]{1,0:T(8,128)(2,1)}, u32[]{:S(2)}) copy-start(bf16[256,1536]{1,0:T(8,128)(2,1)} %param.17) | copy-start | bytes 2359300
  889.1 93.5 %copy-start.24 = (f32[1536]{0:T(1024)S(1)}, f32[1536]{0:T(1024)}, u32[]{:S(2)}) copy-start(f32[1536]{0:T(1024)} %param.19) | copy-start | bytes 18436
  889.1 93.5 %copy-start.45 = (f32[256]{0:T(256)S(1)}, f32[256]{0:T(256)}, u32[]{:S(2)}) copy-start(f32[256]{0:T(256)} %copy-done.44) | copy-start | bytes 3076
  889.1 61.5 %all-to-all-start.5 = ((bf16[16,96,384]{2,1,0:T(8,128)(2,1)}), bf16[16,96,384]{2,1,0:T(8,128)(2,1)S(1)}, u32[]{:S(2)}, u32[]{:S(2)}) async-start(bf16[16,96,384]{2,1,0:T(8,128)(2,1)} %bitcast.34), calls=%async_computation.8 | async-start | bytes 2359296 | tf_op jit(solution)/shard_map/all_to_all | solution.py:48
  949.8 9.7 slice-start.2
  951.4 18.7 %all-to-all-start.4 = ((bf16[8,96,256]{2,1,0:T(8,128)(2,1)}), bf16[8,96,256]{2,1,0:T(8,128)(2,1)S(1)}, u32[]{:S(2)}, u32[]{:S(2)}) async-start(bf16[8,96,256]{2,1,0:T(8,128)(2,1)} %broadcast_in_dim.218), calls=%async_computation.7 | async-start | bytes 786432 | tf_op jit(solution)/shard_map/all_to_all | solution.py:33
  958.0 26.6 %copy-start.55 = (f32[384]{0:T(512)S(1)}, f32[384]{0:T(512)}, u32[]{:S(2)}) copy-start(f32[384]{0:T(512)} %get-tuple-element.758) | copy-start | bytes 4612
  960.5 122.0 %copy-start.13 = (bf16[256,1536]{1,0:T(8,128)(2,1)S(1)}, bf16[256,1536]{1,0:T(8,128)(2,1)}, u32[]{:S(2)}) copy-start(bf16[256,1536]{1,0:T(8,128)(2,1)} %param.18) | copy-start | bytes 2359300
  985.7 100.1 %all-to-all-start.2 = ((f32[16,1,5138]{2,1,0:T(1,128)}), f32[16,1,5138]{2,1,0:T(1,128)S(1)}, u32[]{:S(2)}, u32[]{:S(2)}) async-start(f32[16,1,5138]{2,1,0:T(1,128)} %broadcast_in_dim.216), calls=%async_computation.5 | async-start | bytes 671744 | tf_op jit(solution)/shard_map/all_to_all | solution.py:33
  1087.9 11.0 all-to-all-start.3
  (43 other events, 161.5 us)
Sparse Core Ops, SparseCore 0:
  10.9 40.8 all-gather.5
  54.7 89.0 all-gather.3
  146.1 86.7 all-gather.7
  720.4 88.7 all-reduce.25
  811.5 61.5 reduce-scatter.8
  875.4 74.3 reduce-scatter.12
  952.1 30.3 reduce-scatter.10
  986.9 95.6 reduce-scatter.6
where the time goes:
time: 1120 us; the launch traced here: 1110 us
  waiting for transfers between devices  406 us (36%)
  local copies, waits for them, and re-layouts  314 us (28%)
  matrix products  183 us (16%)
  other arithmetic  154 us (14%)
  starting transfers between devices  21.6 us (2%)
  between operations  15.3 us (1%)
    dynamic_update_slice x56, local copies, waits for them, and re-layouts, ssd_scan(): final, outputs = lax.scan(jax.checkpoint(span_step), state, blocks)  181 us
    reduce_scatter x1, waiting for transfers between devices, shards(): lax.psum_scatter(jnp.dot(piece, out_full, preferred_element_type=jnp.floa...  93.3 us
    all_gather x1, waiting for transfers between devices, shards(): gathered = lax.all_gather(normed, MP, axis=0, tiled=True)  92 us
    another operation x65, other arithmetic  90.8 us
    reduce_scatter x2, waiting for transfers between devices, own_rows_2(): total = lax.psum_scatter(total, axis, scatter_dimension=0, tiled=True)  63 us
    unnamed x9, waiting for transfers between devices  55.9 us
    dot_general x24, matrix products, span_step(): inside = jnp.einsum('hts,shp->thp', mixing, u_blk, precision=EXACT)  53.2 us
    psum x1, waiting for transfers between devices, shards(): bcc_total = lax.psum(grad_bcc.astype(jnp.bfloat16), MP).astype(jnp.float32)  46.4 us
  transfers between devices with their start and end apart: 13, of which 10 were waited for; matrix products, arithmetic and copies ran while one was open for 27% of the time, Pallas kernels for 0%

commit v1 on v0

v1 whole, which is shorter than its diff:
```python
import jax
import jax.numpy as jnp
from jax import lax
from jax.experimental import pallas as pl
from jax.experimental.pallas import tpu as pltpu
from jax.sharding import Mesh
from jax.sharding import PartitionSpec as P

MP = ("z", "yhi")
DP = ("ylo", "x", "core")
DP_MP = DP + MP
BLOCKS = 8
F32 = jnp.float32
BF16 = jnp.bfloat16
ROWS = 256
WIDTH = 1536
GROUPS = 8
COLS = 384
HEADS = 6
HALO = 16
EPS = 1e-05
INNER = GROUPS * COLS
VMEM_LIMIT = 56 * 2**20


def dot(a, b, contract=(1, 0), precision=None):
    return lax.dot_general(
        a, b, (((contract[0],), (contract[1],)), ((), ())),
        preferred_element_type=F32, precision=precision,
    )


def spread(per_head):
    rows = per_head.shape[0]
    low = lax.broadcasted_iota(jnp.int32, (rows, 128), 1) < 64
    tiles = [
        jnp.where(low, per_head[:, 2 * i : 2 * i + 1], per_head[:, 2 * i + 1 : 2 * i + 2])
        for i in range(COLS // 128)
    ]
    return jnp.concatenate(tiles, axis=1)


def gathered_heads(values):
    rows = values.shape[0]
    low = lax.broadcasted_iota(jnp.int32, (rows, 128), 1) < 64
    lane = lax.broadcasted_iota(jnp.int32, (rows, 8), 1)
    out = jnp.zeros((rows, 8), F32)
    for i in range(COLS // 128):
        tile = values[:, 128 * i : 128 * i + 128]
        first = jnp.sum(jnp.where(low, tile, 0.0), axis=1, keepdims=True)
        both = jnp.sum(tile, axis=1, keepdims=True)
        out = jnp.where(lane == 2 * i, first, out)
        out = jnp.where(lane == 2 * i + 1, both - first, out)
    return out


def softplus(v):
    return jnp.maximum(v, 0.0) + jnp.log1p(jnp.exp(-jnp.abs(v)))


def conv_pre(ext, taps):
    total = taps[4:5]
    for j in range(4):
        total = total + ext[HALO - 3 + j : HALO - 3 + j + ROWS] * taps[j : j + 1]
    return total


def conv_transposed(ext, taps, rows=ROWS):
    total = ext[3 : 3 + rows] * taps[0:1]
    for j in range(1, 4):
        total = total + ext[3 - j : 3 - j + rows] * taps[j : j + 1]
    return total


def conv_grads(dpre, ext, sixth, seventh):
    rows = [
        jnp.sum(dpre * ext[HALO - 3 + j : HALO - 3 + j + ROWS], axis=0, keepdims=True)
        for j in range(4)
    ]
    rows.append(jnp.sum(dpre, axis=0, keepdims=True))
    rows += [sixth, seventh, jnp.zeros((1, dpre.shape[1]), F32)]
    return jnp.concatenate(rows, axis=0)


def triangle(upper):
    row = lax.broadcasted_iota(jnp.int32, (ROWS, ROWS), 0)
    col = lax.broadcasted_iota(jnp.int32, (ROWS, ROWS), 1)
    return row <= col if upper else row >= col


def first_kernel(hid, halo, cot, gain, w_small, taps_bc, a_log, dt_bias,
                 normed, normed_t, cot_t, bc_pre, bc_conv, steps, cum_col, step_col, cum_row, step_row):
    for at, part in ((0, halo), (HALO, hid)):
        v = part[...].astype(F32)
        r = lax.rsqrt(jnp.mean(v * v, axis=1, keepdims=True) + EPS)
        normed[at : at + part.shape[0], :] = (v * r * gain[...]).astype(BF16)
    normed_t[...] = normed[HALO:, :].T.reshape(8, 2, 96, ROWS)
    cot_t[...] = cot[...].T.reshape(8, 2, 96, ROWS)
    small = dot(normed[...], w_small[...])
    bc_pre[...] = small[:, :256]
    pre = conv_pre(small[:, :256], taps_bc[...])
    bc_conv[...] = (pre * jax.nn.sigmoid(pre)).astype(BF16)
    shifted = small[HALO:, 256:384] + dt_bias[...]
    steps[...] = shifted
    step = softplus(shifted)
    decay = -step * jnp.exp(a_log[...])
    tri = triangle(False).astype(F32)
    cum = dot(tri, decay, precision=lax.Precision.HIGHEST)
    cum_t = cum.T
    step_t = step.T
    for m in range(GROUPS):
        cum_col[m] = cum[:, HEADS * m : HEADS * m + 8]
        step_col[m] = step[:, HEADS * m : HEADS * m + 8]
        cum_row[m] = cum_t[HEADS * m : HEADS * m + 8]
        step_row[m] = step_t[HEADS * m : HEADS * m + 8]


def sds(*shape, dtype=F32):
    return jax.ShapeDtypeStruct(shape, dtype)


def params():
    return pltpu.CompilerParams(vmem_limit_bytes=VMEM_LIMIT)


def first(hid, halo, cot, gain, w_small, taps_bc, a_log, dt_bias):
    return pl.pallas_call(
        first_kernel,
        out_shape=(
            sds(HALO + ROWS, WIDTH, dtype=BF16), sds(8, 2, 96, ROWS, dtype=BF16), sds(8, 2, 96, ROWS, dtype=BF16),
            sds(HALO + ROWS, 256), sds(ROWS, 256, dtype=BF16),
            sds(ROWS, 128), sds(GROUPS, ROWS, 8), sds(GROUPS, ROWS, 8),
            sds(GROUPS, 8, ROWS), sds(GROUPS, 8, ROWS),
        ),
        compiler_params=params(),
        name="norm_and_small_projections",
    )(hid, halo, cot, gain, w_small, taps_bc, a_log, dt_bias)


def whole(*shape):
    return pl.BlockSpec(shape, lambda m: (0,) * len(shape))


def lead(*shape):
    return pl.BlockSpec((None, *shape), lambda m: (m,) + (0,) * len(shape))


def weight(item):
    return pl.BlockSpec((None, None, WIDTH, COLS), lambda m: (item, m, 0, 0))


def second_kernel(normed, w, taps, bc_conv, cum_col, step_col, x_pre, x_conv, state):
    ext = dot(normed[...], w[...])
    x_pre[...] = ext
    pre = conv_pre(ext, taps[...])
    xc = (pre * jax.nn.sigmoid(pre)).astype(BF16)
    x_conv[...] = xc
    cum = cum_col[...]
    weights = step_col[...] * jnp.exp(cum[ROWS - 1 : ROWS] - cum)
    weighted = (xc.astype(F32) * spread(weights)).astype(BF16)
    state[...] = dot(weighted, bc_conv[:, :128], (0, 0)).astype(BF16)


def second(normed, w_all, taps, bc_conv, cum_col, step_col):
    return pl.pallas_call(
        second_kernel,
        grid=(GROUPS,),
        in_specs=[whole(HALO + ROWS, WIDTH), weight(0), lead(8, COLS), whole(ROWS, 256), lead(ROWS, 8), lead(ROWS, 8)],
        out_specs=(lead(HALO + ROWS, COLS), lead(ROWS, COLS), lead(COLS, 128)),
        out_shape=(sds(GROUPS, HALO + ROWS, COLS), sds(GROUPS, ROWS, COLS, dtype=BF16), sds(GROUPS, COLS, 128, dtype=BF16)),
        compiler_params=params(),
        name="x_projection_and_state",
    )(normed, w_all, taps, bc_conv, cum_col, step_col)


def third_kernel(normed, cot, w_z, w_o, x_conv, bc_conv, cum_col, cum_row, step_row, state, skip, gain,
                 z_out, y_out, d_out, square, inner, gram):
    @pl.when(pl.program_id(0) == 0)
    def _():
        g = dot(bc_conv[:, 128:], bc_conv[:, :128], (1, 1))
        gram[...] = jnp.where(triangle(False), g, 0.0)
        square[...] = jnp.zeros_like(square)
        inner[...] = jnp.zeros_like(inner)

    xc = x_conv[...]
    cum = cum_col[...]
    parts = []
    for h in range(HEADS):
        decay = jnp.exp(jnp.minimum(cum[:, h : h + 1] - cum_row[h : h + 1, :], 0.0))
        mixing = (decay * gram[...] * step_row[h : h + 1, :]).astype(BF16)
        parts.append(dot(mixing, xc[:, 64 * h : 64 * h + 64]))
    inside = jnp.concatenate(parts, axis=1)
    carried = dot(bc_conv[:, 128:], state[...], (1, 1))
    y = inside + spread(jnp.exp(cum)) * carried + skip[...] * xc.astype(F32)
    z = dot(normed[HALO:, :], w_z[...])
    d = dot(cot[...], w_o[...])
    gated = y * (z * jax.nn.sigmoid(z))
    z_out[...] = z
    y_out[...] = y
    d_out[...] = d
    sq = gated * gated
    ip = d * gain[...] * gated
    square[...] += sq[:, :128] + sq[:, 128:256] + sq[:, 256:]
    inner[...] += ip[:, :128] + ip[:, 128:256] + ip[:, 256:]


def third(normed, cot, w_all, x_conv, bc_conv, cum_col, cum_row, step_row, state, skip, gain):
    return pl.pallas_call(
        third_kernel,
        grid=(GROUPS,),
        in_specs=[whole(HALO + ROWS, WIDTH), whole(ROWS, WIDTH), weight(1), weight(2), lead(ROWS, COLS), whole(ROWS, 256),
                  lead(ROWS, 8), lead(8, ROWS), lead(8, ROWS), lead(COLS, 128), lead(1, COLS), lead(1, COLS)],
        out_specs=(lead(ROWS, COLS), lead(ROWS, COLS), lead(ROWS, COLS), whole(ROWS, 128), whole(ROWS, 128)),
        out_shape=(sds(GROUPS, ROWS, COLS), sds(GROUPS, ROWS, COLS), sds(GROUPS, ROWS, COLS), sds(ROWS, 128), sds(ROWS, 128)),
        scratch_shapes=[pltpu.VMEM((ROWS, ROWS), F32)],
        compiler_params=params(),
        name="scan_and_gate",
    )(normed, cot, w_all, w_all, x_conv, bc_conv, cum_col, cum_row, step_row, state, skip, gain)


def fourth_kernel(hid, square, inner, z_in, y_in, d_in, gain, w_o, x_conv, bc_conv, cum_col, step_col, cum_row, step_row,
                  state, skip,
                  result, out_in, d_z, d_x, d_state, d_cum, d_step, d_bc, gain_part, skip_part,
                  gram, d_gram, acc, d_c):
    step_id = pl.program_id(0)

    @pl.when(step_id == 0)
    def _():
        g = dot(bc_conv[:, 128:], bc_conv[:, :128], (1, 1))
        gram[...] = jnp.where(triangle(False), g, 0.0)
        d_gram[...] = jnp.zeros_like(d_gram)
        acc[...] = jnp.zeros_like(acc)
        d_c[...] = jnp.zeros_like(d_c)

    z = z_in[...]
    y = y_in[...]
    d = d_in[...]
    sig = jax.nn.sigmoid(z)
    act = z * sig
    gated = y * act
    r2 = lax.rsqrt(jnp.sum(square[...], axis=1, keepdims=True) / INNER + EPS)
    total = jnp.sum(inner[...], axis=1, keepdims=True)
    unit = gated * r2
    o = (unit * gain[...]).astype(BF16)
    out_in[...] = o
    acc[...] += dot(o, w_o[...], (1, 1))
    gain_part[...] = jnp.sum(d * unit, axis=0, keepdims=True)
    d_gated = r2 * (d * gain[...]) - gated * (r2 * r2 * r2 * (total / INNER))
    dy = d_gated * act
    d_z[...] = (d_gated * y * sig * (1.0 + z * (1.0 - sig))).astype(BF16)

    xc = x_conv[...]
    xf = xc.astype(F32)
    cum = cum_col[...]
    step = step_col[...]
    dyb = dy.astype(BF16)
    c_mat = bc_conv[:, 128:]
    skip_part[...] = jnp.sum(dy * xf, axis=0, keepdims=True)
    grown = spread(jnp.exp(cum))
    dye = (grown * dy).astype(BF16)
    d_c[...] += dot(dye, state[...])
    d_state[...] = dot(dye, c_mat, (0, 0)).astype(BF16)
    carried = grown * dot(c_mat, state[...], (1, 1))
    d_cum_col = gathered_heads(dy * carried)
    lane = lax.broadcasted_iota(jnp.int32, (ROWS, 8), 1)
    parts = []
    cols = []
    for h in range(HEADS):
        xh = xc[:, 64 * h : 64 * h + 64]
        dyh = dyb[:, 64 * h : 64 * h + 64]
        decay = jnp.exp(jnp.minimum(cum[:, h : h + 1] - cum_row[h : h + 1, :], 0.0))
        d_mix = dot(dyh, xh, (1, 1))
        grown_row = step_row[h : h + 1, :]
        plain = decay * gram[...]
        r = plain * d_mix
        cols.append(jnp.sum(r, axis=0, keepdims=True))
        row = jnp.sum(r * grown_row, axis=1, keepdims=True)
        d_cum_col = jnp.where(lane == h, d_cum_col + row, d_cum_col)
        d_gram[...] += decay * d_mix * grown_row
        parts.append(dot((plain * grown_row).astype(BF16), dyh, (0, 0)))
    cols.append(jnp.zeros((2, ROWS), F32))
    cols = jnp.concatenate(cols, axis=0).T
    d_x[...] = jnp.concatenate(parts, axis=1) + skip[...] * dy
    d_step[...] = cols
    d_cum[...] = d_cum_col - cols * step

    @pl.when(step_id == GROUPS - 1)
    def _():
        result[...] = (hid[...].astype(F32) + acc[...]).astype(BF16)
        dg = jnp.where(triangle(False), d_gram[...], 0.0).astype(BF16)
        d_bc[:, :128] = dot(dg, c_mat, (0, 0))
        d_bc[:, 128:] = d_c[...] + dot(dg, bc_conv[:, :128])


def fourth(hid, square, inner, z, y, d, gain, w_all, x_conv, bc_conv, cum_col, step_col, cum_row, step_row, state, skip):
    return pl.pallas_call(
        fourth_kernel,
        grid=(GROUPS,),
        in_specs=[whole(ROWS, WIDTH), whole(ROWS, 128), whole(ROWS, 128), lead(ROWS, COLS), lead(ROWS, COLS), lead(ROWS, COLS),
                  lead(1, COLS), weight(2), lead(ROWS, COLS), whole(ROWS, 256), lead(ROWS, 8), lead(ROWS, 8), lead(8, ROWS),
                  lead(8, ROWS), lead(COLS, 128), lead(1, COLS)],
        out_specs=(whole(ROWS, WIDTH), lead(ROWS, COLS), lead(ROWS, COLS), lead(ROWS, COLS), lead(COLS, 128), lead(ROWS, 8),
                   lead(ROWS, 8), whole(ROWS, 256), lead(1, COLS), lead(1, COLS)),
        out_shape=(sds(ROWS, WIDTH, dtype=BF16), sds(GROUPS, ROWS, COLS, dtype=BF16), sds(GROUPS, ROWS, COLS, dtype=BF16),
                   sds(GROUPS, ROWS, COLS), sds(GROUPS, COLS, 128, dtype=BF16), sds(GROUPS, ROWS, 8), sds(GROUPS, ROWS, 8),
                   sds(ROWS, 256), sds(GROUPS, 1, COLS), sds(GROUPS, 1, COLS)),
        scratch_shapes=[pltpu.VMEM((ROWS, ROWS), F32), pltpu.VMEM((ROWS, ROWS), F32),
                        pltpu.VMEM((ROWS, WIDTH), F32), pltpu.VMEM((ROWS, 128), F32)],
        compiler_params=params(),
        name="gate_backward_and_scan_backward",
    )(hid, square, inner, z, y, d, gain, w_all, x_conv, bc_conv, cum_col, step_col, cum_row, step_row, state, skip)


MESHID = pl.DeviceIdType.MESH
ORDERS = (("x", "y", "z"), ("y", "z", "x"), ("z", "x", "y"))
SUB = 32


def neighbour(axis, s):
    if axis == "core":
        return {"core": 1 - lax.axis_index("core")}
    if axis == "y":
        y = lax.rem(lax.axis_index("yhi") * 2 + lax.axis_index("ylo") + (s + 4), 4)
        return {"ylo": lax.rem(y, 2), "yhi": y // 2}
    return {axis: lax.rem(lax.axis_index(axis) + (s + 4), 4)}

def ag_kernel(w_ref, b_ref, g_ref, gb_ref, tss, trs, css, crs, bss, brs, lsem):
    me = dict(x=lax.axis_index("x"), z=lax.axis_index("z"), y=lax.axis_index("yhi")*2+lax.axis_index("ylo"))
    core = lax.axis_index("core")
    def at(item, r, pos, lo=0, n=SUB):
        z = slice(None) if pos["z"] is None else pos["z"]
        x = slice(None) if pos["x"] is None else pos["x"]
        if pos["y"] is None: yh=yl=slice(None)
        else: yh, yl = pos["y"]//2, lax.rem(pos["y"],2)
        return g_ref.at[item, z, yh, yl, x, core, pl.ds(r*SUB+lo, n)]
    def w(pos, a, d):
        p=dict(pos); p[a]=lax.rem(me[a]+(d+4),4); return p
    bar = pltpu.get_barrier_semaphore()
    for a in "xyz":
        for s in (1,-1):
            pl.semaphore_signal(bar, inc=1, device_id=neighbour(a,s), device_id_type=MESHID)
    pl.semaphore_signal(bar, inc=1, device_id=neighbour("core",1), device_id_type=MESHID)
    own = g_ref.at[:, me["z"], me["y"]//2, lax.rem(me["y"],2), me["x"], core]
    lc = pltpu.make_async_copy(w_ref, own, lsem.at[0]); lc.start()
    lb = pltpu.make_async_copy(b_ref, gb_ref.at[lax.rem(me["y"],2), me["x"], core], lsem.at[1]); lb.start()
    pl.semaphore_wait(bar, 7)
    pend=[]
    def rc(src, dst, ss, rs, dev):
        c=pltpu.make_async_remote_copy(src_ref=src, dst_ref=dst, send_sem=ss, recv_sem=rs, device_id=dev, device_id_type=MESHID)
        c.start(); pend.append(c); return c
    class Chunk:
        def __init__(s, item, r):
            s.item, s.r, s.order, s.k = item, r, ORDERS[r], item*3+r
            s.ncore=0; s.corer=[]
        def pos(s, st):
            p={}
            for i,a in enumerate(s.order): p[a]= None if i<st else me[a]
            return p
        def send(s, st):
            a=s.order[st]; p=s.pos(st); ref=at(s.item,s.r,p); t=s.k*12+st*4
            src = ref if st else w_ref.at[s.item, pl.ds(s.r*SUB,SUB)]
            s.c=[rc(src, ref, tss.at[t+i], trs.at[t+i], neighbour(a,d)) for i,d in enumerate((1,-1))]
            if st==0: s.core_fwd(ref, src)
        def core_fwd(s, ref, src=None):
            k=s.k*10+s.ncore; s.ncore+=1
            s.corer.append(rc(ref if src is None else src, ref, css.at[k], crs.at[k], neighbour("core",1)))
        def fwd(s, st):
            a=s.order[st]; p=s.pos(st); t=s.k*12+st*4+2
            s.f=[]
            for i,d in enumerate((1,-1)):
                s.c[i].wait_recv()
                ps=w(p,a,-d)
                h=at(s.item,s.r,ps,lo=16*i,n=16)
                s.f.append(rc(h,h,tss.at[t+i],trs.at[t+i],neighbour(a,d)))
                s.core_fwd(at(s.item,s.r,ps))
        def fin(s, st):
            for f in s.f: f.wait_recv()
            s.core_fwd(at(s.item,s.r,w(s.pos(st),s.order[st],2)))
    C=[[Chunk(i,r) for r in range(3)] for i in range(3)]
    for it in range(3):
        for c in C[it]: c.send(0)
    def gb(x, yl, lo=0, n=96): return gb_ref.at[yl, x, core, pl.ds(lo,n)]
    yl=lax.rem(me["y"],2); x=me["x"]
    bc=[rc(b_ref, gb(x,yl), bss.at[i], brs.at[i], neighbour("x",d)) for i,d in enumerate((1,-1))]
    bcore=[rc(b_ref, gb(x,yl), bss.at[2], brs.at[2], neighbour("core",1))]
    lc.wait(); lb.wait()
    for c in C[0]: c.fwd(0)
    bf=[]
    for i,d in enumerate((1,-1)):
        bc[i].wait_recv()
        h=gb(lax.rem(x-d+4,4),yl,48*i,48)
        bf.append(rc(h,h,bss.at[3+i],brs.at[3+i],neighbour("x",d)))
    for c in C[0]: c.fin(0); c.send(1)
    for f in bf: f.wait_recv()
    sl=gb_ref.at[yl,:,core]
    by=rc(sl,sl,bss.at[5],brs.at[5],{"ylo":1-yl})
    for dx in (1,2,3):
        h=gb(lax.rem(x+dx,4),yl)
        bcore.append(rc(h,h,bss.at[5+dx],brs.at[5+dx],neighbour("core",1)))
    for it in (1,2):
        for c in C[it]: c.fwd(0)
    for c in C[0]: c.fwd(1)
    for c in C[0]: c.fin(1); c.send(2)
    for it in (1,2):
        for c in C[it]: c.fin(0); c.send(1)
    by.wait_recv()
    sl=gb_ref.at[1-yl,:,core]
    bcore.append(rc(sl,sl,bss.at[9],brs.at[9],neighbour("core",1)))
    for c in C[1]: c.fwd(1)
    for c in C[1]: c.fin(1); c.send(2)
    for c in C[0]: c.fwd(2)
    for c in C[2]: c.fwd(1)
    for c in C[2]: c.fin(1); c.send(2)
    for c in C[0]: c.fin(2)
    for c in C[1]: c.fwd(2)
    for c in C[1]: c.fin(2)
    for c in C[2]: c.fwd(2)
    for c in C[2]: c.fin(2)
    for it in range(3):
        for c in C[it]:
            for q in c.corer: q.wait_recv()
    for q in bcore: q.wait_recv()
    for q in pend: q.wait_send()
def ag(w3, sb):
    A=pl.BlockSpec(memory_space=pl.ANY)
    D=pltpu.SemaphoreType.DMA
    return pl.pallas_call(ag_kernel,
        out_shape=(jax.ShapeDtypeStruct((3,4,2,2,4,2,96,384),jnp.bfloat16), jax.ShapeDtypeStruct((2,4,2,96,384),jnp.bfloat16)),
        in_specs=[A,A], out_specs=(A,A),
        scratch_shapes=[D((108,)),D((108,)),D((90,)),D((90,)),D((10,)),D((10,)),D((2,))],
        compiler_params=pltpu.CompilerParams(collective_id=0, has_side_effects=True))(w3,sb)


def my_place():
    return {"x": lax.axis_index("x"), "z": lax.axis_index("z"), "y": lax.axis_index("yhi") * 2 + lax.axis_index("ylo")}


def block_device(p):
    return {"z": p // 2, "yhi": lax.rem(p, 2)}


def f32(ref):
    return ref[...].astype(F32)


class Sender:
    def __init__(self):
        self.pending = {}

    def __call__(self, src, dst, send, recv, device):
        c = pltpu.make_async_remote_copy(src_ref=src, dst_ref=dst, send_sem=send, recv_sem=recv, device_id=device,
                                         device_id_type=MESHID)
        c.start()
        self.pending[id(c)] = c
        return c

    def sent(self, c):
        c.wait_send()
        del self.pending[id(c)]

    def all_sent(self):
        for c in self.pending.values():
            c.wait_send()


class Total:
    def __init__(self, rc, value, core, xs, yl, yh, zs, send, recv):
        self.rc, self.value, self.core, self.xs, self.yl, self.yh, self.zs = rc, value, core, xs, yl, yh, zs
        self.send, self.recv, self.at = send, recv, 0
        self.me = my_place()

    def push(self, dst, device):
        k = self.at
        self.at += 1
        return self.rc(self.value, dst, self.send.at[k], self.recv.at[k], device)

    def done(self):
        for c in self.flying:
            c.wait_recv()
        for c in self.flying:
            self.rc.sent(c)

    def step(self, j):
        v, me = self.value, self.me
        if j == 0:
            self.flying = [self.push(self.core, neighbour("core", 1))]
        elif j == 1:
            self.done()
            v[...] = v[...] + self.core[...]
            self.xs[me["x"]] = v[...]
            self.flying = [self.push(self.xs.at[me["x"]], neighbour("x", d)) for d in (1, 2, 3)]
        elif j == 2:
            self.done()
            v[...] = (self.xs[0] + self.xs[1]) + (self.xs[2] + self.xs[3])
            self.flying = [self.push(self.yl, {"ylo": 1 - lax.axis_index("ylo")})]
        elif j == 3:
            self.done()
            v[...] = v[...] + self.yl[...]
            self.flying = [self.push(self.yh, {"yhi": 1 - lax.axis_index("yhi")})]
        elif j == 4:
            self.done()
            v[...] = v[...] + self.yh[...]
            self.zs[me["z"]] = v[...]
            self.flying = [self.push(self.zs.at[me["z"]], neighbour("z", d)) for d in (1, 2, 3)]
        elif j == 5:
            self.done()
            v[...] = (self.zs[0] + self.zs[1]) + (self.zs[2] + self.zs[3])


class SmallSum:
    def __init__(self, rc, parts, sib, xs, ys, zs, hs, send, recv):
        self.rc, self.parts, self.sib, self.xs, self.ys, self.zs, self.hs = rc, parts, sib, xs, ys, zs, hs
        self.send, self.recv = send, recv
        self.me = my_place()

    def step(self, j, out=None):
        rc, me, parts, s, r = self.rc, self.me, self.parts, self.send, self.recv
        core, ylo = lax.axis_index("core"), lax.axis_index("ylo")
        if j == 0:
            self.c = [rc(parts.at[:, :, 1 - core], self.sib, s.at[0], r.at[0], neighbour("core", 1))]
        elif j == 1:
            self.c[0].wait_recv()

            def one(x):
                for yl in range(2):
                    m = parts.at[yl, x, core]
                    m[...] = (f32(m) + f32(self.sib.at[yl, x])).astype(BF16)

            pl.loop(0, 4)(one)
            self.c = [rc(parts.at[:, lax.rem(me["x"] + d, 4), core], self.xs.at[d - 1], s.at[d], r.at[d], neighbour("x", d))
                      for d in (1, 2, 3)]
        elif j == 2:
            for c in self.c:
                c.wait_recv()
            for yl in range(2):
                m = parts.at[yl, me["x"], core]
                m[...] = (f32(m) + f32(self.xs.at[0, yl]) + f32(self.xs.at[1, yl]) + f32(self.xs.at[2, yl])).astype(BF16)
            self.c = [rc(parts.at[1 - ylo, me["x"], core], self.ys, s.at[4], r.at[4], {"ylo": 1 - ylo})]
        elif j == 3:
            self.c[0].wait_recv()
            m = parts.at[ylo, me["x"], core]
            m[...] = (f32(m) + f32(self.ys)).astype(BF16)
            self.zs[me["z"]] = m[...]
            self.c = [rc(m, self.zs.at[me["z"]], s.at[4 + d], r.at[4 + d], neighbour("z", d)) for d in (1, 2, 3)]
        elif j == 4:
            for c in self.c:
                c.wait_recv()
            z, hs = self.zs, self.hs
            hs[0] = ((f32(z.at[0]) + f32(z.at[1])) + (f32(z.at[2]) + f32(z.at[3]))).astype(BF16)
            self.c = [rc(hs.at[0], hs.at[1], s.at[8], r.at[8], {"yhi": 1 - lax.axis_index("yhi")})]
        elif j == 5:
            self.c[0].wait_recv()
            out[...] = f32(self.hs.at[0]) + f32(self.hs.at[1])


SLOTS = 4
LAG = 2


def part_of(ref, item, pos, lo, n):
    z = slice(None) if pos["z"] is None else pos["z"]
    x = slice(None) if pos["x"] is None else pos["x"]
    if pos["y"] is None:
        yh = yl = slice(None)
    else:
        yh, yl = pos["y"] // 2, lax.rem(pos["y"], 2)
    return ref.at[item, z, yh, yl, x, pl.ds(lo, n)]


class Chunk:
    def __init__(self, rc, own, out, bufs, sems, item, slot, r):
        self.rc, self.own, self.out, self.item, self.slot, self.r = rc, own, out, item, slot, r
        full1, half1, full2, half2, full3, half3 = bufs
        self.bufs = [(full1[r].at[slot], half1[r].at[slot]), (full2[r].at[slot], half2[r].at[slot]),
                     (full3.at[slot * 3 + r], half3.at[slot * 3 + r])]
        self.send, self.recv = sems
        self.base = (slot * 3 + r) * 12
        self.me = my_place()
        self.sends = []

    def slab(self, st, d, lo=0, n=SUB):
        p = {a: (self.me[a] if i < st else None) for i, a in enumerate(ORDERS[self.r])}
        a = ORDERS[self.r][st]
        p[a] = lax.rem(self.me[a] + (d + 4), 4)
        return part_of(self.own, self.slot, p, self.r * SUB + lo, n)

    def loop(self, st, body):
        sizes = []
        for a, n in (("z", (4,)), ("y", (2, 2)), ("x", (4,))):
            if ORDERS[self.r].index(a) > st:
                sizes += n
        total = 1
        for n in sizes:
            total *= n

        def one(i):
            index = []
            for n in reversed(sizes):
                index.append(lax.rem(i, n))
                i = i // n
            body(tuple(reversed(index)))

        if total == 1:
            body(())
        else:
            pl.loop(0, total)(one)

    def push(self, st, k, src, dst, d):
        t = self.base + st * 4 + k
        c = self.rc(src, dst, self.send.at[t], self.recv.at[t], neighbour(ORDERS[self.r][st], d))
        self.sends.append(c)
        return c

    def far(self, st):
        half = self.bufs[st][1]
        self.far_c = [self.push(st, i, self.slab(st, 2, 16 * i, 16), half.at[i], d) for i, d in enumerate((1, -1))]

    def near(self, st):
        full, half = self.bufs[st]
        self.near_c = []
        for i, d in enumerate((1, -1)):
            self.far_c[i].wait_recv()
            mine = self.slab(st, d, 16 * i, 16)

            def add(index, mine=mine, i=i):
                m = mine.at[index] if index else mine
                m[...] = (f32(m) + f32(half.at[(i, *index)])).astype(BF16)

            self.loop(st, add)
            self.near_c.append(self.push(st, 2 + i, self.slab(st, d), full.at[i], d))

    def finish(self, st):
        full = self.bufs[st][0]
        for c in self.near_c:
            c.wait_recv()
        mine = self.slab(st, 0)
        if st < 2:
            def add(index):
                m = mine.at[index]
                m[...] = (f32(m) + f32(full.at[(0, *index)]) + f32(full.at[(1, *index)])).astype(BF16)

            self.loop(st, add)
            self.far(st + 1)
        else:
            self.out[self.item, pl.ds(self.r * SUB, SUB)] = f32(mine) + f32(full.at[0]) + f32(full.at[1])

    def step(self, j):
        if j == 0:
            self.far(0)
        elif j % 2:
            self.near(j // 2)
        else:
            self.finish(j // 2 - 1)


def backward_kernel(g_ref, x_conv_ref, d_x_ref, x_pre_ref, cum_ref, step_ref, d_cum_ref, d_step_ref,
                    w_small, n_t, c_t, hid, cot, out_in, d_z, d_local, state, dec, taps, d_bc_in, bc_pre, bc_conv, taps_bc,
                    shifted, a_log, gain, gain_part, skip_part,
                    out_ref, sout_ref, vout_ref, nout_ref, grad_hidden, *scr):
    (own, send, sib, rec_a, out_b, rec_b, dxp, tails, halo_src, halo_dst, acc, wbuf, bxc, bdx, bxp, bcum, bstep, bdc, bds,
     d_b, d_cum_all, d_step_all, parts, s_sib, s_xs, s_ys, s_zs, s_hs,
     v_core, v_xs, v_yl, v_yh, v_zs, n_core, n_xs, n_yl, n_yh, n_zs) = scr[:38]
    bufs = [scr[38:41], scr[41:44], scr[44:47], scr[47:50], scr[50], scr[51]]
    (t_s, t_r, c_s, c_r, e_s, e_r, b_s, b_r, h_s, h_r, ss, sr, vs, vr, ns, nr, wsem, lsem, credit, freed) = scr[52:]
    rc = Sender()
    core = lax.axis_index("core")
    block = lax.axis_index("z") * 2 + lax.axis_index("yhi")
    bar = pltpu.get_barrier_semaphore()
    for a in "xyz":
        for s in (1, 2, 3):
            pl.semaphore_signal(bar, inc=1, device_id=neighbour(a, s), device_id_type=MESHID)
    for d in (1, 2, 3):
        diagonal = {"z": lax.rem(lax.axis_index("z") + d, 4), "yhi": 1 - lax.axis_index("yhi")}
        pl.semaphore_signal(bar, inc=1, device_id=diagonal, device_id_type=MESHID)
    pl.semaphore_signal(bar, inc=1, device_id=neighbour("core", 1), device_id_type=MESHID)
    pl.semaphore_wait(bar, 13)

    to_owner = []
    for d in range(1, 8):
        p = lax.rem(block + d, 8)
        to_owner.append(rc(d_local.at[p], rec_a.at[block], e_s.at[d], e_r.at[d], block_device(p)))
    rec_a[block] = d_local[block]

    def core_copy(m):
        k = lax.rem(m, SLOTS)
        return pltpu.make_async_remote_copy(src_ref=send.at[k], dst_ref=sib.at[k], send_sem=c_s.at[k], recv_sem=c_r.at[k],
                                            device_id=neighbour("core", 1), device_id_type=MESHID)

    def gradient(lhs_t, rhs, slot, first_item):
        def one(m):
            @pl.when(m < GROUPS)
            def _():
                k = lax.rem(m, SLOTS)

                def wait_slot():
                    core_copy(m).wait_send()
                    pl.semaphore_wait(credit, 1)

                if first_item:
                    pl.when(m >= SLOTS)(wait_slot)
                else:
                    wait_slot()
                v = dot(lhs_t.at[:, 1 - core][...].reshape(768, ROWS), rhs[m])
                send[k] = v.astype(BF16).reshape(2, 4, 96, COLS)
                core_copy(m).start()

            @pl.when(m >= LAG)
            def _():
                q = m - LAG
                k = lax.rem(q, SLOTS)
                core_copy(q).wait_recv()
                v = dot(lhs_t.at[:, core][...].reshape(768, ROWS), rhs[q])
                own[slot, q // 2, lax.rem(q, 2)] = (v + sib[k].reshape(768, COLS).astype(F32)).astype(BF16).reshape(2, 4, 96, COLS)
                pl.semaphore_signal(credit, inc=1, device_id=neighbour("core", 1), device_id_type=MESHID)

        pl.loop(0, GROUPS + LAG)(one)

    def chunks(item, slot):
        return [Chunk(rc, own, out_ref, bufs, (t_s, t_r), item, slot, r) for r in range(3)]

    def steps(cs, j):
        for c in cs:
            c.step(j)

    oc, zc, xc_ = chunks(2, 0), chunks(1, 1), chunks(0, 0)

    gradient(c_t, out_in, 0, True)
    steps(oc, 0)

    for c in to_owner:
        c.wait_recv()
    for h in range(HEADS):
        rows = pl.ds(64 * h, 64)
        run = jnp.zeros((64, 128), F32)
        for i in range(BLOCKS - 1, -1, -1):
            out_b[i, rows] = run.astype(BF16)
            run = run * dec[i, pl.ds(h, 1)] + rec_a[i, rows].astype(F32)
    back = []
    for d in range(1, 8):
        p = lax.rem(block + d, 8)
        back.append(rc(out_b.at[p], rec_b.at[block], b_s.at[d], b_r.at[d], block_device(p)))
    rec_b[block] = out_b[block]

    gradient(n_t, d_z, 1, False)
    steps(oc, 1)
    steps(zc, 0)
    steps(oc, 2)
    for c in back:
        c.wait_recv()

    streams = ((x_conv_ref, bxc), (d_x_ref, bdx), (x_pre_ref, bxp), (cum_ref, bcum), (step_ref, bstep), (d_cum_ref, bdc),
               (d_step_ref, bds))

    def load(m):
        k = lax.rem(m, 2)
        return [pltpu.make_async_copy(src.at[m], dst.at[k], lsem.at[k, i]) for i, (src, dst) in enumerate(streams)]

    def fifth_group(m):
        k = lax.rem(m, 2)

        @pl.when(m < GROUPS - 1)
        def _():
            for c in load(m + 1):
                c.start()

        for c in load(m):
            c.wait()
        ds = rec_b[m]
        xf = bxc[k].astype(F32)
        cum = bcum[k]
        last = cum[ROWS - 1 : ROWS]
        tail = jnp.exp(last - cum)
        weights = bstep[k] * tail
        wide = spread(weights)
        d_weighted = dot(bc_conv[:, :128], ds, (1, 1))
        d_b[...] += dot((xf * wide).astype(BF16), ds)
        dx = bdx[k] + wide * d_weighted
        d_weights = gathered_heads(d_weighted * xf)
        both = weights * d_weights
        lane = lax.broadcasted_iota(jnp.int32, (1, 8), 1)
        product = jnp.sum(state[m].astype(F32) * ds.astype(F32), axis=1, keepdims=True)
        d_last = jnp.sum(both, axis=0, keepdims=True)
        for h in range(HEADS):
            dots = jnp.sum(product[64 * h : 64 * h + 64], axis=0, keepdims=True)
            d_last = jnp.where(lane == h, d_last + jnp.exp(last) * dots, d_last)
        row = lax.broadcasted_iota(jnp.int32, (ROWS, 8), 0)
        d_cum = bdc[k] - both
        d_cum_all[m] = jnp.where(row == ROWS - 1, d_cum + d_last, d_cum)
        d_step_all[m] = bds[k] + tail * d_weights
        ext = bxp[k]
        tap = taps[m]
        pre = conv_pre(ext, tap)
        sig = jax.nn.sigmoid(pre)
        dp = dx * (sig * (1.0 + pre * (1.0 - sig)))
        v_value[m] = conv_grads(dp, ext, gain_part[m], skip_part[m])
        whole_dx = conv_transposed(jnp.concatenate([dp, jnp.zeros((8, COLS), F32)], axis=0), tap)
        dxp[m] = whole_dx.astype(BF16)
        tails[m] = whole_dx[ROWS - 16 :]
        halo_src[m] = dp[:8]

    v_value = vout_ref
    d_b[...] = jnp.zeros_like(d_b)
    for c in load(0):
        c.start()
    pl.loop(0, 4)(fifth_group)
    steps(zc, 1)
    steps(oc, 3)
    pl.loop(4, GROUPS)(fifth_group)

    d_bc = jnp.concatenate([d_bc_in[:, :128] + d_b[...], d_bc_in[:, 128:]], axis=1)
    ext = bc_pre[...]
    pre = conv_pre(ext, taps_bc[...])
    sig = jax.nn.sigmoid(pre)
    dp_bc = d_bc * (sig * (1.0 + pre * (1.0 - sig)))
    halo_src[GROUPS] = jnp.concatenate([dp_bc[:8], jnp.zeros((8, 128), F32)], axis=1)
    before = lax.rem(block + 7, 8)
    halo = rc(halo_src, halo_dst, h_s, h_r, block_device(before))
    steps(oc, 4)
    steps(zc, 2)
    zero8 = jnp.zeros((1, 256), F32)
    d_cum = jnp.concatenate([d_cum_all[m][:, :HEADS] for m in range(GROUPS)] + [jnp.zeros((ROWS, 80), F32)], axis=1)
    d_step = jnp.concatenate([d_step_all[m][:, :HEADS] for m in range(GROUPS)] + [jnp.zeros((ROWS, 80), F32)], axis=1)
    d_decay = dot(triangle(True).astype(F32), d_cum, precision=lax.Precision.HIGHEST)
    rate = -jnp.exp(a_log[...])
    v = shifted[...]
    d_dt = (d_step + rate * d_decay) * jax.nn.sigmoid(v)
    log_grad = jnp.sum(d_decay * (softplus(v) * rate), axis=0, keepdims=True)
    shift_grad = jnp.sum(d_dt, axis=0, keepdims=True)
    bc_rows = conv_grads(dp_bc, ext, jnp.concatenate([log_grad, shift_grad], axis=1), zero8)
    v_value[GROUPS] = jnp.concatenate([bc_rows, jnp.zeros((8, 128), F32)], axis=1)
    vec = Total(rc, v_value, v_core, v_xs, v_yl, v_yh, v_zs, vs, vr)
    vec.step(0)

    halo.wait_recv()
    inside = block < 7

    def below(k):
        return jnp.where(inside, halo_dst[k], 0.0)

    def fix(m):
        ext = jnp.concatenate([jnp.zeros((16, COLS), F32), below(m)], axis=0)
        dxp[m, pl.ds(ROWS - 16, 16)] = (tails[m] + conv_transposed(ext, taps[m], 16)).astype(BF16)

    pl.loop(0, GROUPS)(fix)
    d_bc = conv_transposed(jnp.concatenate([dp_bc, below(GROUPS)[:, :256]], axis=0), taps_bc[...])
    small = jnp.concatenate([d_bc, d_dt], axis=1).astype(BF16)
    steps(oc, 5)
    steps(oc, 6)
    for c in [c for k in oc for c in k.sends]:
        rc.sent(c)
    for a in "xyz":
        for s in (1, -1):
            pl.semaphore_signal(freed, inc=1, device_id=neighbour(a, s), device_id_type=MESHID)
    vec.step(1)

    def weights(m):
        k = lax.rem(m, 2)
        return [pltpu.make_async_copy(g_ref.at[i, m], wbuf.at[k, i], wsem.at[k, i]) for i in range(2)]

    for c in weights(0):
        c.start()
    gradient(n_t, dxp, 0, False)
    pl.semaphore_wait(freed, 6)
    steps(xc_, 0)
    steps(zc, 3)
    vec.step(2)
    for i in range(2):
        lhs = n_t.at[:, i][...].reshape(768, ROWS)
        parts[:, :, i] = dot(lhs, small).astype(BF16).reshape(2, 4, 96, COLS)
    sums = SmallSum(rc, parts, s_sib, s_xs, s_ys, s_zs, s_hs, ss, sr)
    sums.step(0)
    steps(zc, 4)
    acc[...] = dot(small, w_small[...], (1, 1))
    steps(xc_, 1)

    def input_group(m):
        k = lax.rem(m, 2)

        @pl.when(m < GROUPS - 1)
        def _():
            for c in weights(m + 1):
                c.start()

        for c in weights(m):
            c.wait()
        lhs = jnp.concatenate([dxp[m], d_z[m]], axis=1)
        rhs = jnp.concatenate([wbuf[k, 0], wbuf[k, 1]], axis=1)
        acc[...] += dot(lhs, rhs, (1, 1))

    pl.loop(0, 3)(input_group)
    steps(zc, 5)
    sums.step(1)
    vec.step(3)
    pl.loop(3, 6)(input_group)
    steps(xc_, 2)
    sums.step(2)
    vec.step(4)
    steps(zc, 6)
    pl.loop(6, GROUPS)(input_group)
    steps(xc_, 3)
    v = hid[...].astype(F32)
    r = lax.rsqrt(jnp.mean(v * v, axis=1, keepdims=True) + EPS)
    unit = v * r
    dn = acc[...]
    gain_grad = jnp.sum(dn * unit, axis=0, keepdims=True)
    for i in range(4):
        nout_ref[0, pl.ds(i, 1)] = gain_grad[:, COLS * i : COLS * i + COLS]
    nout_ref[0, pl.ds(4, 4)] = jnp.zeros((4, COLS), F32)
    nvec = Total(rc, nout_ref, n_core, n_xs, n_yl, n_yh, n_zs, ns, nr)
    nvec.step(0)
    sums.step(3)
    d_in = dn * gain[...]
    grad_hidden[...] = r * (d_in - unit * jnp.mean(d_in * unit, axis=1, keepdims=True)) + cot[...].astype(F32)
    vec.step(5)
    steps(xc_, 4)
    nvec.step(1)
    sums.step(4)
    steps(xc_, 5)
    nvec.step(2)
    sums.step(5, sout_ref)
    steps(xc_, 6)
    for j in (3, 4, 5):
        nvec.step(j)
    for k in range(SLOTS):
        core_copy(GROUPS - SLOTS + k).wait_send()
    pl.semaphore_wait(credit, SLOTS)
    rc.all_sent()


def backward(w_all, x_conv, d_x, x_pre, cum_col, step_col, d_cum, d_step, w_small, n_t, c_t, hid, cot, out_in, d_z, d_local,
             state, dec, taps, d_bc, bc_pre, bc_conv, taps_bc, shifted, a_log, gain, gain_part, skip_part):
    hbm = pl.BlockSpec(memory_space=pl.ANY)
    vmem = pl.BlockSpec(memory_space=pltpu.VMEM)
    sem = pltpu.SemaphoreType.DMA

    def buf(*shape, dtype=BF16):
        return pltpu.VMEM((*shape, COLS), dtype)

    def v(*shape, dtype=F32):
        return pltpu.VMEM(shape, dtype)

    scratch = [
        buf(2, 4, 2, 2, 4, 96), buf(SLOTS, 2, 4, 96), buf(SLOTS, 2, 4, 96),
        v(GROUPS, COLS, 128, dtype=BF16), v(GROUPS, COLS, 128, dtype=BF16), v(GROUPS, COLS, 128, dtype=BF16),
        buf(GROUPS, ROWS), buf(GROUPS, 16, dtype=F32), buf(GROUPS + 1, 8, dtype=F32), buf(GROUPS + 1, 8, dtype=F32),
        v(ROWS, WIDTH), buf(2, 2, WIDTH),
        buf(2, ROWS), buf(2, ROWS, dtype=F32), buf(2, HALO + ROWS, dtype=F32),
        v(2, ROWS, 8), v(2, ROWS, 8), v(2, ROWS, 8), v(2, ROWS, 8),
        v(ROWS, 128), v(GROUPS, ROWS, 8), v(GROUPS, ROWS, 8),
        buf(2, 4, 2, 96), buf(2, 4, 96), buf(3, 2, 96), buf(96), buf(4, 96), buf(2, 96),
    ]
    for n in (GROUPS + 1, 1):
        one = buf(n, 8, dtype=F32)
        four = buf(4, n, 8, dtype=F32)
        scratch += [one, four, one, one, four]
    scratch += [buf(2, 2, 4, 2, 2, SUB), buf(2, 2, 4, 4, SUB), buf(2, 2, 2, 2, 4, SUB)]
    scratch += [buf(2, 2, 4, 2, 2, 16), buf(2, 2, 4, 4, 16), buf(2, 2, 2, 2, 4, 16)]
    scratch += [buf(2, 2, 4, SUB), buf(2, 2, 4, SUB), buf(2, 2, 2, 2, SUB)]
    scratch += [buf(2, 2, 4, 16), buf(2, 2, 4, 16), buf(2, 2, 2, 2, 16)]
    scratch += [buf(6, 2, SUB), buf(6, 2, 16)]
    scratch += [sem((72,)), sem((72,)), sem((SLOTS,)), sem((SLOTS,)), sem((8,)), sem((8,)), sem((8,)), sem((8,)),
                sem, sem, sem((9,)), sem((9,)), sem((9,)), sem((9,)), sem((9,)), sem((9,)), sem((2, 2)), sem((2, 7)),
                pltpu.SemaphoreType.REGULAR, pltpu.SemaphoreType.REGULAR]
    return pl.pallas_call(
        backward_kernel,
        out_shape=(sds(3, 96, COLS), sds(96, COLS), sds(GROUPS + 1, 8, COLS), sds(1, 8, COLS), sds(ROWS, WIDTH)),
        in_specs=[hbm] * 8 + [vmem] * 20,
        out_specs=(vmem,) * 5,
        scratch_shapes=scratch,
        compiler_params=pltpu.CompilerParams(collective_id=1, has_side_effects=True, vmem_limit_bytes=62 * 2**20),
        name="backward_between_devices",
    )(w_all, x_conv, d_x, x_pre, cum_col, step_col, d_cum, d_step, w_small, n_t, c_t, hid, cot, out_in, d_z, d_local,
      state, dec, taps, d_bc, bc_pre, bc_conv, taps_bc, shifted, a_log, gain, gain_part, skip_part)
def to_everyone(array):
    copies = jnp.broadcast_to(array, (BLOCKS, *array.shape))
    return lax.all_to_all(copies, MP, split_axis=0, concat_axis=0, tiled=True)


def swapped(array):
    return lax.all_to_all(array, MP, split_axis=0, concat_axis=0, tiled=True)


def carried_states(local, decays, backward):
    blocks = swapped(local).astype(F32)
    state = jnp.zeros(blocks.shape[1:], F32)
    out = [None] * BLOCKS
    for i in range(BLOCKS - 1, -1, -1) if backward else range(BLOCKS):
        out[i] = state.astype(BF16)
        state = state * jnp.repeat(decays[i], 64)[:, None] + blocks[i]
    return swapped(jnp.stack(out))


def shards(hidden, grad_out, norm_gain, w_zx, w_bc, w_dt, conv_x, conv_bc, a_log, dt_bias, d_skip, gate_gain, w_out):
    index = lax.axis_index(MP)
    down = [(i, i + 1) for i in range(BLOCKS - 1)]
    up = [(i + 1, i) for i in range(BLOCKS - 1)]

    halo = lax.ppermute(hidden[-HALO:], MP, down)
    heads = jnp.concatenate([a_log, dt_bias, d_skip, jnp.zeros((COLS - 3 * HEADS,), F32)])[None]
    packed = jnp.concatenate([conv_x, gate_gain[None], heads, jnp.pad(w_dt.astype(F32).reshape(-1), (0, 192)).reshape(2, COLS),
                              jnp.zeros((7, COLS), F32)])
    everyone = to_everyone(packed)
    taps = jnp.pad(everyone[:, :5], ((0, 0), (0, 3), (0, 0)))
    gate = everyone[:, 5:6]
    per_head = [everyone[:, 6, HEADS * i : HEADS * i + HEADS].reshape(1, -1) for i in range(3)]
    log_rate, shift, skip = per_head
    pad = ((0, 0), (0, 128 - BLOCKS * HEADS))
    log_rate, shift = jnp.pad(log_rate, pad), jnp.pad(shift, pad)
    skip = jnp.repeat(skip, 64, axis=1).reshape(GROUPS, 1, COLS)
    w_steps = jnp.moveaxis(everyone[:, 7:9].reshape(BLOCKS, 768)[:, :576].reshape(BLOCKS, 96, HEADS), 0, 1).reshape(96, BLOCKS * HEADS).astype(BF16)
    w_small_own = jnp.concatenate([w_bc, w_steps, jnp.zeros((96, 80), BF16)], axis=1)
    taps_bc = jnp.pad(conv_bc, ((0, 3), (0, 0)))
    gain = norm_gain[None]

    w_all, w_small = ag(jnp.stack([w_zx[:, 1], w_zx[:, 0], w_out.T]), w_small_own)
    w_all = w_all.reshape(3, GROUPS, WIDTH, COLS)
    w_small = w_small.reshape(WIDTH, 384)

    normed, normed_t, cot_t, bc_pre, bc_conv, shifted, cum_col, step_col, cum_row, step_row = first(
        hidden, halo, grad_out, gain, w_small, taps_bc, log_rate, shift)
    x_pre, x_conv, local = second(normed, w_all, taps, bc_conv, cum_col, step_col)
    decays = jnp.exp(swapped(cum_col[:, ROWS - 1, :]))
    state = carried_states(local, decays[:, :HEADS], False)
    z, y, d, square, inner = third(normed, grad_out, w_all, x_conv, bc_conv, cum_col, cum_row, step_row, state, skip, gate)
    result, out_in, d_z, d_x, d_local, d_cum, d_step, d_bc, gain_part, skip_part = fourth(
        hidden, square, inner, z, y, d, gate, w_all, x_conv, bc_conv, cum_col, step_col, cum_row, step_row, state, skip)
    owned, small, vector, norm_sum, grad_hidden = backward(
        w_all, x_conv, d_x, x_pre, cum_col, step_col, d_cum, d_step, w_small, normed_t, cot_t, hidden, grad_out, out_in, d_z,
        d_local, state, jnp.broadcast_to(decays[:, :, None], (BLOCKS, 8, 128)), taps, d_bc, bc_pre, bc_conv, taps_bc, shifted,
        log_rate, gain, gain_part, skip_part)

    def own(flat):
        return lax.dynamic_slice_in_dim(flat, index * HEADS, HEADS, flat.ndim - 1)

    mine = lax.dynamic_index_in_dim(vector, index, 0, keepdims=False)
    return (
        result,
        grad_hidden,
        norm_sum[0, :4].reshape(WIDTH),
        jnp.stack([owned[1], owned[0]], axis=1),
        small[:, :256],
        own(small[:, 256:304]),
        mine[:5],
        vector[GROUPS, :5, :256],
        own(vector[GROUPS, 5, :48]),
        own(vector[GROUPS, 5, 128:176]),
        mine[6].reshape(HEADS, 64).sum(axis=1),
        mine[5],
        owned[2].T,
    )


def solution(mesh):
    finer = Mesh(mesh.devices.reshape(2, 4, 2, 4, 2), DP_MP)
    rows = P(DP_MP, None)
    placed = (rows, rows, P(), P(DP, None, MP), P(DP, None), P(DP, MP), P(None, MP), P(), P(MP), P(MP), P(MP), P(MP),
              P(MP, DP))
    return jax.shard_map(
        shards,
        mesh=finer,
        in_specs=placed,
        out_specs=(rows, rows, P(), P(DP, None, MP), P(DP, None), P(DP, MP), P(None, MP), P(), P(MP), P(MP), P(MP), P(MP),
                   P(MP, DP)),
        check_vma=False,
    )
```

time: 1120 us -> 378 us (0.34); the launches traced: 1110 us -> 377 us
  waiting for transfers between devices: 406 us -> 25.2 us
  local copies, waits for them, and re-layouts: 314 us -> 28.7 us
  Pallas kernels: 0 us -> 284 us
  matrix products: 183 us -> 0 us
  other arithmetic: 154 us -> 9.08 us
  between operations: 15.3 us -> 0.92 us
    pallas_call x0 -> x6, Pallas kernels: none -> 284 us  [the longest x1 135 us: backward(): pl.pallas_call(backward_kernel, out_shape=(sds(3, 96, COLS), sds(96, COLS...]
    dot_general x124 -> x0, matrix products: 183 us -> none  [the longest x24 53.2 us: span_step(): inside = jnp.einsum('hts,shp->thp', mixing, u_blk, precision=EXACT)]
    dynamic_update_slice x56 -> x0, local copies, waits for them, and re-layouts: 181 us -> none  [ssd_scan(): final, outputs = lax.scan(jax.checkpoint(span_step), state, blocks)]
    reduce_scatter x3 -> x0, waiting for transfers between devices: 156 us -> none  [the longest x1 93.3 us: shards(): lax.psum_scatter(jnp.dot(piece, out_full, preferred_element_type=jnp.floa...]
    all_gather x3 -> x0, waiting for transfers between devices: 128 us -> none  [the longest x1 92 us: shards(): gathered = lax.all_gather(normed, MP, axis=0, tiled=True)]
    another operation x73 -> x3, other arithmetic: 90.9 us -> 1.51 us  [the longest x1 0.77 us: carried_states(): return swapped(jnp.stack(out))]
    unnamed x9 -> x0, waiting for transfers between devices: 55.9 us -> none
    psum x1 -> x0, waiting for transfers between devices: 46.4 us -> none  [shards(): bcc_total = lax.psum(grad_bcc.astype(jnp.bfloat16), MP).astype(jnp.float32)]
  transfers between devices with their start and end apart: 13 -> 5, of which waited for: 10 -> 2; matrix products, arithmetic and copies ran while one was open for 27% -> 3% of each run, Pallas kernels for 0% -> 25%
where the time goes in v1:
time: 378 us; the launch traced here: 377 us
  Pallas kernels  284 us (75%)
  local copies, waits for them, and re-layouts  28.7 us (8%)
  starting transfers between devices  28.3 us (7%)
  waiting for transfers between devices  25.2 us (7%)
  other arithmetic  9.08 us (2%)
    pallas_call x1, Pallas kernels, backward(): pl.pallas_call(backward_kernel, out_shape=(sds(3, 96, COLS), sds(96, COLS...  135 us
    pallas_call x1, Pallas kernels, ag(): pl.pallas_call(ag_kernel, out_shape=(jax.ShapeDtypeStruct((3, 4, 2, 2, 4,...  82.5 us
    pallas_call x1, Pallas kernels, fourth(): pl.pallas_call(fourth_kernel, grid=(GROUPS,), in_specs=[whole(ROWS, WIDTH...  31.6 us
    all_to_all x3, waiting for transfers between devices, swapped(): return lax.all_to_all(array, MP, split_axis=0, concat_axis=0, tiled=True)  25.2 us
    pallas_call x1, Pallas kernels, third(): pl.pallas_call(third_kernel, grid=(GROUPS,), in_specs=[whole(HALO + ROWS,...  17.2 us
    all_to_all x3, starting transfers between devices, swapped(): return lax.all_to_all(array, MP, split_axis=0, concat_axis=0, tiled=True)  14.9 us
    pallas_call x1, Pallas kernels, second(): pl.pallas_call(second_kernel, grid=(GROUPS,), in_specs=[whole(HALO + ROWS...  12.4 us
    all_to_all x1, starting transfers between devices, to_everyone(): return lax.all_to_all(copies, MP, split_axis=0, concat_axis=0, tiled=True)  8.03 us
  transfers between devices with their start and end apart: 5, of which 2 were waited for; matrix products, arithmetic and copies ran while one was open for 3% of the time, Pallas kernels for 25%

profile of v1, /device:TPU:0, one launch (start us, length us, event | category | flops | bytes accessed | tf_op | source)
XLA Modules:
  0.0 376.6 jit_solution(4821903710792778405)
XLA Ops:
  0.7 0.8 copy.33
  1.7 0.8 pad_maximum_fusion.2
  2.5 0.7 broadcast_in_dim.57
  3.2 0.8 concatenate.10
  4.0 0.7 broadcast_in_dim.61
  4.7 8.0 %all-to-all-start = ((f32[8,16,384]{2,1,0:T(8,128)}), f32[8,16,384]{2,1,0:T(8,128)S(1)}, u32[]{:S(2)}, u32[]{:S(2)}) async-start(f32[8,16,384]{2,1,0:T(8,128)} %broadcast_in_dim.61), calls=%async_computation | async-start | bytes 393216 | tf_op jit(solution)/shard_map/all_to_all | solution.py:976
  12.7 0.8 slice.129
  13.5 5.4 %collective-permute-start = (bf16[16,1536]{1,0:T(8,128)(2,1)S(1)}, bf16[16,1536]{1,0:T(8,128)(2,1)S(1)}, u32[]{:S(2)}, u32[]{:S(2)}) collective-permute-start(bf16[16,1536]{1,0:T(8,128)(2,1)S(1)} %slice.129), channel_id=1, source_target_pairs={{0,1},{1,2},{2,3},{3,4},{4,5},{5,6},{6,7},{8,9},{9,10},{10,11},{11... | collective-permute-start | bytes 147464 | tf_op jit(solution)/shard_map/ppermute | solution.py:998
  18.9 1.2 fusion.7
  21.5 0.7 pad_maximum_fusion.1.w_ref
  23.0 0.7 maximum_maximum_fusion.b_ref
  24.9 82.5 %shard_map.228 = (bf16[3,4,2,2,4,2,96,384]{7,6,5,4,3,2,1,0:T(8,128)(2,1)}, bf16[2,4,2,96,384]{4,3,2,1,0:T(8,128)(2,1)}) custom-call(bf16[3,96,384]{2,1,0:T(8,128)(2,1)} %pad_maximum_fusion.1.w_ref, bf16[96,384]{1,0:T(8,128)(2,1)} %maximum_maximum_fusion.b_ref), custom_call_target="tpu_custom_call" | custom-call | tf_op jit(solution)/shard_map/pallas_call | solution.py:427
  107.5 0.6 copy-done.4
  108.1 5.6 %norm_and_small_projections.1 = (bf16[272,1536]{1,0:T(8,128)(2,1)}, bf16[8,2,96,256]{3,2,1,0:T(8,128)(2,1)}, bf16[8,2,96,256]{3,2,1,0:T(8,128)(2,1)}, f32[272,25...) custom-call(bf16[256,1536]{1,0:T(8,128)(2,1)} %hid.5, ...), custom_call_target="tpu_custom_call" | custom-call | tf_op jit(solution)/shard_map/norm_and_small_projections/pallas_call | solution.py:127
  113.6 1.4 slice.137
  115.0 4.0 %all-to-all-start.1 = ((f32[8,1,8]{2,1,0:T(1,128)}), f32[8,1,8]{2,1,0:T(1,128)S(1)}, u32[]{:S(2)}, u32[]{:S(2)}) async-start(f32[8,1,8]{2,1,0:T(1,128)} %slice.137), calls=%async_computation.1 | async-start | bytes 8192 | tf_op jit(solution)/shard_map/all_to_all | solution.py:980
  118.9 0.7 slice_select_fusion.taps
  119.7 12.4 %x_projection_and_state.1 = (f32[8,272,384]{2,1,0:T(8,128)}, bf16[8,256,384]{2,1,0:T(8,128)(2,1)}, bf16[8,384,128]{2,1,0:T(8,128)(2,1)}) custom-call(bf16[272,1536]{1,0:T(8,128)(2,1)} %get-tuple-element.49.normed, bf16[3,8,1536,384]{3,2,1,0:T(8,128)(2,1)} %bitcast.47, f32[8,8,384]{2,1,0:T(8,128)} %slice_select_fusion.taps, ...), custom_call_target="tpu_custom_call" | custom-call | tf_op jit(solution)/shard_map/x_projection_and_state/pallas_call | solution.py:165
  132.1 7.2 %all-to-all-start.2 = ((bf16[8,384,128]{2,1,0:T(8,128)(2,1)}), bf16[8,384,128]{2,1,0:T(8,128)(2,1)S(1)}, u32[]{:S(2)}, u32[]{:S(2)}) async-start(bf16[8,384,128]{2,1,0:T(8,128)(2,1)} %get-tuple-element.57), calls=%async_computation.2 | async-start | bytes 1572864 | tf_op jit(solution)/shard_map/all_to_all | solution.py:980
  139.3 0.6 broadcast_dynamic-update-slice_fusion
  141.0 13.0 %all-to-all-done.2 = bf16[8,384,128]{2,1,0:T(8,128)(2,1)S(1)} async-done(((bf16[8,384,128]{2,1,0:T(8,128)(2,1)}), bf16[8,384,128]{2,1,0:T(8,128)(2,1)S(1)}, u32[]{:S(2)}, u32[]{:S(2)}) %all-to-all-start.2) | async-done | bytes 786464 | tf_op jit(solution)/shard_map/all_to_all | solution.py:980
  154.1 0.8 fusion.2
  154.9 0.8 convert_dynamic-update-slice_fusion.4
  155.7 0.8 convert_dynamic-update-slice_fusion.3
  156.4 0.8 convert_dynamic-update-slice_fusion.2
  157.2 0.8 convert_dynamic-update-slice_fusion.1
  158.0 0.8 convert_dynamic-update-slice_fusion
  158.8 0.8 fusion.3
  159.6 3.7 all-to-all-start.3
  163.4 0.7 broadcast_in_dim.74.skip
  164.1 0.6 slice.181.gain
  164.7 12.2 %all-to-all-done.3.state = bf16[8,384,128]{2,1,0:T(8,128)(2,1)S(1)} async-done(((bf16[8,384,128]{2,1,0:T(8,128)(2,1)}), bf16[8,384,128]{2,1,0:T(8,128)(2,1)S(1)}, u32[]{:S(2)}, u32[]{:S(2)}) %all-to-all-start.3) | async-done | bytes 786464 | tf_op jit(solution)/shard_map/all_to_all | solution.py:980
  176.9 0.9 copy-done
  177.7 17.2 %scan_and_gate.1 = (f32[8,256,384]{2,1,0:T(8,128)}, f32[8,256,384]{2,1,0:T(8,128)}, f32[8,256,384]{2,1,0:T(8,128)}, f32[256,128]{1,0:T(8,128)}, f32[256,128]{1,0:T(8,128)}) custom-call(bf16[272,1536]{1,0:T(8,128)(2,1)} %get-tuple-element.49.normed, bf16[256,1536]{1,0:T(8,128)(2,1)} %cot.5, bf16[3,8,1536,384]{3,2,1,0:T(8,128)(2,1)} %bitcast.48, ...), custom_call_target="tpu_custom_call" | custom-call | tf_op jit(solution)/shard_map/scan_and_gate/pallas_call | solution.py:208
  195.0 31.6 %gate_backward_and_scan_backward.1 = (bf16[256,1536]{1,0:T(8,128)(2,1)}, bf16[8,256,384]{2,1,0:T(8,128)(2,1)}, bf16[8,256,384]{2,1,0:T(8,128)(2,1)}, f32[8,256,3...) custom-call(bf16[256,1536]{1,0:T(8,128)(2,1)} %hid.5, ...), custom_call_target="tpu_custom_call" | custom-call | tf_op jit(solution)/shard_map/gate_backward_and_scan_backward/pallas_call | solution.py:296
  226.6 0.7 broadcast_in_dim.73.dec
  227.3 135.1 %backward_between_devices.1 = (f32[3,96,384]{2,1,0:T(8,128)}, f32[96,384]{1,0:T(8,128)}, f32[9,8,384]{2,1,0:T(8,128)}, f32[1,8,384]{2,1,0:T(8,128)}, f32[256,1536]{1,0:T(8,128)}) custom-call(bf16[3,8,1536,384]{3,2,1,0:T(8,128)(2,1)} %bitcast.51, bf16[8,256,384]{2,1,0:T(8,128)(2,1)} %get-tuple-element.54.x_conv.x_conv_ref, ...), custom_call_target="tpu_custom_call" | custom-call | tf_op jit(solution)/shard_map/backward_between_devices/pallas_call | solution.py:964
  362.4 0.9 slice.159
  363.3 1.5 slice.158
  364.8 0.7 fusion.8
  365.5 1.3 slice_bitcast_fusion.3
  366.8 1.7 slice_bitcast_fusion
  368.6 0.9 copy.38
  369.6 0.7 copy.39
  370.3 1.3 dynamic-slice_bitcast_fusion
  371.6 1.4 dynamic-slice_reduce_fusion
  373.0 0.6 reduce_sum.9
  375.4 1.1 copy.53
  (67 shorter events, 6.6 us)
Async XLA Ops:
  0.6 19.6 %copy-start.6 = (f32[5,256]{1,0:T(8,128)S(1)}, f32[5,256]{1,0:T(8,128)}, u32[]{:S(2)}) copy-start(f32[5,256]{1,0:T(8,128)} %param.20) | copy-start | bytes 15364
  0.7 20.2 %copy-start.5 = (f32[1536]{0:T(1024)S(1)}, f32[1536]{0:T(1024)}, u32[]{:S(2)}) copy-start(f32[1536]{0:T(1024)} %param.15) | copy-start | bytes 18436
  0.7 20.9 %copy-start.2 = (bf16[384,96]{0,1:T(8,128)(2,1)S(1)}, bf16[384,96]{0,1:T(8,128)(2,1)}, u32[]{:S(2)}) copy-start(bf16[384,96]{0,1:T(8,128)(2,1)} %param.25) | copy-start | bytes 221188
  0.7 22.3 %copy-start.3 = (bf16[96,256]{1,0:T(8,128)(2,1)S(1)}, bf16[96,256]{1,0:T(8,128)(2,1)}, u32[]{:S(2)}) copy-start(bf16[96,256]{1,0:T(8,128)(2,1)} %param.17) | copy-start | bytes 147460
  4.7 17.6 %all-to-all-start = ((f32[8,16,384]{2,1,0:T(8,128)}), f32[8,16,384]{2,1,0:T(8,128)S(1)}, u32[]{:S(2)}, u32[]{:S(2)}) async-start(f32[8,16,384]{2,1,0:T(8,128)} %broadcast_in_dim.61), calls=%async_computation | async-start | bytes 393216 | tf_op jit(solution)/shard_map/all_to_all | solution.py:976
  13.5 93.9 %collective-permute-start = (bf16[16,1536]{1,0:T(8,128)(2,1)S(1)}, bf16[16,1536]{1,0:T(8,128)(2,1)S(1)}, u32[]{:S(2)}, u32[]{:S(2)}) collective-permute-start(bf16[16,1536]{1,0:T(8,128)(2,1)S(1)} %slice.129), channel_id=1, source_target_pairs={{0,1},{1,2},{2,3},{3,4},{4,5},{5,6},{6,7},{8,9},{9,10},{10,11},{11... | collective-permute-start | bytes 147464 | tf_op jit(solution)/shard_map/ppermute | solution.py:998
  23.8 95.2 %copy-start.8 = (pred[8]{0:T(512)(128)(4,1)S(1)}, pred[8]{0:T(512)(128)(4,1)}, u32[]{:S(2)}) copy-start(pred[8]{0:T(512)(128)(4,1)} %constant.12.clone.1) | copy-start | bytes 28
  107.4 0.6 copy-start.4
  115.0 17.1 %all-to-all-start.1 = ((f32[8,1,8]{2,1,0:T(1,128)}), f32[8,1,8]{2,1,0:T(1,128)S(1)}, u32[]{:S(2)}, u32[]{:S(2)}) async-start(f32[8,1,8]{2,1,0:T(1,128)} %slice.137), calls=%async_computation.1 | async-start | bytes 8192 | tf_op jit(solution)/shard_map/all_to_all | solution.py:980
  132.1 21.9 %all-to-all-start.2 = ((bf16[8,384,128]{2,1,0:T(8,128)(2,1)}), bf16[8,384,128]{2,1,0:T(8,128)(2,1)S(1)}, u32[]{:S(2)}, u32[]{:S(2)}) async-start(bf16[8,384,128]{2,1,0:T(8,128)(2,1)} %get-tuple-element.57), calls=%async_computation.2 | async-start | bytes 1572864 | tf_op jit(solution)/shard_map/all_to_all | solution.py:980
  159.6 17.3 %all-to-all-start.3 = ((bf16[8,384,128]{2,1,0:T(8,128)(2,1)}), bf16[8,384,128]{2,1,0:T(8,128)(2,1)S(1)}, u32[]{:S(2)}, u32[]{:S(2)}) async-start(bf16[8,384,128]{2,1,0:T(8,128)(2,1)} %fusion.3), calls=%async_computation.3 | async-start | bytes 1572864 | tf_op jit(solution)/shard_map/all_to_all | solution.py:980
  176.9 0.9 copy-start
  362.3 12.5 %copy-start.7 = (f32[1,8,384]{2,1,0:T(8,128)S(1)}, f32[1,8,384]{2,1,0:T(8,128)}, u32[]{:S(2)}) copy-start(f32[1,8,384]{2,1,0:T(8,128)} %get-tuple-element.79) | copy-start | bytes 36868
  362.4 13.1 %copy-start.1 = (f32[256,1536]{1,0:T(8,128)S(1)}, f32[256,1536]{1,0:T(8,128)}, u32[]{:S(2)}) copy-start(f32[256,1536]{1,0:T(8,128)} %get-tuple-element.150) | copy-start | bytes 4718596

commit v2 on v1

v2 whole, which is shorter than its diff:
```python
import jax
import jax.numpy as jnp
from jax import lax
from jax.experimental import pallas as pl
from jax.experimental.pallas import tpu as pltpu
from jax.sharding import Mesh
from jax.sharding import PartitionSpec as P

MP = ("z", "yhi")
DP = ("ylo", "x", "core")
DP_MP = DP + MP
BLOCKS = 8
F32 = jnp.float32
BF16 = jnp.bfloat16
ROWS = 256
WIDTH = 1536
GROUPS = 8
COLS = 384
HEADS = 6
HALO = 16
EPS = 1e-05
INNER = GROUPS * COLS
VMEM_LIMIT = 56 * 2**20


def dot(a, b, contract=(1, 0), precision=None):
    return lax.dot_general(
        a, b, (((contract[0],), (contract[1],)), ((), ())),
        preferred_element_type=F32, precision=precision,
    )


def spread(per_head):
    rows = per_head.shape[0]
    low = lax.broadcasted_iota(jnp.int32, (rows, 128), 1) < 64
    tiles = [
        jnp.where(low, per_head[:, 2 * i : 2 * i + 1], per_head[:, 2 * i + 1 : 2 * i + 2])
        for i in range(COLS // 128)
    ]
    return jnp.concatenate(tiles, axis=1)


def gathered_heads(values):
    rows = values.shape[0]
    low = lax.broadcasted_iota(jnp.int32, (rows, 128), 1) < 64
    lane = lax.broadcasted_iota(jnp.int32, (rows, 8), 1)
    out = jnp.zeros((rows, 8), F32)
    for i in range(COLS // 128):
        tile = values[:, 128 * i : 128 * i + 128]
        first = jnp.sum(jnp.where(low, tile, 0.0), axis=1, keepdims=True)
        both = jnp.sum(tile, axis=1, keepdims=True)
        out = jnp.where(lane == 2 * i, first, out)
        out = jnp.where(lane == 2 * i + 1, both - first, out)
    return out


def softplus(v):
    return jnp.maximum(v, 0.0) + jnp.log1p(jnp.exp(-jnp.abs(v)))


def conv_pre(ext, taps):
    total = taps[4:5]
    for j in range(4):
        total = total + ext[HALO - 3 + j : HALO - 3 + j + ROWS] * taps[j : j + 1]
    return total


def conv_transposed(ext, taps, rows=ROWS):
    total = ext[3 : 3 + rows] * taps[0:1]
    for j in range(1, 4):
        total = total + ext[3 - j : 3 - j + rows] * taps[j : j + 1]
    return total


def conv_grads(dpre, ext, sixth, seventh):
    rows = [
        jnp.sum(dpre * ext[HALO - 3 + j : HALO - 3 + j + ROWS], axis=0, keepdims=True)
        for j in range(4)
    ]
    rows.append(jnp.sum(dpre, axis=0, keepdims=True))
    rows += [sixth, seventh, jnp.zeros((1, dpre.shape[1]), F32)]
    return jnp.concatenate(rows, axis=0)


def triangle(upper):
    row = lax.broadcasted_iota(jnp.int32, (ROWS, ROWS), 0)
    col = lax.broadcasted_iota(jnp.int32, (ROWS, ROWS), 1)
    return row <= col if upper else row >= col


def sds(*shape, dtype=F32):
    return jax.ShapeDtypeStruct(shape, dtype)


def params():
    return pltpu.CompilerParams(vmem_limit_bytes=VMEM_LIMIT)


def whole(*shape):
    return pl.BlockSpec(shape, lambda m: (0,) * len(shape))


def lead(*shape):
    return pl.BlockSpec((None, *shape), lambda m: (m,) + (0,) * len(shape))


def weight(item):
    return pl.BlockSpec((None, None, WIDTH, COLS), lambda m: (item, m, 0, 0))


def fourth_kernel(hid, square, inner, z_in, y_in, d_in, taps, w_o, x_conv, bc_conv, cols, cum_row, step_row,
                  state,
                  result, out_in, d_z, d_x, d_state, d_cols, d_bc, gain_part, skip_part,
                  gram, d_gram, acc, d_c):
    step_id = pl.program_id(0)

    @pl.when(step_id == 0)
    def _():
        g = dot(bc_conv[:, 128:], bc_conv[:, :128], (1, 1))
        gram[...] = jnp.where(triangle(False), g, 0.0)
        d_gram[...] = jnp.zeros_like(d_gram)
        acc[...] = jnp.zeros_like(acc)
        d_c[...] = jnp.zeros_like(d_c)

    z = z_in[...]
    y = y_in[...]
    d = d_in[...]
    gain = taps[5:6]
    skip = spread(taps[6:7, 12:20])
    sig = jax.nn.sigmoid(z)
    act = z * sig
    gated = y * act
    r2 = lax.rsqrt(jnp.sum(square[...], axis=1, keepdims=True) / INNER + EPS)
    total = jnp.sum(inner[...], axis=1, keepdims=True)
    unit = gated * r2
    o = (unit * gain).astype(BF16)
    out_in[...] = o
    acc[...] += dot(o, w_o[...], (1, 1))
    gain_part[...] = jnp.sum(d * unit, axis=0, keepdims=True)
    d_gated = r2 * (d * gain) - gated * (r2 * r2 * r2 * (total / INNER))
    dy = d_gated * act
    d_z[...] = (d_gated * y * sig * (1.0 + z * (1.0 - sig))).astype(BF16)

    xc = x_conv[...]
    xf = xc.astype(F32)
    cum, step = cols[:, :8], cols[:, 8:]
    dyb = dy.astype(BF16)
    c_mat = bc_conv[:, 128:]
    skip_part[...] = jnp.sum(dy * xf, axis=0, keepdims=True)
    grown = spread(jnp.exp(cum))
    dye = (grown * dy).astype(BF16)
    d_c[...] += dot(dye, state[...])
    d_state[...] = dot(dye, c_mat, (0, 0)).astype(BF16)
    carried = grown * dot(c_mat, state[...], (1, 1))
    d_cum_col = gathered_heads(dy * carried)
    lane = lax.broadcasted_iota(jnp.int32, (ROWS, 8), 1)
    parts = []
    sums = []
    for h in range(HEADS):
        xh = xc[:, 64 * h : 64 * h + 64]
        dyh = dyb[:, 64 * h : 64 * h + 64]
        decay = jnp.exp(jnp.minimum(cum[:, h : h + 1] - cum_row[h : h + 1, :], 0.0))
        d_mix = dot(dyh, xh, (1, 1))
        grown_row = step_row[h : h + 1, :]
        plain = decay * gram[...]
        r = plain * d_mix
        sums.append(jnp.sum(r, axis=0, keepdims=True))
        row = jnp.sum(r * grown_row, axis=1, keepdims=True)
        d_cum_col = jnp.where(lane == h, d_cum_col + row, d_cum_col)
        d_gram[...] += decay * d_mix * grown_row
        parts.append(dot((plain * grown_row).astype(BF16), dyh, (0, 0)))
    sums.append(jnp.zeros((2, ROWS), F32))
    sums = jnp.concatenate(sums, axis=0).T
    d_x[...] = jnp.concatenate(parts, axis=1) + skip * dy
    d_cols[...] = jnp.concatenate([d_cum_col - sums * step, sums], axis=1)

    @pl.when(step_id == GROUPS - 1)
    def _():
        result[...] = (hid[...].astype(F32) + acc[...]).astype(BF16)
        dg = jnp.where(triangle(False), d_gram[...], 0.0).astype(BF16)
        d_bc[:, :128] = dot(dg, c_mat, (0, 0))
        d_bc[:, 128:] = d_c[...] + dot(dg, bc_conv[:, :128])


def fourth(hid, square, inner, z, y, d, taps, w_all, x_conv, bc_conv, cols, cum_row, step_row, state):
    return pl.pallas_call(
        fourth_kernel,
        grid=(GROUPS,),
        in_specs=[whole(ROWS, WIDTH), whole(ROWS, 128), whole(ROWS, 128), lead(ROWS, COLS), lead(ROWS, COLS), lead(ROWS, COLS),
                  lead(8, COLS), weight(2), lead(ROWS, COLS), whole(ROWS, 256), lead(ROWS, 16), lead(8, ROWS),
                  lead(8, ROWS), lead(COLS, 128)],
        out_specs=(whole(ROWS, WIDTH), lead(ROWS, COLS), lead(ROWS, COLS), lead(ROWS, COLS), lead(COLS, 128), lead(ROWS, 16),
                   whole(ROWS, 256), lead(1, COLS), lead(1, COLS)),
        out_shape=(sds(ROWS, WIDTH, dtype=BF16), sds(GROUPS, ROWS, COLS, dtype=BF16), sds(GROUPS, ROWS, COLS, dtype=BF16),
                   sds(GROUPS, ROWS, COLS), sds(GROUPS, COLS, 128, dtype=BF16), sds(GROUPS, ROWS, 16),
                   sds(ROWS, 256), sds(GROUPS, 1, COLS), sds(GROUPS, 1, COLS)),
        scratch_shapes=[pltpu.VMEM((ROWS, ROWS), F32), pltpu.VMEM((ROWS, ROWS), F32),
                        pltpu.VMEM((ROWS, WIDTH), F32), pltpu.VMEM((ROWS, 128), F32)],
        compiler_params=params(),
        name="gate_backward_and_scan_backward",
    )(hid, square, inner, z, y, d, taps, w_all, x_conv, bc_conv, cols, cum_row, step_row, state)


MESHID = pl.DeviceIdType.MESH
ORDERS = (("x", "y", "z"), ("y", "z", "x"), ("z", "x", "y"))
SUB = 32


def neighbour(axis, s):
    if axis == "core":
        return {"core": 1 - lax.axis_index("core")}
    if axis == "y":
        y = lax.rem(lax.axis_index("yhi") * 2 + lax.axis_index("ylo") + (s + 4), 4)
        return {"ylo": lax.rem(y, 2), "yhi": y // 2}
    return {axis: lax.rem(lax.axis_index(axis) + (s + 4), 4)}


def my_place():
    return {"x": lax.axis_index("x"), "z": lax.axis_index("z"), "y": lax.axis_index("yhi") * 2 + lax.axis_index("ylo")}


def block_device(p):
    return {"z": p // 2, "yhi": lax.rem(p, 2)}


def f32(ref):
    return ref[...].astype(F32)


class Sender:
    def __init__(self):
        self.pending = {}

    def __call__(self, src, dst, send, recv, device):
        c = pltpu.make_async_remote_copy(src_ref=src, dst_ref=dst, send_sem=send, recv_sem=recv, device_id=device,
                                         device_id_type=MESHID)
        c.start()
        self.pending[id(c)] = c
        return c

    def sent(self, c):
        c.wait_send()
        del self.pending[id(c)]

    def all_sent(self):
        for c in self.pending.values():
            c.wait_send()


def greet():
    bar = pltpu.get_barrier_semaphore()
    for a in "xyz":
        for s in (1, 2, 3):
            pl.semaphore_signal(bar, inc=1, device_id=neighbour(a, s), device_id_type=MESHID)
    for d in (1, 2, 3):
        diagonal = {"z": lax.rem(lax.axis_index("z") + d, 4), "yhi": 1 - lax.axis_index("yhi")}
        pl.semaphore_signal(bar, inc=1, device_id=diagonal, device_id_type=MESHID)
    pl.semaphore_signal(bar, inc=1, device_id=neighbour("core", 1), device_id_type=MESHID)
    return lambda: pl.semaphore_wait(bar, 13)


def to_peers(rc, src_of, dst, send, recv, block):
    out = []
    for d in range(1, 8):
        p = lax.rem(block + d, 8)
        out.append(rc(src_of(p), dst.at[block], send.at[d], recv.at[d], block_device(p)))
    return out


class Gather:
    def __init__(self, rc, g, w, sems, item, r):
        self.rc, self.g, self.w, self.item, self.r = rc, g, w, item, r
        self.ts, self.tr, self.cs, self.cr = sems
        self.k = item * 3 + r
        self.me = my_place()
        self.core = lax.axis_index("core")
        self.forwarded = []

    def at(self, pos, lo=0, n=SUB):
        z = slice(None) if pos["z"] is None else pos["z"]
        x = slice(None) if pos["x"] is None else pos["x"]
        if pos["y"] is None:
            yh = yl = slice(None)
        else:
            yh, yl = pos["y"] // 2, lax.rem(pos["y"], 2)
        return self.g.at[self.item, z, yh, yl, x, self.core, pl.ds(self.r * SUB + lo, n)]

    def pos(self, st, d=0):
        p = {a: (None if i < st else self.me[a]) for i, a in enumerate(ORDERS[self.r])}
        a = ORDERS[self.r][st]
        p[a] = lax.rem(self.me[a] + (d + 4), 4)
        return p

    def to_sibling(self, ref, src=None):
        k = self.k * 10 + len(self.forwarded)
        self.forwarded.append(self.rc(ref if src is None else src, ref, self.cs.at[k], self.cr.at[k], neighbour("core", 1)))

    def send(self, st):
        a, t = ORDERS[self.r][st], self.k * 12 + st * 4
        ref = self.at(self.pos(st))
        src = ref if st else self.w.at[self.item, pl.ds(self.r * SUB, SUB)]
        self.c = [self.rc(src, ref, self.ts.at[t + i], self.tr.at[t + i], neighbour(a, d)) for i, d in enumerate((1, -1))]
        if st == 0:
            self.to_sibling(ref, src)

    def pass_on(self, st):
        a, t = ORDERS[self.r][st], self.k * 12 + st * 4 + 2
        self.f = []
        for i, d in enumerate((1, -1)):
            self.c[i].wait_recv()
            p = self.pos(st, -d)
            half = self.at(p, 16 * i, 16)
            self.f.append(self.rc(half, half, self.ts.at[t + i], self.tr.at[t + i], neighbour(a, d)))
            self.to_sibling(self.at(p))

    def last(self, st):
        for f in self.f:
            f.wait_recv()
        self.to_sibling(self.at(self.pos(st, 2)))

    def complete(self):
        for c in self.forwarded:
            c.wait_recv()


def forward_kernel(w_ref, bc_ref, dt_ref, pk_ref, hid, cot, gain, taps_bc,
                   g_ref, gb_ref, x_pre_out, x_conv_out, z_out, y_out, d_out,
                   normed_t, cot_t, pk, bc_pre, bc_conv, steps, cols, cum_row, step_row, state, dec, rates, square,
                   inner,
                   normed, halo, dts, small_own, small_all, x_pre, x_conv, zb, yb, db, wbuf, gram, local, rec_a, out_b, dec_own,
                   ts, tr, cs, cr, bs, br, ps, pr, qs, qr, es, er, fs, fr, ds, dr, hs, hr, lsem, wsem, osem):
    rc = Sender()
    me = my_place()
    core = lax.axis_index("core")
    x, ylo = me["x"], lax.axis_index("ylo")
    block = lax.axis_index("z") * 2 + lax.axis_index("yhi")
    arrived = greet()
    own_w = pltpu.make_async_copy(w_ref, g_ref.at[:, me["z"], me["y"] // 2, ylo, x, core], lsem.at[0])
    own_w.start()
    arrived()

    gx, gz, go = [[Gather(rc, g_ref, w_ref, (ts, tr, cs, cr), i, r) for r in range(3)] for i in range(3)]

    def each(group, name, *args):
        for c in group:
            getattr(c, name)(*args)

    each(gx, "send", 0)
    dt_c = to_peers(rc, lambda p: dt_ref, dts, ps, pr, block)
    pk_c = to_peers(rc, lambda p: pk_ref, pk, qs, qr, block)
    halo_c = rc(hid.at[pl.ds(ROWS - HALO, HALO)], halo, hs, hr, block_device(lax.rem(block + 1, 8)))
    each(gz, "send", 0)
    each(go, "send", 0)
    dts[block] = dt_ref[...]
    pk[block] = pk_ref[...]

    def normalize(part, at):
        v = part[...].astype(F32)
        r = lax.rsqrt(jnp.mean(v * v, axis=1, keepdims=True) + EPS)
        normed[pl.ds(at, part.shape[0])] = (v * r * gain[...]).astype(BF16)

    normalize(hid, HALO)
    own_w.wait()
    each(gx, "pass_on", 0)

    for c in dt_c:
        c.wait_recv()
    total = f32(dts.at[0])
    for i in range(1, 8):
        total = total + f32(dts.at[i])
    small_own[:, :256] = bc_ref[...]
    small_own[:, 256:] = total.astype(BF16)
    mine = gb_ref.at[ylo, x, core]
    own_b = pltpu.make_async_copy(small_own, mine, lsem.at[1])
    own_b.start()
    b_c = [rc(small_own, mine, bs.at[i], br.at[i], neighbour("x", d)) for i, d in enumerate((1, -1))]
    b_core = [rc(small_own, mine, bs.at[2], br.at[2], neighbour("core", 1))]
    normed_t[...] = normed[HALO:, :].T.reshape(8, 2, 96, ROWS)
    each(gx, "last", 0)
    each(gx, "send", 1)
    each(gz, "pass_on", 0)
    each(go, "pass_on", 0)
    b_f = []
    for i, d in enumerate((1, -1)):
        b_c[i].wait_recv()
        from_x = lax.rem(x - d + 4, 4)
        h = gb_ref.at[ylo, from_x, core, pl.ds(48 * i, 48)]
        b_f.append(rc(h, h, bs.at[3 + i], br.at[3 + i], neighbour("x", d)))
    cot_t[...] = cot[...].T.reshape(8, 2, 96, ROWS)
    each(gx, "pass_on", 1)
    for c in b_f:
        c.wait_recv()
    own_b.wait()
    line = gb_ref.at[ylo, :, core]
    b_y = rc(line, line, bs.at[5], br.at[5], {"ylo": 1 - ylo})
    for dx in (1, 2, 3):
        h = gb_ref.at[ylo, lax.rem(x + dx, 4), core]
        b_core.append(rc(h, h, bs.at[5 + dx], br.at[5 + dx], neighbour("core", 1)))
    each(gx, "last", 1)
    each(gx, "send", 2)
    each(gz, "last", 0)
    each(gz, "send", 1)
    each(go, "last", 0)
    each(go, "send", 1)
    halo_c.wait_recv()
    normalize(halo, 0)

    @pl.when(block == 0)
    def _():
        normed[pl.ds(0, HALO)] = jnp.zeros((HALO, WIDTH), BF16)

    b_y.wait_recv()
    line = gb_ref.at[1 - ylo, :, core]
    b_core.append(rc(line, line, bs.at[9], br.at[9], neighbour("core", 1)))
    for c in b_core:
        c.wait_recv()
    small_in = pltpu.make_async_copy(gb_ref, small_all, lsem.at[1])
    small_in.start()
    each(gz, "pass_on", 1)
    for c in pk_c:
        c.wait_recv()
    small_in.wait()

    def row(lo):
        pieces = [pk[m, 6:7, lo : lo + HEADS] for m in range(GROUPS)]
        return jnp.concatenate(pieces + [jnp.zeros((1, 80), F32)], axis=1)

    rates[0:1] = row(0)
    rates[1:2] = row(HEADS)
    rates[2:8] = jnp.zeros((6, 128), F32)
    small = dot(normed[...], small_all[...].reshape(WIDTH, COLS))
    bc_pre[...] = small[:, :256]
    pre = conv_pre(small[:, :256], taps_bc[...])
    bc_conv[...] = (pre * jax.nn.sigmoid(pre)).astype(BF16)
    shifted = small[HALO:, 256:384] + rates[1:2]
    steps[...] = shifted
    step = softplus(shifted)
    decay = -step * jnp.exp(rates[0:1])
    cum = dot(triangle(False).astype(F32), decay, precision=lax.Precision.HIGHEST)
    cum_t = cum.T
    step_t = step.T
    lasts = jnp.broadcast_to(jnp.exp(cum_t[:, ROWS - 1 : ROWS]), (128, 128))
    for m in range(GROUPS):
        at = slice(HEADS * m, HEADS * m + 8)
        cols[m] = jnp.concatenate([cum[:, at], step[:, at]], axis=1)
        cum_row[m] = cum_t[HEADS * m : HEADS * m + 8]
        step_row[m] = step_t[HEADS * m : HEADS * m + 8]
        dec_own[m] = lasts[HEADS * m : HEADS * m + 8]
    dec_c = to_peers(rc, lambda p: dec_own.at[p], dec, ds, dr, block)
    dec[block] = dec_own[block]
    gram[...] = jnp.where(triangle(False), dot(bc_conv[:, 128:], bc_conv[:, :128], (1, 1)), 0.0)
    each(gz, "last", 1)
    each(gz, "send", 2)
    each(gx, "pass_on", 2)
    each(go, "pass_on", 1)
    each(gx, "last", 2)
    each(gx, "complete")

    g_flat = g_ref.reshape(3, GROUPS, WIDTH, COLS)

    def weights(item, m):
        k = lax.rem(m, 2)
        return pltpu.make_async_copy(g_flat.at[item, m], wbuf.at[k], wsem.at[k])

    def over_groups(item, lo, hi, body):
        weights(item, lo).start()

        @pl.loop(lo, hi)
        def _(m):
            @pl.when(m < hi - 1)
            def _():
                weights(item, m + 1).start()

            weights(item, m).wait()
            body(m, wbuf.at[lax.rem(m, 2)])

    def second_group(m, w):
        ext = dot(normed[...], w[...])
        x_pre[m] = ext
        pre = conv_pre(ext, pk[m])
        xc = (pre * jax.nn.sigmoid(pre)).astype(BF16)
        x_conv[m] = xc
        cum, step = cols[m][:, :8], cols[m][:, 8:]
        weighted = (xc.astype(F32) * spread(step * jnp.exp(cum[ROWS - 1 : ROWS] - cum))).astype(BF16)
        local[m] = dot(weighted, bc_conv[:, :128], (0, 0)).astype(BF16)

    over_groups(0, 0, 4, second_group)
    each(go, "last", 1)
    over_groups(0, 4, GROUPS, second_group)
    a_c = to_peers(rc, lambda p: local.at[p], rec_a, es, er, block)
    rec_a[block] = local[block]
    each(gz, "pass_on", 2)
    each(go, "send", 2)
    outs = [pltpu.make_async_copy(x_pre, x_pre_out, osem.at[0]), pltpu.make_async_copy(x_conv, x_conv_out, osem.at[1])]

    def scan_group(m):
        xc = x_conv[m]
        cum = cols[m][:, :8]
        rows = cum_row[m]
        step_rows = step_row[m]
        parts = []
        for h in range(HEADS):
            decay = jnp.exp(jnp.minimum(cum[:, h : h + 1] - rows[h : h + 1, :], 0.0))
            mixing = (decay * gram[...] * step_rows[h : h + 1, :]).astype(BF16)
            parts.append(dot(mixing, xc[:, 64 * h : 64 * h + 64]))
        yb[m] = jnp.concatenate(parts, axis=1) + spread(pk[m, 6:7, 12:20]) * xc.astype(F32)

    for c in outs:
        c.start()
    pl.loop(0, 3)(scan_group)
    for c in dec_c + a_c:
        c.wait_recv()
    for h in range(HEADS):
        rows = pl.ds(64 * h, 64)
        run = jnp.zeros((64, 128), F32)
        for i in range(BLOCKS):
            out_b[i, rows] = run.astype(BF16)
            run = run * dec[i, pl.ds(h, 1)] + rec_a[i, rows].astype(F32)
    f_c = to_peers(rc, lambda p: out_b.at[p], state, fs, fr, block)
    state[block] = out_b[block]
    each(gz, "last", 2)
    pl.loop(3, GROUPS)(scan_group)
    each(go, "pass_on", 2)
    each(gz, "complete")

    def gate_group(m, w):
        zb[m] = dot(normed[HALO:, :], w[...])

    over_groups(1, 0, GROUPS, gate_group)
    z_c = pltpu.make_async_copy(zb, z_out, osem.at[2])
    z_c.start()
    each(go, "last", 2)
    for c in f_c:
        c.wait_recv()
    each(go, "complete")
    square[...] = jnp.zeros_like(square)
    inner[...] = jnp.zeros_like(inner)

    def out_group(m, w):
        carried = dot(bc_conv[:, 128:], state[m], (1, 1))
        y = yb[m] + spread(jnp.exp(cols[m][:, :8])) * carried
        yb[m] = y
        d = dot(cot[...], w[...])
        db[m] = d
        z = zb[m]
        gated = y * (z * jax.nn.sigmoid(z))
        sq = gated * gated
        ip = d * pk[m, 5:6] * gated
        square[...] += sq[:, :128] + sq[:, 128:256] + sq[:, 256:]
        inner[...] += ip[:, :128] + ip[:, 128:256] + ip[:, 256:]

    over_groups(2, 0, GROUPS, out_group)
    more = [pltpu.make_async_copy(yb, y_out, osem.at[3]), pltpu.make_async_copy(db, d_out, osem.at[4])]
    for c in more:
        c.start()
    for c in outs + [z_c] + more:
        c.wait()
    rc.all_sent()


def forward(w3, bc, dt, pk, hid, cot, gain, taps_bc):
    hbm = pl.BlockSpec(memory_space=pl.ANY)
    vmem = pl.BlockSpec(memory_space=pltpu.VMEM)
    sem = pltpu.SemaphoreType.DMA

    def v(*shape, dtype=F32):
        return pltpu.VMEM(shape, dtype)

    def b(*shape):
        return v(*shape, dtype=BF16)

    groups = (GROUPS, ROWS, COLS)
    return pl.pallas_call(
        forward_kernel,
        out_shape=(
            sds(3, 4, 2, 2, 4, 2, 96, COLS, dtype=BF16), sds(2, 4, 2, 96, COLS, dtype=BF16),
            sds(GROUPS, HALO + ROWS, COLS), sds(*groups, dtype=BF16), sds(*groups), sds(*groups), sds(*groups),
            sds(8, 2, 96, ROWS, dtype=BF16), sds(8, 2, 96, ROWS, dtype=BF16), sds(GROUPS, 8, COLS),
            sds(HALO + ROWS, 256), sds(ROWS, 256, dtype=BF16), sds(ROWS, 128), sds(GROUPS, ROWS, 16),
            sds(GROUPS, 8, ROWS), sds(GROUPS, 8, ROWS), sds(GROUPS, COLS, 128, dtype=BF16), sds(BLOCKS, 8, 128), sds(8, 128),
            sds(ROWS, 128), sds(ROWS, 128),
        ),
        in_specs=[hbm] + [vmem] * 7,
        out_specs=(hbm,) * 7 + (vmem,) * 14,
        scratch_shapes=[
            b(HALO + ROWS, WIDTH), b(HALO, WIDTH), b(BLOCKS, 96, 128), b(96, COLS), b(2, 4, 2, 96, COLS),
            v(GROUPS, HALO + ROWS, COLS), b(*groups), v(*groups), v(*groups), v(*groups), b(2, WIDTH, COLS), v(ROWS, ROWS),
            b(GROUPS, COLS, 128), b(GROUPS, COLS, 128), b(GROUPS, COLS, 128), v(GROUPS, 8, 128),
            sem((108,)), sem((108,)), sem((90,)), sem((90,)), sem((10,)), sem((10,)), sem((8,)), sem((8,)), sem((8,)),
            sem((8,)), sem((8,)), sem((8,)), sem((8,)), sem((8,)), sem((8,)), sem((8,)), sem, sem, sem((2,)), sem((2,)),
            sem((5,)),
        ],
        compiler_params=pltpu.CompilerParams(collective_id=0, has_side_effects=True, vmem_limit_bytes=60 * 2**20),
        name="forward_between_devices",
    )(w3, bc, dt, pk, hid, cot, gain, taps_bc)


class Total:
    def __init__(self, rc, value, core, xs, yl, yh, zs, send, recv):
        self.rc, self.value, self.core, self.xs, self.yl, self.yh, self.zs = rc, value, core, xs, yl, yh, zs
        self.send, self.recv, self.at = send, recv, 0
        self.me = my_place()

    def push(self, dst, device):
        k = self.at
        self.at += 1
        return self.rc(self.value, dst, self.send.at[k], self.recv.at[k], device)

    def done(self):
        for c in self.flying:
            c.wait_recv()
        for c in self.flying:
            self.rc.sent(c)

    def step(self, j):
        v, me = self.value, self.me
        if j == 0:
            self.flying = [self.push(self.core, neighbour("core", 1))]
        elif j == 1:
            self.done()
            v[...] = v[...] + self.core[...]
            self.xs[me["x"]] = v[...]
            self.flying = [self.push(self.xs.at[me["x"]], neighbour("x", d)) for d in (1, 2, 3)]
        elif j == 2:
            self.done()
            v[...] = (self.xs[0] + self.xs[1]) + (self.xs[2] + self.xs[3])
            self.flying = [self.push(self.yl, {"ylo": 1 - lax.axis_index("ylo")})]
        elif j == 3:
            self.done()
            v[...] = v[...] + self.yl[...]
            self.flying = [self.push(self.yh, {"yhi": 1 - lax.axis_index("yhi")})]
        elif j == 4:
            self.done()
            v[...] = v[...] + self.yh[...]
            self.zs[me["z"]] = v[...]
            self.flying = [self.push(self.zs.at[me["z"]], neighbour("z", d)) for d in (1, 2, 3)]
        elif j == 5:
            self.done()
            v[...] = (self.zs[0] + self.zs[1]) + (self.zs[2] + self.zs[3])


class SmallSum:
    def __init__(self, rc, parts, sib, xs, ys, zs, hs, send, recv):
        self.rc, self.parts, self.sib, self.xs, self.ys, self.zs, self.hs = rc, parts, sib, xs, ys, zs, hs
        self.send, self.recv = send, recv
        self.me = my_place()

    def step(self, j, out=None):
        rc, me, parts, s, r = self.rc, self.me, self.parts, self.send, self.recv
        core, ylo = lax.axis_index("core"), lax.axis_index("ylo")
        if j == 0:
            self.c = [rc(parts.at[:, :, 1 - core], self.sib, s.at[0], r.at[0], neighbour("core", 1))]
        elif j == 1:
            self.c[0].wait_recv()

            def one(x):
                for yl in range(2):
                    m = parts.at[yl, x, core]
                    m[...] = (f32(m) + f32(self.sib.at[yl, x])).astype(BF16)

            pl.loop(0, 4)(one)
            self.c = [rc(parts.at[:, lax.rem(me["x"] + d, 4), core], self.xs.at[d - 1], s.at[d], r.at[d], neighbour("x", d))
                      for d in (1, 2, 3)]
        elif j == 2:
            for c in self.c:
                c.wait_recv()
            for yl in range(2):
                m = parts.at[yl, me["x"], core]
                m[...] = (f32(m) + f32(self.xs.at[0, yl]) + f32(self.xs.at[1, yl]) + f32(self.xs.at[2, yl])).astype(BF16)
            self.c = [rc(parts.at[1 - ylo, me["x"], core], self.ys, s.at[4], r.at[4], {"ylo": 1 - ylo})]
        elif j == 3:
            self.c[0].wait_recv()
            m = parts.at[ylo, me["x"], core]
            m[...] = (f32(m) + f32(self.ys)).astype(BF16)
            self.zs[me["z"]] = m[...]
            self.c = [rc(m, self.zs.at[me["z"]], s.at[4 + d], r.at[4 + d], neighbour("z", d)) for d in (1, 2, 3)]
        elif j == 4:
            for c in self.c:
                c.wait_recv()
            z, hs = self.zs, self.hs
            hs[0] = ((f32(z.at[0]) + f32(z.at[1])) + (f32(z.at[2]) + f32(z.at[3]))).astype(BF16)
            self.c = [rc(hs.at[0], hs.at[1], s.at[8], r.at[8], {"yhi": 1 - lax.axis_index("yhi")})]
        elif j == 5:
            self.c[0].wait_recv()
            out[...] = f32(self.hs.at[0]) + f32(self.hs.at[1])


SLOTS = 4
LAG = 2


def part_of(ref, item, pos, lo, n):
    z = slice(None) if pos["z"] is None else pos["z"]
    x = slice(None) if pos["x"] is None else pos["x"]
    if pos["y"] is None:
        yh = yl = slice(None)
    else:
        yh, yl = pos["y"] // 2, lax.rem(pos["y"], 2)
    return ref.at[item, z, yh, yl, x, pl.ds(lo, n)]


class Chunk:
    def __init__(self, rc, own, out, bufs, sems, item, slot, wide, r):
        self.rc, self.own, self.out, self.item, self.slot, self.r = rc, own, out, item, slot, r
        full, half, second, third = bufs
        self.full, self.half = full[r].at[wide], half[r].at[wide]
        self.direct = {1: second[r].at[slot], 2: third.at[slot * 3 + r]}
        self.send, self.recv = sems
        self.base = (slot * 3 + r) * 10
        self.me = my_place()

    def slab(self, st, d, lo=0, n=SUB):
        p = {a: (self.me[a] if i < st else None) for i, a in enumerate(ORDERS[self.r])}
        a = ORDERS[self.r][st]
        p[a] = lax.rem(self.me[a] + (d + 4), 4)
        return part_of(self.own, self.slot, p, self.r * SUB + lo, n)

    def loop(self, st, body):
        sizes = []
        for a, n in (("z", (4,)), ("y", (2, 2)), ("x", (4,))):
            if ORDERS[self.r].index(a) > st:
                sizes += n
        if not sizes:
            body(())
        elif len(sizes) == 1 or sizes == [2, 2]:
            for i in range(4):
                body((i,) if len(sizes) == 1 else (i // 2, i % 2))
        else:
            @pl.loop(0, 4)
            def _(i):
                for k in range(4):
                    if sizes == [4, 4]:
                        body((i, k))
                    elif sizes == [4, 2, 2]:
                        body((i, k // 2, k % 2))
                    else:
                        body((i // 2, lax.rem(i, 2), k))

    def push(self, k, src, dst, st, d):
        t = self.base + k
        return self.rc(src, dst, self.send.at[t], self.recv.at[t], neighbour(ORDERS[self.r][st], d))

    def far(self):
        self.far_c = [self.push(i, self.slab(0, 2, 16 * i, 16), self.half.at[i], 0, d) for i, d in enumerate((1, -1))]

    def near(self):
        self.near_c = []
        for i, d in enumerate((1, -1)):
            self.far_c[i].wait_recv()
            mine = self.slab(0, d, 16 * i, 16)

            def add(index, mine=mine, i=i):
                m = mine.at[index]
                m[...] = m[...] + self.half[(i, *index)]

            self.loop(0, add)
            self.near_c.append(self.push(2 + i, self.slab(0, d), self.full.at[i], 0, d))

    def straight(self, st):
        self.straight_c = [self.push(1 + 3 * st + d - 1, self.slab(st, d), self.direct[st].at[d - 1], st, d) for d in (1, 2, 3)]

    def step(self, j):
        if j == 0:
            self.far()
        elif j == 1:
            self.near()
        elif j == 2:
            for c in self.near_c:
                c.wait_recv()
            mine = self.slab(0, 0)

            def add(index):
                m = mine.at[index]
                m[...] = (f32(m) + f32(self.full.at[(0, *index)]) + f32(self.full.at[(1, *index)])).astype(BF16)

            self.loop(0, add)
            self.straight(1)
        else:
            for c in self.straight_c:
                c.wait_recv()
            st = j - 2
            mine = self.slab(st, 0)
            got = self.direct[st]

            def total(index):
                m = mine.at[index] if index else mine
                return (f32(m) + f32(got.at[(0, *index)])) + (f32(got.at[(1, *index)]) + f32(got.at[(2, *index)]))

            if st == 1:
                def add(index):
                    mine[index] = total(index).astype(BF16)

                self.loop(1, add)
                self.straight(2)
            else:
                self.out[self.item, pl.ds(self.r * SUB, SUB)] = total(())


def backward_kernel(g_ref, x_conv_ref, d_x_ref, x_pre_ref, cols_ref, d_cols_ref,
                    w_small, n_t, c_t, hid, cot, out_in, d_z, d_local, state, dec, taps, d_bc_in, bc_pre, bc_conv, taps_bc,
                    shifted, a_log, gain, gain_part, skip_part,
                    out_ref, sout_ref, vout_ref, nout_ref, grad_hidden, *scr):
    (own, send, sib, rec_a, out_b, rec_b, dxp, tails, halo_src, halo_dst, acc, wbuf, bxc, bdx, bxp, bcols, bdc,
     d_b, d_all, parts, s_sib, s_xs, s_ys, s_zs, s_hs,
     v_core, v_xs, v_yl, v_yh, v_zs, n_core, n_xs, n_yl, n_yh, n_zs) = scr[:35]
    bufs = [scr[35:38], scr[38:41], scr[41:44], scr[44]]
    (t_s, t_r, c_s, c_r, e_s, e_r, b_s, b_r, h_s, h_r, ss, sr, vs, vr, ns, nr, wsem, lsem, credit, freed) = scr[45:]
    rc = Sender()
    core = lax.axis_index("core")
    block = lax.axis_index("z") * 2 + lax.axis_index("yhi")
    greet()()

    to_owner = []
    for d in range(1, 8):
        p = lax.rem(block + d, 8)
        to_owner.append(rc(d_local.at[p], rec_a.at[block], e_s.at[d], e_r.at[d], block_device(p)))
    rec_a[block] = d_local[block]

    def core_copy(m):
        k = lax.rem(m, SLOTS)
        return pltpu.make_async_remote_copy(src_ref=send.at[k], dst_ref=sib.at[k], send_sem=c_s.at[k], recv_sem=c_r.at[k],
                                            device_id=neighbour("core", 1), device_id_type=MESHID)

    def gradient(lhs_t, rhs, slot, first_item):
        def one(m):
            @pl.when(m < GROUPS)
            def _():
                k = lax.rem(m, SLOTS)

                def wait_slot():
                    core_copy(m).wait_send()
                    pl.semaphore_wait(credit, 1)

                if first_item:
                    pl.when(m >= SLOTS)(wait_slot)
                else:
                    wait_slot()
                v = dot(lhs_t.at[:, 1 - core][...].reshape(768, ROWS), rhs[m])
                send[k] = v.astype(BF16).reshape(2, 4, 96, COLS)
                core_copy(m).start()

            @pl.when(m >= LAG)
            def _():
                q = m - LAG
                k = lax.rem(q, SLOTS)
                core_copy(q).wait_recv()
                v = dot(lhs_t.at[:, core][...].reshape(768, ROWS), rhs[q])
                own[slot, q // 2, lax.rem(q, 2)] = (v + sib[k].reshape(768, COLS).astype(F32)).astype(BF16).reshape(2, 4, 96, COLS)
                pl.semaphore_signal(credit, inc=1, device_id=neighbour("core", 1), device_id_type=MESHID)

        pl.loop(0, GROUPS + LAG)(one)

    def chunks(item, slot, wide):
        return [Chunk(rc, own, out_ref, bufs, (t_s, t_r), item, slot, wide, r) for r in range(3)]

    def steps(cs, j):
        for c in cs:
            c.step(j)

    oc, zc, xc_ = chunks(2, 0, 0), chunks(1, 1, 1), chunks(0, 2, 0)

    gradient(c_t, out_in, 0, True)
    steps(oc, 0)

    for c in to_owner:
        c.wait_recv()
    for h in range(HEADS):
        rows = pl.ds(64 * h, 64)
        run = jnp.zeros((64, 128), F32)
        for i in range(BLOCKS - 1, -1, -1):
            out_b[i, rows] = run.astype(BF16)
            run = run * dec[i, pl.ds(h, 1)] + rec_a[i, rows].astype(F32)
    back = []
    for d in range(1, 8):
        p = lax.rem(block + d, 8)
        back.append(rc(out_b.at[p], rec_b.at[block], b_s.at[d], b_r.at[d], block_device(p)))
    rec_b[block] = out_b[block]

    gradient(n_t, d_z, 1, False)
    steps(oc, 1)
    steps(zc, 0)
    for c in back:
        c.wait_recv()

    streams = ((x_conv_ref, bxc), (d_x_ref, bdx), (x_pre_ref, bxp), (cols_ref, bcols), (d_cols_ref, bdc))

    def load(m):
        k = lax.rem(m, 2)
        return [pltpu.make_async_copy(src.at[m], dst.at[k], lsem.at[k, i]) for i, (src, dst) in enumerate(streams)]

    def fifth_group(m):
        k = lax.rem(m, 2)

        @pl.when(m < GROUPS - 1)
        def _():
            for c in load(m + 1):
                c.start()

        for c in load(m):
            c.wait()
        ds = rec_b[m]
        xf = bxc[k].astype(F32)
        cum, step = bcols[k][:, :8], bcols[k][:, 8:]
        last = cum[ROWS - 1 : ROWS]
        tail = jnp.exp(last - cum)
        weights = step * tail
        wide = spread(weights)
        d_weighted = dot(bc_conv[:, :128], ds, (1, 1))
        d_b[...] += dot((xf * wide).astype(BF16), ds)
        dx = bdx[k] + wide * d_weighted
        d_weights = gathered_heads(d_weighted * xf)
        both = weights * d_weights
        lane = lax.broadcasted_iota(jnp.int32, (1, 8), 1)
        product = jnp.sum(state[m].astype(F32) * ds.astype(F32), axis=1, keepdims=True)
        d_last = jnp.sum(both, axis=0, keepdims=True)
        for h in range(HEADS):
            dots = jnp.sum(product[64 * h : 64 * h + 64], axis=0, keepdims=True)
            d_last = jnp.where(lane == h, d_last + jnp.exp(last) * dots, d_last)
        row = lax.broadcasted_iota(jnp.int32, (ROWS, 8), 0)
        d_cum = bdc[k][:, :8] - both
        d_cum = jnp.where(row == ROWS - 1, d_cum + d_last, d_cum)
        d_all[m] = jnp.concatenate([d_cum, bdc[k][:, 8:] + tail * d_weights], axis=1)
        ext = bxp[k]
        tap = taps[m]
        pre = conv_pre(ext, tap)
        sig = jax.nn.sigmoid(pre)
        dp = dx * (sig * (1.0 + pre * (1.0 - sig)))
        v_value[m] = conv_grads(dp, ext, gain_part[m], skip_part[m])
        whole_dx = conv_transposed(jnp.concatenate([dp, jnp.zeros((8, COLS), F32)], axis=0), tap)
        dxp[m] = whole_dx.astype(BF16)
        tails[m] = whole_dx[ROWS - 16 :]
        halo_src[m] = dp[:8]

    v_value = vout_ref
    d_b[...] = jnp.zeros_like(d_b)
    for c in load(0):
        c.start()
    pl.loop(0, 4)(fifth_group)
    steps(zc, 1)
    pl.loop(4, GROUPS)(fifth_group)

    d_bc = jnp.concatenate([d_bc_in[:, :128] + d_b[...], d_bc_in[:, 128:]], axis=1)
    ext = bc_pre[...]
    pre = conv_pre(ext, taps_bc[...])
    sig = jax.nn.sigmoid(pre)
    dp_bc = d_bc * (sig * (1.0 + pre * (1.0 - sig)))
    halo_src[GROUPS] = jnp.concatenate([dp_bc[:8], jnp.zeros((8, 128), F32)], axis=1)
    before = lax.rem(block + 7, 8)
    halo = rc(halo_src, halo_dst, h_s, h_r, block_device(before))
    steps(oc, 2)
    for a in "xyz":
        for s in (1, -1):
            pl.semaphore_signal(freed, inc=1, device_id=neighbour(a, s), device_id_type=MESHID)
    zero8 = jnp.zeros((1, 256), F32)
    d_cum = jnp.concatenate([d_all[m][:, :HEADS] for m in range(GROUPS)] + [jnp.zeros((ROWS, 80), F32)], axis=1)
    d_step = jnp.concatenate([d_all[m][:, 8 : 8 + HEADS] for m in range(GROUPS)] + [jnp.zeros((ROWS, 80), F32)], axis=1)
    d_decay = dot(triangle(True).astype(F32), d_cum, precision=lax.Precision.HIGHEST)
    rate = -jnp.exp(a_log[0:1])
    v = shifted[...]
    d_dt = (d_step + rate * d_decay) * jax.nn.sigmoid(v)
    log_grad = jnp.sum(d_decay * (softplus(v) * rate), axis=0, keepdims=True)
    shift_grad = jnp.sum(d_dt, axis=0, keepdims=True)
    bc_rows = conv_grads(dp_bc, ext, jnp.concatenate([log_grad, shift_grad], axis=1), zero8)
    v_value[GROUPS] = jnp.concatenate([bc_rows, jnp.zeros((8, 128), F32)], axis=1)
    vec = Total(rc, v_value, v_core, v_xs, v_yl, v_yh, v_zs, vs, vr)
    vec.step(0)

    halo.wait_recv()
    inside = block < 7

    def below(k):
        return jnp.where(inside, halo_dst[k], 0.0)

    def fix(m):
        ext = jnp.concatenate([jnp.zeros((16, COLS), F32), below(m)], axis=0)
        dxp[m, pl.ds(ROWS - 16, 16)] = (tails[m] + conv_transposed(ext, taps[m], 16)).astype(BF16)

    pl.loop(0, GROUPS)(fix)
    d_bc = conv_transposed(jnp.concatenate([dp_bc, below(GROUPS)[:, :256]], axis=0), taps_bc[...])
    small = jnp.concatenate([d_bc, d_dt], axis=1).astype(BF16)
    def weights(m):
        k = lax.rem(m, 2)
        return [pltpu.make_async_copy(g_ref.at[i, m], wbuf.at[k, i], wsem.at[k, i]) for i in range(2)]

    for c in weights(0):
        c.start()
    gradient(n_t, dxp, 2, False)
    pl.semaphore_wait(freed, 6)
    steps(xc_, 0)
    steps(oc, 3)
    steps(zc, 2)
    for i in range(2):
        lhs = n_t.at[:, i][...].reshape(768, ROWS)
        parts[:, :, i] = dot(lhs, small).astype(BF16).reshape(2, 4, 96, COLS)
    sums = SmallSum(rc, parts, s_sib, s_xs, s_ys, s_zs, s_hs, ss, sr)
    sums.step(0)
    acc[...] = dot(small, w_small[...], (1, 1))

    def input_group(m):
        k = lax.rem(m, 2)

        @pl.when(m < GROUPS - 1)
        def _():
            for c in weights(m + 1):
                c.start()

        for c in weights(m):
            c.wait()
        lhs = jnp.concatenate([dxp[m], d_z[m]], axis=1)
        rhs = jnp.concatenate([wbuf[k, 0], wbuf[k, 1]], axis=1)
        acc[...] += dot(lhs, rhs, (1, 1))

    pl.loop(0, 2)(input_group)
    steps(xc_, 1)
    pl.loop(2, 5)(input_group)
    steps(oc, 4)
    steps(zc, 3)
    sums.step(1)
    vec.step(1)
    pl.loop(5, GROUPS)(input_group)
    sums.step(2)
    vec.step(2)
    v = hid[...].astype(F32)
    r = lax.rsqrt(jnp.mean(v * v, axis=1, keepdims=True) + EPS)
    unit = v * r
    dn = acc[...]
    gain_grad = jnp.sum(dn * unit, axis=0, keepdims=True)
    for i in range(4):
        nout_ref[0, pl.ds(i, 1)] = gain_grad[:, COLS * i : COLS * i + COLS]
    nout_ref[0, pl.ds(4, 4)] = jnp.zeros((4, COLS), F32)
    nvec = Total(rc, nout_ref, n_core, n_xs, n_yl, n_yh, n_zs, ns, nr)
    nvec.step(0)
    steps(xc_, 2)
    nvec.step(1)
    d_in = dn * gain[...]
    grad_hidden[...] = r * (d_in - unit * jnp.mean(d_in * unit, axis=1, keepdims=True)) + cot[...].astype(F32)
    sums.step(3)
    vec.step(3)
    steps(zc, 4)
    nvec.step(2)
    steps(xc_, 3)
    sums.step(4)
    vec.step(4)
    nvec.step(3)
    sums.step(5, sout_ref)
    vec.step(5)
    steps(xc_, 4)
    nvec.step(4)
    nvec.step(5)
    for k in range(SLOTS):
        core_copy(GROUPS - SLOTS + k).wait_send()
    pl.semaphore_wait(credit, SLOTS)
    rc.all_sent()


def backward(w_all, x_conv, d_x, x_pre, cols, d_cols, w_small, n_t, c_t, hid, cot, out_in, d_z, d_local,
             state, dec, taps, d_bc, bc_pre, bc_conv, taps_bc, shifted, a_log, gain, gain_part, skip_part):
    hbm = pl.BlockSpec(memory_space=pl.ANY)
    vmem = pl.BlockSpec(memory_space=pltpu.VMEM)
    sem = pltpu.SemaphoreType.DMA

    def buf(*shape, dtype=BF16):
        return pltpu.VMEM((*shape, COLS), dtype)

    def v(*shape, dtype=F32):
        return pltpu.VMEM(shape, dtype)

    scratch = [
        buf(3, 4, 2, 2, 4, 96), buf(SLOTS, 2, 4, 96), buf(SLOTS, 2, 4, 96),
        v(GROUPS, COLS, 128, dtype=BF16), v(GROUPS, COLS, 128, dtype=BF16), v(GROUPS, COLS, 128, dtype=BF16),
        buf(GROUPS, ROWS), buf(GROUPS, 16, dtype=F32), buf(GROUPS + 1, 8, dtype=F32), buf(GROUPS + 1, 8, dtype=F32),
        v(ROWS, WIDTH), buf(2, 2, WIDTH),
        buf(2, ROWS), buf(2, ROWS, dtype=F32), buf(2, HALO + ROWS, dtype=F32),
        v(2, ROWS, 16), v(2, ROWS, 16),
        v(ROWS, 128), v(GROUPS, ROWS, 16),
        buf(2, 4, 2, 96), buf(2, 4, 96), buf(3, 2, 96), buf(96), buf(4, 96), buf(2, 96),
    ]
    for n in (GROUPS + 1, 1):
        one = buf(n, 8, dtype=F32)
        four = buf(4, n, 8, dtype=F32)
        scratch += [one, four, one, one, four]
    scratch += [buf(2, 2, 4, 2, 2, SUB), buf(2, 2, 4, 4, SUB), buf(2, 2, 2, 2, 4, SUB)]
    scratch += [buf(2, 2, 4, 2, 2, 16), buf(2, 2, 4, 4, 16), buf(2, 2, 2, 2, 4, 16)]
    scratch += [buf(3, 3, 4, SUB), buf(3, 3, 4, SUB), buf(3, 3, 2, 2, SUB), buf(9, 3, SUB)]
    scratch += [sem((90,)), sem((90,)), sem((SLOTS,)), sem((SLOTS,)), sem((8,)), sem((8,)), sem((8,)), sem((8,)),
                sem, sem, sem((9,)), sem((9,)), sem((9,)), sem((9,)), sem((9,)), sem((9,)), sem((2, 2)), sem((2, 5)),
                pltpu.SemaphoreType.REGULAR, pltpu.SemaphoreType.REGULAR]
    return pl.pallas_call(
        backward_kernel,
        out_shape=(sds(3, 96, COLS), sds(96, COLS), sds(GROUPS + 1, 8, COLS), sds(1, 8, COLS), sds(ROWS, WIDTH)),
        in_specs=[hbm] * 6 + [vmem] * 20,
        out_specs=(vmem,) * 5,
        scratch_shapes=scratch,
        compiler_params=pltpu.CompilerParams(collective_id=1, has_side_effects=True, vmem_limit_bytes=63 * 2**20),
        name="backward_between_devices",
    )(w_all, x_conv, d_x, x_pre, cols, d_cols, w_small, n_t, c_t, hid, cot, out_in, d_z, d_local,
      state, dec, taps, d_bc, bc_pre, bc_conv, taps_bc, shifted, a_log, gain, gain_part, skip_part)
def shards(hidden, grad_out, norm_gain, w_zx, w_bc, w_dt, conv_x, conv_bc, a_log, dt_bias, d_skip, gate_gain, w_out):
    index = lax.axis_index(MP)
    heads = jnp.concatenate([a_log, dt_bias, d_skip, jnp.zeros((COLS - 3 * HEADS,), F32)])[None]
    packed = jnp.concatenate([conv_x, gate_gain[None], heads, jnp.zeros((1, COLS), F32)])
    steps_own = lax.dynamic_update_slice(jnp.zeros((96, 128), BF16), w_dt, (0, index * HEADS))
    taps_bc = jnp.pad(conv_bc, ((0, 3), (0, 0)))
    gain = norm_gain[None]
    (w_all, w_small, x_pre, x_conv, z, y, d, normed_t, cot_t, taps, bc_pre, bc_conv, shifted, cols, cum_row,
     step_row, state, decays, rates, square, inner) = forward(
        jnp.stack([w_zx[:, 1], w_zx[:, 0], w_out.T]), w_bc, steps_own, packed, hidden, grad_out, gain, taps_bc)
    w_all = w_all.reshape(3, GROUPS, WIDTH, COLS)
    w_small = w_small.reshape(WIDTH, COLS)
    result, out_in, d_z, d_x, d_local, d_cols, d_bc, gain_part, skip_part = fourth(
        hidden, square, inner, z, y, d, taps, w_all, x_conv, bc_conv, cols, cum_row, step_row, state)
    owned, small, vector, norm_sum, grad_hidden = backward(
        w_all, x_conv, d_x, x_pre, cols, d_cols, w_small, normed_t, cot_t, hidden, grad_out, out_in, d_z,
        d_local, state, decays, taps, d_bc, bc_pre, bc_conv, taps_bc, shifted,
        rates, gain, gain_part, skip_part)

    def own(flat):
        return lax.dynamic_slice_in_dim(flat, index * HEADS, HEADS, flat.ndim - 1)

    mine = lax.dynamic_index_in_dim(vector, index, 0, keepdims=False)
    return (
        result,
        grad_hidden,
        norm_sum[0, :4].reshape(WIDTH),
        jnp.stack([owned[1], owned[0]], axis=1),
        small[:, :256],
        own(small[:, 256:304]),
        mine[:5],
        vector[GROUPS, :5, :256],
        own(vector[GROUPS, 5, :48]),
        own(vector[GROUPS, 5, 128:176]),
        mine[6].reshape(HEADS, 64).sum(axis=1),
        mine[5],
        owned[2].T,
    )


def solution(mesh):
    finer = Mesh(mesh.devices.reshape(2, 4, 2, 4, 2), DP_MP)
    rows = P(DP_MP, None)
    placed = (rows, rows, P(), P(DP, None, MP), P(DP, None), P(DP, MP), P(None, MP), P(), P(MP), P(MP), P(MP), P(MP),
              P(MP, DP))
    return jax.shard_map(
        shards,
        mesh=finer,
        in_specs=placed,
        out_specs=(rows, rows, P(), P(DP, None, MP), P(DP, None), P(DP, MP), P(None, MP), P(), P(MP), P(MP), P(MP), P(MP),
                   P(MP, DP)),
        check_vma=False,
    )
```

time: 378 us -> 314 us (0.83)
  starting transfers between devices: 28.3 us -> 0 us
  waiting for transfers between devices: 25.2 us -> 0 us
  local copies, waits for them, and re-layouts: 28.7 us -> 19.9 us
  other arithmetic: 9.08 us -> 4.39 us
    all_to_all x4 -> x0, waiting for transfers between devices: 25.2 us -> none  [the longest x3 25.2 us: swapped(): return lax.all_to_all(array, MP, split_axis=0, concat_axis=0, tiled=True)]
    all_to_all x4 -> x0, starting transfers between devices: 22.9 us -> none  [the longest x3 14.9 us: swapped(): return lax.all_to_all(array, MP, split_axis=0, concat_axis=0, tiled=True)]
    pallas_call x4 -> x1, Pallas kernels: 118 us -> 131 us  [forward(): pl.pallas_call(forward_kernel, out_shape=(sds(3, 4, 2, 2, 4, 2, 96, COLS,...]
    pallas_call x1, Pallas kernels: 135 us -> 126 us  [backward(): pl.pallas_call(backward_kernel, out_shape=(sds(3, 96, COLS), sds(96, COLS...]
    ppermute x1 -> x0, starting transfers between devices: 5.42 us -> none  [shards(): halo = lax.ppermute(hidden[-HALO:], MP, down)]
    unnamed x6 -> x0, other arithmetic: 4.69 us -> none
  transfers between devices with their start and end apart: 5 -> 0, of which waited for: 2 -> 0; matrix products, arithmetic and copies ran while one was open for 3% -> 0% of each run, Pallas kernels for 25% -> 0%
where the time goes in v2:
time: 314 us; the launch traced here: 312 us
  Pallas kernels  287 us (91%)
  local copies, waits for them, and re-layouts  19.9 us (6%)
  other arithmetic  4.39 us (1%)
    pallas_call x1, Pallas kernels, forward(): pl.pallas_call(forward_kernel, out_shape=(sds(3, 4, 2, 2, 4, 2, 96, COLS,...  131 us
    pallas_call x1, Pallas kernels, backward(): pl.pallas_call(backward_kernel, out_shape=(sds(3, 96, COLS), sds(96, COLS...  126 us
    pallas_call x1, Pallas kernels, fourth(): pl.pallas_call(fourth_kernel, grid=(GROUPS,), in_specs=[whole(ROWS, WIDTH...  30.4 us

profile of v2, /device:TPU:0, one launch (start us, length us, event | category | flops | bytes accessed | tf_op | source)
XLA Modules:
  0.0 311.8 jit_solution(13298084565428765030)
XLA Ops:
  0.7 0.8 copy.28
  1.5 0.2 dynamic_update_slice.3.dt_ref
  1.6 0.0 copy-start.1
  1.7 1.2 fusion.2
  2.9 1.6 pad_maximum_fusion.1.w_ref
  4.5 1.3 pad.4.taps_bc
  5.8 1.3 broadcast_in_dim.23.gain
  7.1 0.8 pad_maximum_fusion.2
  7.9 0.7 broadcast_in_dim.19
  8.6 0.1 pad.10.clone
  8.7 1.4 maximum_maximum_fusion.pk_ref
  10.0 0.0 copy-done.1
  10.0 130.9 %forward_between_devices.1 = (bf16[3,4,2,2,4,2,96,384]{7,6,5,4,3,2,1,0:T(8,128)(2,1)}, bf16[2,4,2,96,384]{4,3,2,1,0:T(8,128)(2,1)}, f32[8,272,384]{2,1,0:T(8,128...) custom-call(bf16[3,96,384]{2,1,0:T(8,128)(2,1)} %pad_maximum_fusion., ...), custom_call_target="tpu_custom_call" | custom-call | tf_op jit(solution)/shard_map/forward_between_devices/pallas_call | solution.py:573
  140.9 30.4 %gate_backward_and_scan_backward.1 = (bf16[256,1536]{1,0:T(8,128)(2,1)}, bf16[8,256,384]{2,1,0:T(8,128)(2,1)}, bf16[8,256,384]{2,1,0:T(8,128)(2,1)}, f32[8,256,3...) custom-call(bf16[256,1536]{1,0:T(8,128)(2,1)} %hid.5, ...), custom_call_target="tpu_custom_call" | custom-call | tf_op jit(solution)/shard_map/gate_backward_and_scan_backward/pallas_call | solution.py:186
  171.3 125.6 %backward_between_devices.1 = (f32[3,96,384]{2,1,0:T(8,128)}, f32[96,384]{1,0:T(8,128)}, f32[9,8,384]{2,1,0:T(8,128)}, f32[1,8,384]{2,1,0:T(8,128)}, f32[256,1536]{1,0:T(8,128)}) custom-call(bf16[3,8,1536,384]{3,2,1,0:T(8,128)(2,1)} %bitcast.27, bf16[8,256,384]{2,1,0:T(8,128)(2,1)} %get-tuple-element.55.x_conv.x_conv_ref, ...), custom_call_target="tpu_custom_call" | custom-call | tf_op jit(solution)/shard_map/backward_between_devices/pallas_call | solution.py:1088
  296.9 0.0 copy-start
  296.9 1.9 slice_bitcast_fusion
  298.8 0.9 copy.29
  299.7 0.8 slice.53
  300.5 0.1 constant_dynamic-slice_fusion.2
  300.6 0.7 copy.30
  301.3 1.5 slice.52
  302.8 1.3 dynamic-slice_bitcast_fusion
  304.1 1.4 dynamic-slice_reduce_fusion
  305.5 0.1 reshape_squeeze.7
  305.6 0.6 reduce_sum.9
  306.2 0.7 fusion.3
  306.9 0.6 fusion
  307.5 0.6 fusion.1
  308.1 0.7 slice.49
  308.8 0.6 reshape_squeeze.6
  309.4 1.3 slice_bitcast_fusion.3
  310.7 0.0 copy-done
  310.7 1.1 copy.37
  (5 shorter events, 0.1 us)
Async XLA Ops:
  1.6 8.4 %copy-start.1 = (bf16[96,128]{1,0:T(8,128)(2,1)}, bf16[96,128]{1,0:T(8,128)(2,1)S(1)}, u32[]{:S(2)}) copy-start(bf16[96,128]{1,0:T(8,128)(2,1)S(1)} %dynamic_update_slice.3.dt_ref) | copy-start | bytes 73732
  296.9 13.8 %copy-start = (f32[256,1536]{1,0:T(8,128)S(1)}, f32[256,1536]{1,0:T(8,128)}, u32[]{:S(2)}) copy-start(f32[256,1536]{1,0:T(8,128)} %get-tuple-element.121) | copy-start | bytes 4718596

commit v3 on v2

v3 whole, which is shorter than its diff:
```python
import jax
import jax.numpy as jnp
from jax import lax
from jax.experimental import pallas as pl
from jax.experimental.pallas import tpu as pltpu
from jax.sharding import Mesh
from jax.sharding import PartitionSpec as P

MP = ("z", "yhi")
DP = ("ylo", "x", "core")
DP_MP = DP + MP
BLOCKS = 8
F32 = jnp.float32
BF16 = jnp.bfloat16
ROWS = 256
WIDTH = 1536
GROUPS = 8
COLS = 384
HEADS = 6
HALO = 16
EPS = 1e-05
INNER = GROUPS * COLS
VMEM_LIMIT = 56 * 2**20


def dot(a, b, contract=(1, 0), precision=None):
    return lax.dot_general(
        a, b, (((contract[0],), (contract[1],)), ((), ())),
        preferred_element_type=F32, precision=precision,
    )


def spread(per_head):
    rows = per_head.shape[0]
    low = lax.broadcasted_iota(jnp.int32, (rows, 128), 1) < 64
    tiles = [
        jnp.where(low, per_head[:, 2 * i : 2 * i + 1], per_head[:, 2 * i + 1 : 2 * i + 2])
        for i in range(COLS // 128)
    ]
    return jnp.concatenate(tiles, axis=1)


def gathered_heads(values):
    rows = values.shape[0]
    low = lax.broadcasted_iota(jnp.int32, (rows, 128), 1) < 64
    lane = lax.broadcasted_iota(jnp.int32, (rows, 8), 1)
    out = jnp.zeros((rows, 8), F32)
    for i in range(COLS // 128):
        tile = values[:, 128 * i : 128 * i + 128]
        first = jnp.sum(jnp.where(low, tile, 0.0), axis=1, keepdims=True)
        both = jnp.sum(tile, axis=1, keepdims=True)
        out = jnp.where(lane == 2 * i, first, out)
        out = jnp.where(lane == 2 * i + 1, both - first, out)
    return out


def softplus(v):
    return jnp.maximum(v, 0.0) + jnp.log1p(jnp.exp(-jnp.abs(v)))


def conv_pre(ext, taps):
    total = taps[4:5]
    for j in range(4):
        total = total + ext[HALO - 3 + j : HALO - 3 + j + ROWS] * taps[j : j + 1]
    return total


def conv_transposed(ext, taps, rows=ROWS):
    total = ext[3 : 3 + rows] * taps[0:1]
    for j in range(1, 4):
        total = total + ext[3 - j : 3 - j + rows] * taps[j : j + 1]
    return total


def conv_grads(dpre, ext, sixth, seventh):
    rows = [
        jnp.sum(dpre * ext[HALO - 3 + j : HALO - 3 + j + ROWS], axis=0, keepdims=True)
        for j in range(4)
    ]
    rows.append(jnp.sum(dpre, axis=0, keepdims=True))
    rows += [sixth, seventh, jnp.zeros((1, dpre.shape[1]), F32)]
    return jnp.concatenate(rows, axis=0)


def triangle(upper):
    row = lax.broadcasted_iota(jnp.int32, (ROWS, ROWS), 0)
    col = lax.broadcasted_iota(jnp.int32, (ROWS, ROWS), 1)
    return row <= col if upper else row >= col


def sds(*shape, dtype=F32):
    return jax.ShapeDtypeStruct(shape, dtype)


def params():
    return pltpu.CompilerParams(vmem_limit_bytes=VMEM_LIMIT)


MESHID = pl.DeviceIdType.MESH
ORDERS = (("x", "y", "z"), ("y", "z", "x"), ("z", "x", "y"))
SUB = 32


def neighbour(axis, s):
    if axis == "core":
        return {"core": 1 - lax.axis_index("core")}
    if axis == "y":
        y = lax.rem(lax.axis_index("yhi") * 2 + lax.axis_index("ylo") + (s + 4), 4)
        return {"ylo": lax.rem(y, 2), "yhi": y // 2}
    return {axis: lax.rem(lax.axis_index(axis) + (s + 4), 4)}


def my_place():
    return {"x": lax.axis_index("x"), "z": lax.axis_index("z"), "y": lax.axis_index("yhi") * 2 + lax.axis_index("ylo")}


def block_device(p):
    return {"z": p // 2, "yhi": lax.rem(p, 2)}


def f32(ref):
    return ref[...].astype(F32)


class Sender:
    def __init__(self):
        self.pending = {}

    def __call__(self, src, dst, send, recv, device):
        c = pltpu.make_async_remote_copy(src_ref=src, dst_ref=dst, send_sem=send, recv_sem=recv, device_id=device,
                                         device_id_type=MESHID)
        c.start()
        self.pending[id(c)] = c
        return c

    def sent(self, c):
        c.wait_send()
        del self.pending[id(c)]

    def all_sent(self):
        for c in self.pending.values():
            c.wait_send()


def greet():
    bar = pltpu.get_barrier_semaphore()
    for a in "xyz":
        for s in (1, 2, 3):
            pl.semaphore_signal(bar, inc=1, device_id=neighbour(a, s), device_id_type=MESHID)
    for d in (1, 2, 3):
        diagonal = {"z": lax.rem(lax.axis_index("z") + d, 4), "yhi": 1 - lax.axis_index("yhi")}
        pl.semaphore_signal(bar, inc=1, device_id=diagonal, device_id_type=MESHID)
    pl.semaphore_signal(bar, inc=1, device_id=neighbour("core", 1), device_id_type=MESHID)
    return lambda: pl.semaphore_wait(bar, 13)


def to_peers(rc, src_of, dst, send, recv, block):
    out = []
    for d in range(1, 8):
        p = lax.rem(block + d, 8)
        out.append(rc(src_of(p), dst.at[block], send.at[d], recv.at[d], block_device(p)))
    return out


class Gather:
    def __init__(self, rc, g, w, sems, item, r):
        self.rc, self.g, self.w, self.item, self.r = rc, g, w, item, r
        self.ts, self.tr, self.cs, self.cr = sems
        self.k = item * 3 + r
        self.me = my_place()
        self.core = lax.axis_index("core")
        self.forwarded = []

    def at(self, pos, lo=0, n=SUB):
        z = slice(None) if pos["z"] is None else pos["z"]
        x = slice(None) if pos["x"] is None else pos["x"]
        if pos["y"] is None:
            yh = yl = slice(None)
        else:
            yh, yl = pos["y"] // 2, lax.rem(pos["y"], 2)
        return self.g.at[self.item, z, yh, yl, x, self.core, pl.ds(self.r * SUB + lo, n)]

    def pos(self, st, d=0):
        p = {a: (None if i < st else self.me[a]) for i, a in enumerate(ORDERS[self.r])}
        a = ORDERS[self.r][st]
        p[a] = lax.rem(self.me[a] + (d + 4), 4)
        return p

    def to_sibling(self, ref, src=None):
        k = self.k * 10 + len(self.forwarded)
        self.forwarded.append(self.rc(ref if src is None else src, ref, self.cs.at[k], self.cr.at[k], neighbour("core", 1)))

    def straight(self, st):
        ref, t = self.at(self.pos(st)), self.k * 10 + st * 3 - 1
        src = ref if st else self.w.at[self.item, pl.ds(self.r * SUB, SUB)]
        self.c = [self.rc(src, ref, self.ts.at[t + d], self.tr.at[t + d], neighbour(ORDERS[self.r][st], d)) for d in (1, 2, 3)]
        if st == 0:
            self.to_sibling(ref, src)

    def line(self, st):
        for d in (1, 2, 3):
            self.c[d - 1].wait_recv()
            self.to_sibling(self.at(self.pos(st, -d)))

    def near(self):
        a, t = ORDERS[self.r][2], self.k * 10 + 6
        ref = self.at(self.pos(2))
        self.c = [self.rc(ref, ref, self.ts.at[t + i], self.tr.at[t + i], neighbour(a, d)) for i, d in enumerate((1, -1))]

    def pass_on(self):
        a, t = ORDERS[self.r][2], self.k * 10 + 8
        self.f = []
        for i, d in enumerate((1, -1)):
            self.c[i].wait_recv()
            p = self.pos(2, -d)
            half = self.at(p, 16 * i, 16)
            self.f.append(self.rc(half, half, self.ts.at[t + i], self.tr.at[t + i], neighbour(a, d)))
            self.to_sibling(self.at(p))

    def last(self):
        for f in self.f:
            f.wait_recv()
        self.to_sibling(self.at(self.pos(2, 2)))

    def complete(self):
        for c in self.forwarded:
            c.wait_recv()


def forward_kernel(w_ref, bc_ref, dt_ref, pk_ref, hid, cot_ref, gain, taps_bc, g_ref, gb_ref,
                   pk_out, x_pre_out, x_conv_out, d_x_out, normed_t_out, cot_t_out, state_out, bc_pre_out, bc_conv_out,
                   steps_out, rates_out, cols_out, cum_row_out, step_row_out, dec_out, result_out,
                   out_in_out, d_z_out, gain_part_out, skip_part_out, d_cols_out, d_bc_out, d_state_out,
                   normed_t2_out, cot_t2_out, out_in2_out, d_z2_out, *scr):
    (pk, x_pre, x_conv, normed_t, cot_t, state, bc_pre, bc_conv, steps, rates, cols, cum_row, step_row, dec,
     result, out_in, d_z, gain_part, skip_part, d_cols, d_bc, d_state,
     cot, normed, halo, dts, dt_own, small_all, zb, yb, db, wbuf, gram, d_gram, local, rec_a, out_b, dec_own, square, inner,
     scales, acc, d_c,
     ts, tr, cs, cr, bs, br, ps, pr, qs, qr, es, er, fs, fr, gs, gr, ds, dr, hs, hr, lsem, wsem, osem, ysem, xs, xr) = scr
    rc = Sender()
    me = my_place()
    core = lax.axis_index("core")
    x, ylo = me["x"], lax.axis_index("ylo")
    block = lax.axis_index("z") * 2 + lax.axis_index("yhi")
    arrived = greet()
    writes = []

    def out(src, dst):
        c = pltpu.make_async_copy(src, dst, osem.at[len(writes)])
        c.start()
        writes.append(c)

    cot_c = pltpu.make_async_copy(cot_ref, cot, lsem.at[3])
    cot_c.start()
    own_w = pltpu.make_async_copy(w_ref, g_ref.at[:, me["z"], me["y"] // 2, ylo, x, core], lsem.at[0])
    own_w.start()
    arrived()

    gx, gz, go = [[Gather(rc, g_ref, w_ref, (ts, tr, cs, cr), i, r) for r in range(3)] for i in range(3)]

    def each(group, name, *args):
        for c in group:
            getattr(c, name)(*args)

    each(gx, "straight", 0)
    dt_c = to_peers(rc, lambda p: dt_ref, dts, ps, pr, block)

    def small(lo, n):
        cols = pl.ds(lo, n)
        sems = iter(range(9 * (lo // 256), 9 * (lo // 256) + 9))

        def push(src, dst, device):
            k = next(sems)
            return rc(src, dst, bs.at[k], br.at[k], device)

        def at(yl, x_at):
            return gb_ref.at[yl, x_at, core, :, cols]

        def over_y(src):
            own = pltpu.make_async_copy(src, at(ylo, x), lsem.at[1 + lo // 256])
            own.start()
            return [push(src, at(ylo, x), {"ylo": 1 - ylo}), push(src, at(ylo, x), neighbour("core", 1))], own

        def over_x(first, own):
            first[0].wait_recv()
            own.wait()
            line = gb_ref.at[:, x, core, :, cols]
            other = at(1 - ylo, x)
            rest = [push(line, line, neighbour("x", d)) for d in (1, 2, 3)]
            return rest, [first[1], push(other, other, neighbour("core", 1))]

        def to_sibling(rest, cores):
            for d in (1, 2, 3):
                rest[d - 1].wait_recv()
                line = gb_ref.at[:, lax.rem(x + 4 - d, 4), core, :, cols]
                cores.append(push(line, line, neighbour("core", 1)))
            return cores

        return over_y, over_x, to_sibling

    bc_y, bc_x, bc_end = small(0, 256)
    dt_y, dt_x, dt_end = small(256, 128)
    bc_s = bc_y(bc_ref)
    halo_c = rc(hid.at[pl.ds(ROWS - HALO, HALO)], halo, hs, hr, block_device(lax.rem(block + 1, 8)))
    each(gz, "straight", 0)
    each(go, "straight", 0)
    pk_c = to_peers(rc, lambda p: pk_ref, pk, qs, qr, block)
    dts[block] = dt_ref[...]
    pk[block] = pk_ref[...]

    def normalize(part, at):
        v = part[...].astype(F32)
        r = lax.rsqrt(jnp.mean(v * v, axis=1, keepdims=True) + EPS)
        normed[pl.ds(at, part.shape[0])] = (v * r * gain[...]).astype(BF16)

    normalize(hid, HALO)
    own_w.wait()
    bc_s = bc_x(*bc_s)
    each(gx, "line", 0)
    each(gx, "straight", 1)

    for c in dt_c:
        c.wait_recv()
    total = f32(dts.at[0])
    for i in range(1, 8):
        total = total + f32(dts.at[i])
    dt_own[...] = total.astype(BF16)
    dt_s = dt_y(dt_own)
    normed_t[...] = normed[HALO:, :].T.reshape(8, 2, 96, ROWS)
    out(normed_t, normed_t_out)
    dt_s = dt_x(*dt_s)
    each(gx, "line", 1)
    each(gx, "near")
    each(gz, "line", 0)
    each(gz, "straight", 1)
    cot_c.wait()
    cot_t[...] = cot[...].T.reshape(8, 2, 96, ROWS)
    out(cot_t, cot_t_out)
    halo_c.wait_recv()
    normalize(halo, 0)

    @pl.when(block == 0)
    def _():
        normed[pl.ds(0, HALO)] = jnp.zeros((HALO, WIDTH), BF16)

    each(go, "line", 0)
    for c in pk_c:
        c.wait_recv()
    out(pk, pk_out)
    b_core = bc_end(*bc_s) + dt_end(*dt_s)
    for c in b_core:
        c.wait_recv()
    small_in = pltpu.make_async_copy(gb_ref, small_all, lsem.at[1])
    small_in.start()
    each(gx, "pass_on")
    each(go, "straight", 1)
    small_in.wait()

    def row(lo):
        pieces = [pk[m, 6:7, lo : lo + HEADS] for m in range(GROUPS)]
        return jnp.concatenate(pieces + [jnp.zeros((1, 80), F32)], axis=1)

    rates[0:1] = row(0)
    rates[1:2] = row(HEADS)
    rates[2:8] = jnp.zeros((6, 128), F32)
    little = dot(normed[...], small_all[...].reshape(WIDTH, COLS))
    bc_pre[...] = little[:, :256]
    pre = conv_pre(little[:, :256], taps_bc[...])
    bc_conv[...] = (pre * jax.nn.sigmoid(pre)).astype(BF16)
    shifted = little[HALO:, 256:384] + rates[1:2]
    steps[...] = shifted
    step = softplus(shifted)
    decay = -step * jnp.exp(rates[0:1])
    cum = dot(triangle(False).astype(F32), decay, precision=lax.Precision.HIGHEST)
    cum_t = cum.T
    step_t = step.T
    lasts = jnp.broadcast_to(jnp.exp(cum_t[:, ROWS - 1 : ROWS]), (128, 128))
    for m in range(GROUPS):
        at = slice(HEADS * m, HEADS * m + 8)
        cols[m] = jnp.concatenate([cum[:, at], step[:, at]], axis=1)
        cum_row[m] = cum_t[HEADS * m : HEADS * m + 8]
        step_row[m] = step_t[HEADS * m : HEADS * m + 8]
        dec_own[m] = lasts[HEADS * m : HEADS * m + 8]
    dec_c = to_peers(rc, lambda p: dec_own.at[p], dec, ds, dr, block)
    dec[block] = dec_own[block]
    gram[...] = jnp.where(triangle(False), dot(bc_conv[:, 128:], bc_conv[:, :128], (1, 1)), 0.0)
    out(bc_pre, bc_pre_out)
    out(bc_conv, bc_conv_out)
    out(steps, steps_out)
    out(rates, rates_out)
    out(cols, cols_out)
    out(cum_row, cum_row_out)
    out(step_row, step_row_out)
    each(gz, "line", 1)
    each(gz, "near")
    each(gx, "last")
    each(gx, "complete")

    g_flat = g_ref.reshape(3, GROUPS, WIDTH, COLS)

    def weights(item, m, buf):
        return pltpu.make_async_copy(g_flat.at[item, m], wbuf.at[buf, m], wsem.at[buf, m])

    def load(item, buf):
        for m in range(GROUPS):
            weights(item, m, buf).start()

    def pairs(item, buf, lo, hi, body):
        @pl.loop(lo, hi)
        def _(i):
            for k in range(2):
                weights(item, 2 * i + k, buf).wait()
            body(i, jnp.concatenate([wbuf[buf, 2 * i], wbuf[buf, 2 * i + 1]], axis=1))

    load(0, 0)

    def to_owner(m):
        return pltpu.make_async_remote_copy(src_ref=local.at[m], dst_ref=rec_a.at[block], send_sem=es.at[m], recv_sem=er.at[block],
                                            device_id=block_device(m), device_id_type=MESHID)

    def second_pair(i, w):
        both = dot(normed[...], w)
        for k in range(2):
            m = 2 * i + k
            ext = both[:, COLS * k : COLS * k + COLS]
            x_pre[m] = ext
            pre = conv_pre(ext, pk[m])
            xc = (pre * jax.nn.sigmoid(pre)).astype(BF16)
            x_conv[m] = xc
            cum, step = cols[m][:, :8], cols[m][:, 8:]
            weighted = (xc.astype(F32) * spread(step * jnp.exp(cum[ROWS - 1 : ROWS] - cum))).astype(BF16)
            local[m] = dot(weighted, bc_conv[:, :128], (0, 0)).astype(BF16)
            pl.when(m != block)(lambda m=m: to_owner(m).start())

    pairs(0, 0, 0, 4, second_pair)
    rec_a[block] = local[block]
    out(x_pre, x_pre_out)
    out(x_conv, x_conv_out)

    top, low = slice(0, HALF), slice(HALF, ROWS)

    def decays(cum, rows, h):
        col, row = cum[:, h : h + 1], rows[h : h + 1, :]
        return (jnp.exp(jnp.minimum(col[top] - row[:, top], 0.0)), jnp.exp(jnp.minimum(col[low] - row, 0.0)))

    def scan_group(m):
        xc = x_conv[m]
        cum = cols[m][:, :8]
        rows = cum_row[m]
        step_rows = step_row[m]
        parts = []
        for h in range(HEADS):
            xh = xc[:, 64 * h : 64 * h + 64]
            step = step_rows[h : h + 1, :]
            upper, lower = decays(cum, rows, h)
            upper = (upper * gram[top, top] * step[:, top]).astype(BF16)
            lower = (lower * gram[low] * step).astype(BF16)
            parts.append(jnp.concatenate([dot(upper, xh[top]), dot(lower, xh)], axis=0))
        yb[m] = jnp.concatenate(parts, axis=1) + spread(pk[m, 6:7, 12:20]) * xc.astype(F32)

    each(go, "line", 1)
    each(gz, "pass_on")
    each(go, "near")
    pl.loop(0, GROUPS)(scan_group)
    for c in dec_c:
        c.wait_recv()
    out(dec, dec_out)

    def exchanged(src, sends, recvs):
        for d in range(1, 8):
            other = lax.rem(block + d, 8)
            pltpu.make_async_remote_copy(src_ref=src.at[other], dst_ref=rec_a.at[other], send_sem=sends.at[other],
                                         recv_sem=recvs.at[other], device_id=block_device(other), device_id_type=MESHID).wait()

    def carry(order):
        for h in range(HEADS):
            rows = pl.ds(64 * h, 64)
            run = jnp.zeros((64, 128), F32)
            for i in order:
                out_b[i, rows] = run.astype(BF16)
                run = run * dec[i, pl.ds(h, 1)] + rec_a[i, rows].astype(F32)

    exchanged(local, es, er)
    carry(range(BLOCKS))
    f_c = to_peers(rc, lambda p: out_b.at[p], state, fs, fr, block)
    state[block] = out_b[block]
    each(gz, "last")
    each(go, "pass_on")
    each(gz, "complete")
    load(1, 1)

    def gate_pair(i, w):
        z = dot(normed[HALO:, :], w)
        for k in range(2):
            zb[2 * i + k] = z[:, COLS * k : COLS * k + COLS]

    pairs(1, 1, 0, 4, gate_pair)
    each(go, "last")
    each(go, "complete")
    load(2, 0)

    def cot_pair(i, w):
        d = dot(cot[...], w)
        for k in range(2):
            db[2 * i + k] = d[:, COLS * k : COLS * k + COLS]

    pairs(2, 0, 0, 4, cot_pair)
    for c in f_c:
        c.wait_recv()
        rc.sent(c)
    out(state, state_out)
    square[...] = jnp.zeros_like(square)
    inner[...] = jnp.zeros_like(inner)
    c_mat = bc_conv[:, 128:]

    @pl.loop(0, GROUPS)
    def _(m):
        carried = dot(c_mat, state[m], (1, 1))
        y = yb[m] + spread(jnp.exp(cols[m][:, :8])) * carried
        yb[m] = y
        z = zb[m]
        gated = y * (z * jax.nn.sigmoid(z))
        sq = gated * gated
        ip = db[m] * pk[m, 5:6] * gated
        square[...] += sq[:, :128] + sq[:, 128:256] + sq[:, 256:]
        inner[...] += ip[:, :128] + ip[:, 128:256] + ip[:, 256:]

    r2 = lax.rsqrt(jnp.sum(square[...], axis=1, keepdims=True) / INNER + EPS)
    slope = r2 * r2 * r2 * (jnp.sum(inner[...], axis=1, keepdims=True) / INNER)
    scales[...] = jnp.concatenate([r2, slope, jnp.zeros((ROWS, 6), F32)], axis=1)
    acc[...] = jnp.zeros_like(acc)
    d_c[...] = jnp.zeros_like(d_c)
    d_gram[...] = jnp.zeros_like(d_gram)

    def to_owner_back(m):
        return pltpu.make_async_remote_copy(src_ref=local.at[m], dst_ref=rec_a.at[block], send_sem=gs.at[m], recv_sem=gr.at[block],
                                            device_id=block_device(m), device_id_type=MESHID)

    @pl.loop(0, 4)
    def _(i):
        r2, slope = scales[:, 0:1], scales[:, 1:2]
        for k in range(2):
            m = 2 * i + k
            z, y, d = zb[m], yb[m], db[m]
            gain_row = pk[m, 5:6]
            sig = jax.nn.sigmoid(z)
            act = z * sig
            gated = y * act
            unit = gated * r2
            out_in[m] = (unit * gain_row).astype(BF16)
            gain_part[m] = jnp.sum(d * unit, axis=0, keepdims=True)
            d_gated = r2 * (d * gain_row) - gated * slope
            dy = d_gated * act
            d_z[m] = (d_gated * y * sig * (1.0 + z * (1.0 - sig))).astype(BF16)
            yb[m] = dy
            skip_part[m] = jnp.sum(dy * x_conv[m].astype(F32), axis=0, keepdims=True)
            grown = spread(jnp.exp(cols[m][:, :8]))
            dye = (grown * dy).astype(BF16)
            d_c[...] += dot(dye, state[m])
            local[m] = dot(dye, c_mat, (0, 0)).astype(BF16)
            pl.when(m != block)(lambda m=m: to_owner_back(m).start())
            d_cols[m] = jnp.concatenate([gathered_heads(dy * (grown * dot(c_mat, state[m], (1, 1)))), jnp.zeros((ROWS, 8), F32)],
                                        axis=1)
        acc[...] += dot(jnp.concatenate([out_in[2 * i], out_in[2 * i + 1]], axis=1),
                        jnp.concatenate([wbuf[0, 2 * i], wbuf[0, 2 * i + 1]], axis=1), (1, 1))

    rec_a[block] = local[block]
    result[...] = (hid[...].astype(F32) + acc[...]).astype(BF16)
    across = [rc(src, dst, xs.at[i], xr.at[i], neighbour("core", 1)) for i, (src, dst) in enumerate((
        (cot_t.at[:, 1 - core], cot_t2_out), (out_in, out_in2_out), (normed_t.at[:, 1 - core], normed_t2_out),
        (d_z, d_z2_out)))]
    out(result, result_out)
    out(out_in, out_in_out)
    out(d_z, d_z_out)
    out(gain_part, gain_part_out)
    out(skip_part, skip_part_out)

    def d_x_copy(m):
        return pltpu.make_async_copy(zb.at[m], d_x_out.at[m], ysem.at[m])

    def inner_group(m):
        dy = yb[m]
        dyb = dy.astype(BF16)
        xc = x_conv[m]
        cum = cols[m][:, :8]
        rows = cum_row[m]
        step_rows = step_row[m]
        d_cum = d_cols[m][:, :8]
        lane = lax.broadcasted_iota(jnp.int32, (ROWS, 8), 1)
        parts = []
        sums = []
        for h in range(HEADS):
            xh = xc[:, 64 * h : 64 * h + 64]
            dyh = dyb[:, 64 * h : 64 * h + 64]
            step = step_rows[h : h + 1, :]
            upper, lower = decays(cum, rows, h)
            d_upper = dot(dyh[top], xh[top], (1, 1))
            d_lower = dot(dyh[low], xh, (1, 1))
            up, lo = upper * gram[top, top], lower * gram[low]
            ru, rl = up * d_upper, lo * d_lower
            col = jnp.sum(rl, axis=0, keepdims=True)
            sums.append(jnp.concatenate([col[:, top] + jnp.sum(ru, axis=0, keepdims=True), col[:, low]], axis=1))
            row = jnp.concatenate([jnp.sum(ru * step[:, top], axis=1, keepdims=True),
                                   jnp.sum(rl * step, axis=1, keepdims=True)], axis=0)
            d_cum = jnp.where(lane == h, d_cum + row, d_cum)
            d_gram[top, top] += upper * d_upper * step[:, top]
            d_gram[low] += lower * d_lower * step
            below = dot((lo * step).astype(BF16), dyh[low], (0, 0))
            parts.append(jnp.concatenate([below[top] + dot((up * step[:, top]).astype(BF16), dyh[top], (0, 0)), below[low]],
                                         axis=0))
        sums = jnp.concatenate(sums + [jnp.zeros((2, ROWS), F32)], axis=0).T
        zb[m] = jnp.concatenate(parts, axis=1) + spread(pk[m, 6:7, 12:20]) * dy
        d_x_copy(m).start()
        d_cols[m] = jnp.concatenate([d_cum - sums * cols[m][:, 8:], sums], axis=1)

    pl.loop(0, 4)(inner_group)
    exchanged(local, gs, gr)
    carry(range(BLOCKS - 1, -1, -1))
    b_c = to_peers(rc, lambda p: out_b.at[p], d_state, fs, fr, block)
    d_state[block] = out_b[block]
    pl.loop(4, GROUPS)(inner_group)
    out(d_cols, d_cols_out)
    dg = jnp.where(triangle(False), d_gram[...], 0.0).astype(BF16)
    d_bc[:, :128] = dot(dg, c_mat, (0, 0))
    d_bc[:, 128:] = d_c[...] + dot(dg, bc_conv[:, :128])
    out(d_bc, d_bc_out)
    for c in b_c + across:
        c.wait_recv()
    out(d_state, d_state_out)
    for c in writes:
        c.wait()
    for m in range(GROUPS):
        d_x_copy(m).wait()
    rc.all_sent()


HALF = ROWS // 2
RESULTS = (
    ("pk", (GROUPS, 8, COLS), F32), ("x_pre", (GROUPS, HALO + ROWS, COLS), F32), ("x_conv", (GROUPS, ROWS, COLS), BF16),
    ("d_x", (GROUPS, ROWS, COLS), F32), ("normed_t", (8, 2, 96, ROWS), BF16), ("cot_t", (8, 2, 96, ROWS), BF16),
    ("state", (GROUPS, COLS, 128), BF16), ("bc_pre", (HALO + ROWS, 256), F32), ("bc_conv", (ROWS, 256), BF16),
    ("steps", (ROWS, 128), F32), ("rates", (8, 128), F32), ("cols", (GROUPS, ROWS, 16), F32),
    ("cum_row", (GROUPS, 8, ROWS), F32), ("step_row", (GROUPS, 8, ROWS), F32), ("dec", (BLOCKS, 8, 128), F32),
    ("result", (ROWS, WIDTH), BF16), ("out_in", (GROUPS, ROWS, COLS), BF16), ("d_z", (GROUPS, ROWS, COLS), BF16),
    ("gain_part", (GROUPS, 1, COLS), F32), ("skip_part", (GROUPS, 1, COLS), F32), ("d_cols", (GROUPS, ROWS, 16), F32),
    ("d_bc", (ROWS, 256), F32), ("d_state", (GROUPS, COLS, 128), BF16),
)
SIBLING = (
    ("normed_t2", (8, 96, ROWS), BF16), ("cot_t2", (8, 96, ROWS), BF16), ("out_in2", (GROUPS, ROWS, COLS), BF16),
    ("d_z2", (GROUPS, ROWS, COLS), BF16),
)


def forward(w3, bc, dt, pk, hid, cot, gain, taps_bc):
    hbm = pl.BlockSpec(memory_space=pl.ANY)
    vmem = pl.BlockSpec(memory_space=pltpu.VMEM)
    sem = pltpu.SemaphoreType.DMA

    def v(*shape, dtype=F32):
        return pltpu.VMEM(shape, dtype)

    def b(*shape):
        return v(*shape, dtype=BF16)

    groups = (GROUPS, ROWS, COLS)
    outs = pl.pallas_call(
        forward_kernel,
        out_shape=(sds(3, 4, 2, 2, 4, 2, 96, COLS, dtype=BF16), sds(2, 4, 2, 96, COLS, dtype=BF16),
                   *[sds(*shape, dtype=dtype) for _, shape, dtype in RESULTS + SIBLING]),
        in_specs=[hbm, vmem, vmem, vmem, vmem, hbm, vmem, vmem],
        out_specs=(hbm,) * (2 + len(RESULTS) + len(SIBLING)),
        scratch_shapes=[
            *[pltpu.VMEM(shape, dtype) for name, shape, dtype in RESULTS if name != "d_x"],
            b(ROWS, WIDTH), b(HALO + ROWS, WIDTH), b(HALO, WIDTH), b(BLOCKS, 96, 128), b(96, 128), b(2, 4, 2, 96, COLS),
            v(*groups), v(*groups), v(*groups), b(2, GROUPS, WIDTH, COLS), v(ROWS, ROWS), v(ROWS, ROWS),
            b(GROUPS, COLS, 128), b(GROUPS, COLS, 128), b(GROUPS, COLS, 128), v(GROUPS, 8, 128),
            v(ROWS, 128), v(ROWS, 128), v(ROWS, 8), v(ROWS, WIDTH), v(ROWS, 128),
            sem((90,)), sem((90,)), sem((90,)), sem((90,)), sem((18,)), sem((18,)), sem((8,)), sem((8,)), sem((8,)),
            sem((8,)), sem((8,)), sem((8,)), sem((8,)), sem((8,)), sem((8,)), sem((8,)), sem((8,)), sem((8,)), sem, sem,
            sem((4,)), sem((2, GROUPS)), sem((len(RESULTS),)), sem((GROUPS,)), sem((4,)), sem((4,)),
        ],
        compiler_params=pltpu.CompilerParams(collective_id=0, has_side_effects=True, vmem_limit_bytes=62 * 2**20),
        name="forward_between_devices",
    )(w3, bc, dt, pk, hid, cot, gain, taps_bc)
    return outs[0], outs[1], dict(zip([name for name, _, _ in RESULTS + SIBLING], outs[2:]))


class Total:
    def __init__(self, rc, value, core, xs, yl, yh, zs, send, recv):
        self.rc, self.value, self.core, self.xs, self.yl, self.yh, self.zs = rc, value, core, xs, yl, yh, zs
        self.send, self.recv, self.at = send, recv, 0
        self.me = my_place()

    def push(self, dst, device):
        k = self.at
        self.at += 1
        return self.rc(self.value, dst, self.send.at[k], self.recv.at[k], device)

    def done(self):
        for c in self.flying:
            c.wait_recv()
        for c in self.flying:
            self.rc.sent(c)

    def step(self, j):
        v, me = self.value, self.me
        if j == 0:
            self.flying = [self.push(self.core, neighbour("core", 1))]
        elif j == 1:
            self.done()
            v[...] = v[...] + self.core[...]
            self.xs[me["x"]] = v[...]
            self.flying = [self.push(self.xs.at[me["x"]], neighbour("x", d)) for d in (1, 2, 3)]
        elif j == 2:
            self.done()
            v[...] = (self.xs[0] + self.xs[1]) + (self.xs[2] + self.xs[3])
            self.flying = [self.push(self.yl, {"ylo": 1 - lax.axis_index("ylo")})]
        elif j == 3:
            self.done()
            v[...] = v[...] + self.yl[...]
            self.flying = [self.push(self.yh, {"yhi": 1 - lax.axis_index("yhi")})]
        elif j == 4:
            self.done()
            v[...] = v[...] + self.yh[...]
            self.zs[me["z"]] = v[...]
            self.flying = [self.push(self.zs.at[me["z"]], neighbour("z", d)) for d in (1, 2, 3)]
        elif j == 5:
            self.done()
            v[...] = (self.zs[0] + self.zs[1]) + (self.zs[2] + self.zs[3])


class SmallSum:
    def __init__(self, rc, parts, xs, ys, zs, hs, send, recv):
        self.rc, self.parts, self.xs, self.ys, self.zs, self.hs = rc, parts, xs, ys, zs, hs
        self.send, self.recv = send, recv
        self.me = my_place()

    def step(self, j, out=None):
        rc, me, parts, s, r = self.rc, self.me, self.parts, self.send, self.recv
        ylo = lax.axis_index("ylo")
        if j == 0:
            self.c = [rc(parts.at[:, lax.rem(me["x"] + d, 4)], self.xs.at[d - 1], s.at[d], r.at[d], neighbour("x", d))
                      for d in (1, 2, 3)]
        elif j == 1:
            for c in self.c:
                c.wait_recv()
            for yl in range(2):
                m = parts.at[yl, me["x"]]
                m[...] = (f32(m) + f32(self.xs.at[0, yl]) + f32(self.xs.at[1, yl]) + f32(self.xs.at[2, yl])).astype(BF16)
            self.c = [rc(parts.at[1 - ylo, me["x"]], self.ys, s.at[4], r.at[4], {"ylo": 1 - ylo})]
        elif j == 2:
            self.c[0].wait_recv()
            m = parts.at[ylo, me["x"]]
            m[...] = (f32(m) + f32(self.ys)).astype(BF16)
            self.zs[me["z"]] = m[...]
            self.c = [rc(m, self.zs.at[me["z"]], s.at[4 + d], r.at[4 + d], neighbour("z", d)) for d in (1, 2, 3)]
        elif j == 3:
            for c in self.c:
                c.wait_recv()
            z, hs = self.zs, self.hs
            hs[0] = ((f32(z.at[0]) + f32(z.at[1])) + (f32(z.at[2]) + f32(z.at[3]))).astype(BF16)
            self.c = [rc(hs.at[0], hs.at[1], s.at[8], r.at[8], {"yhi": 1 - lax.axis_index("yhi")})]
        elif j == 4:
            self.c[0].wait_recv()
            out[...] = f32(self.hs.at[0]) + f32(self.hs.at[1])


def part_of(ref, item, pos, lo, n):
    z = slice(None) if pos["z"] is None else pos["z"]
    x = slice(None) if pos["x"] is None else pos["x"]
    if pos["y"] is None:
        yh = yl = slice(None)
    else:
        yh, yl = pos["y"] // 2, lax.rem(pos["y"], 2)
    return ref.at[item, z, yh, yl, x, pl.ds(lo, n)]


class Chunk:
    def __init__(self, rc, own, out, bufs, sems, item, slot, wide, r):
        self.rc, self.own, self.out, self.item, self.slot, self.r = rc, own, out, item, slot, r
        full, half, second, third = bufs
        self.full, self.half = full[r].at[wide], half[r].at[wide]
        self.direct = {1: second[r].at[slot], 2: third.at[slot * 3 + r]}
        self.send, self.recv = sems
        self.base = (slot * 3 + r) * 10
        self.me = my_place()

    def slab(self, st, d, lo=0, n=SUB):
        p = {a: (self.me[a] if i < st else None) for i, a in enumerate(ORDERS[self.r])}
        a = ORDERS[self.r][st]
        p[a] = lax.rem(self.me[a] + (d + 4), 4)
        return part_of(self.own, self.slot, p, self.r * SUB + lo, n)

    def loop(self, st, body):
        sizes = []
        for a, n in (("z", (4,)), ("y", (2, 2)), ("x", (4,))):
            if ORDERS[self.r].index(a) > st:
                sizes += n
        if not sizes:
            body(())
        elif len(sizes) == 1 or sizes == [2, 2]:
            for i in range(4):
                body((i,) if len(sizes) == 1 else (i // 2, i % 2))
        else:
            @pl.loop(0, 4)
            def _(i):
                for k in range(4):
                    if sizes == [4, 4]:
                        body((i, k))
                    elif sizes == [4, 2, 2]:
                        body((i, k // 2, k % 2))
                    else:
                        body((i // 2, lax.rem(i, 2), k))

    def push(self, k, src, dst, st, d):
        t = self.base + k
        return self.rc(src, dst, self.send.at[t], self.recv.at[t], neighbour(ORDERS[self.r][st], d))

    def far(self):
        self.far_c = [self.push(i, self.slab(0, 2, 16 * i, 16), self.half.at[i], 0, d) for i, d in enumerate((1, -1))]

    def near(self):
        self.near_c = []
        for i, d in enumerate((1, -1)):
            self.far_c[i].wait_recv()
            mine = self.slab(0, d, 16 * i, 16)

            def add(index, mine=mine, i=i):
                m = mine.at[index]
                m[...] = m[...] + self.half[(i, *index)]

            self.loop(0, add)
            self.near_c.append(self.push(2 + i, self.slab(0, d), self.full.at[i], 0, d))

    def straight(self, st):
        self.straight_c = [self.push(1 + 3 * st + d - 1, self.slab(st, d), self.direct[st].at[d - 1], st, d) for d in (1, 2, 3)]

    def step(self, j):
        if j == 0:
            self.far()
        elif j == 1:
            self.near()
        elif j == 2:
            for c in self.near_c:
                c.wait_recv()
            mine = self.slab(0, 0)

            def add(index):
                m = mine.at[index]
                m[...] = (f32(m) + f32(self.full.at[(0, *index)]) + f32(self.full.at[(1, *index)])).astype(BF16)

            self.loop(0, add)
            self.straight(1)
        else:
            for c in self.straight_c:
                c.wait_recv()
            st = j - 2
            mine = self.slab(st, 0)
            got = self.direct[st]

            def total(index):
                m = mine.at[index] if index else mine
                return (f32(m) + f32(got.at[(0, *index)])) + (f32(got.at[(1, *index)]) + f32(got.at[(2, *index)]))

            if st == 1:
                def add(index):
                    mine[index] = total(index).astype(BF16)

                self.loop(1, add)
                self.straight(2)
            else:
                self.out[self.item, pl.ds(self.r * SUB, SUB)] = total(())


def backward_kernel(g_ref, x_conv_ref, d_x_ref, x_pre_ref, cols_ref, d_cols_ref, cot_t_ref, cot_t2_ref, out_in_ref, out_in2_ref,
                    normed_t_ref, normed_t2_ref, d_z_ref, d_z2_ref, state_ref, d_state_ref, w_small_ref, hid_ref, cot_ref,
                    taps, d_bc_in, bc_pre, bc_conv, taps_bc, shifted, rates, gain, gain_part, skip_part,
                    out_ref, sout_ref, vout_ref, nout_ref, grad_hidden, *scr):
    (own, l_c, l_c2, l_n, l_n2, rhs_o, rhs_z, rhs_x, state, d_state, w_small, hid, cot, tails, halo_src, halo_dst, acc, wbuf,
     bxc, bdx, bxp, bcols, bdc, d_b, d_all, parts, small2, s_xs, s_ys, s_zs, s_hs,
     v_core, v_xs, v_yl, v_yh, v_zs, n_core, n_xs, n_yl, n_yh, n_zs) = scr[:41]
    bufs = [scr[41:44], scr[44:47], scr[47:50], scr[50]]
    (t_s, t_r, x_s, x_r, h_s, h_r, m_s, m_r, ss, sr, vs, vr, ns, nr, wsem, lsem, isem, freed) = scr[51:]
    rc = Sender()
    core = lax.axis_index("core")
    block = lax.axis_index("z") * 2 + lax.axis_index("yhi")
    arrived = greet()

    loads = {}

    def load_in(name, *pairs):
        loads[name] = []
        for src, dst in pairs:
            c = pltpu.make_async_copy(src, dst, isem.at[sum(len(v) for v in loads.values())])
            c.start()
            loads[name].append(c)

    def ready(name):
        for c in loads[name]:
            c.wait()

    load_in("o", (cot_t_ref.at[:, core], l_c), (cot_t2_ref, l_c2), (out_in_ref, rhs_o.at[0]), (out_in2_ref, rhs_o.at[1]))
    load_in("z", (normed_t_ref.at[:, core], l_n), (normed_t2_ref, l_n2), (d_z_ref, rhs_z.at[0]), (d_z2_ref, rhs_z.at[1]))
    load_in("s", (state_ref, state), (d_state_ref, d_state))

    def chunks(item, slot, wide):
        return [Chunk(rc, own, out_ref, bufs, (t_s, t_r), item, slot, wide, r) for r in range(3)]

    def steps(cs, j):
        for c in cs:
            c.step(j)

    def both_tokens(own_t, other_t):
        return jnp.concatenate([own_t[...].reshape(768, ROWS), other_t[...].reshape(768, ROWS)], axis=1)

    def gradient(left, left2, rhs, slot):
        def one(m):
            v = dot(both_tokens(left, left2), jnp.concatenate([rhs[0, m], rhs[1, m]], axis=0))
            own[slot, m // 2, lax.rem(m, 2)] = v.astype(BF16).reshape(2, 4, 96, COLS)

        pl.loop(0, GROUPS)(one)

    oc, zc, xc_ = chunks(2, 0, 0), chunks(1, 1, 1), chunks(0, 2, 0)
    ready("o")
    gradient(l_c, l_c2, rhs_o, 0)
    arrived()
    steps(oc, 0)
    ready("z")

    streams = ((x_conv_ref, bxc), (d_x_ref, bdx), (x_pre_ref, bxp), (cols_ref, bcols), (d_cols_ref, bdc))

    def load(m):
        k = lax.rem(m, 2)
        return [pltpu.make_async_copy(src.at[m], dst.at[k], lsem.at[k, i]) for i, (src, dst) in enumerate(streams)]

    for c in load(0):
        c.start()
    gradient(l_n, l_n2, rhs_z, 1)
    steps(zc, 0)
    ready("s")
    load_in("end", (w_small_ref, w_small), (hid_ref, hid), (cot_ref, cot))

    def fifth_group(m):
        k = lax.rem(m, 2)

        @pl.when(m < GROUPS - 1)
        def _():
            for c in load(m + 1):
                c.start()

        for c in load(m):
            c.wait()
        ds = d_state[m]
        xf = bxc[k].astype(F32)
        cum, step = bcols[k][:, :8], bcols[k][:, 8:]
        last = cum[ROWS - 1 : ROWS]
        tail = jnp.exp(last - cum)
        weights = step * tail
        wide = spread(weights)
        d_weighted = dot(bc_conv[:, :128], ds, (1, 1))
        d_b[...] += dot((xf * wide).astype(BF16), ds)
        dx = bdx[k] + wide * d_weighted
        d_weights = gathered_heads(d_weighted * xf)
        both = weights * d_weights
        lane = lax.broadcasted_iota(jnp.int32, (1, 8), 1)
        product = jnp.sum(state[m].astype(F32) * ds.astype(F32), axis=1, keepdims=True)
        d_last = jnp.sum(both, axis=0, keepdims=True)
        for h in range(HEADS):
            dots = jnp.sum(product[64 * h : 64 * h + 64], axis=0, keepdims=True)
            d_last = jnp.where(lane == h, d_last + jnp.exp(last) * dots, d_last)
        row = lax.broadcasted_iota(jnp.int32, (ROWS, 8), 0)
        d_cum = bdc[k][:, :8] - both
        d_cum = jnp.where(row == ROWS - 1, d_cum + d_last, d_cum)
        d_all[m] = jnp.concatenate([d_cum, bdc[k][:, 8:] + tail * d_weights], axis=1)
        ext = bxp[k]
        tap = taps[m]
        pre = conv_pre(ext, tap)
        sig = jax.nn.sigmoid(pre)
        dp = dx * (sig * (1.0 + pre * (1.0 - sig)))
        vout_ref[m] = conv_grads(dp, ext, gain_part[m], skip_part[m])
        whole_dx = conv_transposed(jnp.concatenate([dp, jnp.zeros((8, COLS), F32)], axis=0), tap)
        rhs_x[0, m] = whole_dx.astype(BF16)
        tails[m] = whole_dx[ROWS - 16 :]
        halo_src[m] = dp[:8]

    d_b[...] = jnp.zeros_like(d_b)
    pl.loop(0, 2)(fifth_group)
    steps(oc, 1)
    pl.loop(2, GROUPS)(fifth_group)

    d_bc = jnp.concatenate([d_bc_in[:, :128] + d_b[...], d_bc_in[:, 128:]], axis=1)
    ext = bc_pre[...]
    pre = conv_pre(ext, taps_bc[...])
    sig = jax.nn.sigmoid(pre)
    dp_bc = d_bc * (sig * (1.0 + pre * (1.0 - sig)))
    halo_src[GROUPS] = jnp.concatenate([dp_bc[:8], jnp.zeros((8, 128), F32)], axis=1)
    halo = rc(halo_src, halo_dst, h_s, h_r, block_device(lax.rem(block + 7, 8)))
    steps(zc, 1)
    steps(oc, 2)
    for a in "xyz":
        for s in (1, -1):
            pl.semaphore_signal(freed, inc=1, device_id=neighbour(a, s), device_id_type=MESHID)
    zero8 = jnp.zeros((1, 256), F32)
    d_cum = jnp.concatenate([d_all[m][:, :HEADS] for m in range(GROUPS)] + [jnp.zeros((ROWS, 80), F32)], axis=1)
    d_step = jnp.concatenate([d_all[m][:, 8 : 8 + HEADS] for m in range(GROUPS)] + [jnp.zeros((ROWS, 80), F32)], axis=1)
    d_decay = dot(triangle(True).astype(F32), d_cum, precision=lax.Precision.HIGHEST)
    rate = -jnp.exp(rates[0:1])
    v = shifted[...]
    d_dt = (d_step + rate * d_decay) * jax.nn.sigmoid(v)
    log_grad = jnp.sum(d_decay * (softplus(v) * rate), axis=0, keepdims=True)
    shift_grad = jnp.sum(d_dt, axis=0, keepdims=True)
    bc_rows = conv_grads(dp_bc, ext, jnp.concatenate([log_grad, shift_grad], axis=1), zero8)
    vout_ref[GROUPS] = jnp.concatenate([bc_rows, jnp.zeros((8, 128), F32)], axis=1)
    vec = Total(rc, vout_ref, v_core, v_xs, v_yl, v_yh, v_zs, vs, vr)
    vec.step(0)

    halo.wait_recv()
    inside = block < 7

    def below(k):
        return jnp.where(inside, halo_dst[k], 0.0)

    def across(m):
        return pltpu.make_async_remote_copy(src_ref=rhs_x.at[0, m], dst_ref=rhs_x.at[1, m], send_sem=x_s.at[m],
                                            recv_sem=x_r.at[m], device_id=neighbour("core", 1), device_id_type=MESHID)

    def fix(m):
        ext = jnp.concatenate([jnp.zeros((16, COLS), F32), below(m)], axis=0)
        rhs_x[0, m, pl.ds(ROWS - 16, 16)] = (tails[m] + conv_transposed(ext, taps[m], 16)).astype(BF16)
        across(m).start()

    pl.loop(0, GROUPS)(fix)
    d_bc = conv_transposed(jnp.concatenate([dp_bc, below(GROUPS)[:, :256]], axis=0), taps_bc[...])
    small2[0] = jnp.concatenate([d_bc, d_dt], axis=1).astype(BF16)
    small_c = rc(small2.at[0], small2.at[1], m_s, m_r, neighbour("core", 1))
    vec.step(1)

    def weights(m):
        k = lax.rem(m, 2)
        return [pltpu.make_async_copy(g_ref.at[i, m], wbuf.at[k, i], wsem.at[k, i]) for i in range(2)]

    for c in weights(0):
        c.start()
    for m in range(GROUPS):
        across(m).wait()
    gradient(l_n, l_n2, rhs_x, 2)
    pl.semaphore_wait(freed, 6)
    steps(xc_, 0)
    small_c.wait_recv()
    parts[...] = dot(both_tokens(l_n, l_n2), small2[...].reshape(2 * ROWS, COLS)).astype(BF16).reshape(2, 4, 96, COLS)
    ready("end")
    acc[...] = dot(small2[0], w_small[...], (1, 1))

    def input_group(m):
        k = lax.rem(m, 2)

        @pl.when(m < GROUPS - 1)
        def _():
            for c in weights(m + 1):
                c.start()

        for c in weights(m):
            c.wait()
        lhs = jnp.concatenate([rhs_x[0, m], rhs_z[0, m]], axis=1)
        rhs = jnp.concatenate([wbuf[k, 0], wbuf[k, 1]], axis=1)
        acc[...] += dot(lhs, rhs, (1, 1))

    pl.loop(0, 4)(input_group)
    vec.step(2)
    steps(xc_, 1)
    sums = SmallSum(rc, parts, s_xs, s_ys, s_zs, s_hs, ss, sr)
    sums.step(0)
    pl.loop(4, GROUPS)(input_group)
    v = hid[...].astype(F32)
    r = lax.rsqrt(jnp.mean(v * v, axis=1, keepdims=True) + EPS)
    unit = v * r
    dn = acc[...]
    gain_grad = jnp.sum(dn * unit, axis=0, keepdims=True)
    for i in range(4):
        nout_ref[0, pl.ds(i, 1)] = gain_grad[:, COLS * i : COLS * i + COLS]
    nout_ref[0, pl.ds(4, 4)] = jnp.zeros((4, COLS), F32)
    nvec = Total(rc, nout_ref, n_core, n_xs, n_yl, n_yh, n_zs, ns, nr)
    nvec.step(0)
    vec.step(3)
    d_in = dn * gain[...]
    grad_hidden[...] = r * (d_in - unit * jnp.mean(d_in * unit, axis=1, keepdims=True)) + cot[...].astype(F32)
    nvec.step(1)
    steps(zc, 2)
    steps(oc, 3)
    vec.step(4)
    nvec.step(2)
    steps(xc_, 2)
    sums.step(1)
    nvec.step(3)
    vec.step(5)
    sums.step(2)
    nvec.step(4)
    steps(oc, 4)
    steps(zc, 3)
    steps(xc_, 3)
    sums.step(3)
    nvec.step(5)
    steps(zc, 4)
    sums.step(4, sout_ref)
    steps(xc_, 4)
    rc.all_sent()


def backward(w_all, r, w_small, hid, cot, taps_bc, gain):
    hbm = pl.BlockSpec(memory_space=pl.ANY)
    vmem = pl.BlockSpec(memory_space=pltpu.VMEM)
    sem = pltpu.SemaphoreType.DMA

    def buf(*shape, dtype=BF16):
        return pltpu.VMEM((*shape, COLS), dtype)

    def v(*shape, dtype=F32):
        return pltpu.VMEM(shape, dtype)

    def b(*shape):
        return v(*shape, dtype=BF16)

    scratch = [
        buf(3, 4, 2, 2, 4, 96), b(8, 96, ROWS), b(8, 96, ROWS), b(8, 96, ROWS), b(8, 96, ROWS),
        buf(2, GROUPS, ROWS), buf(2, GROUPS, ROWS), buf(2, GROUPS, ROWS), b(GROUPS, COLS, 128), b(GROUPS, COLS, 128),
        buf(WIDTH), b(ROWS, WIDTH), b(ROWS, WIDTH),
        buf(GROUPS, 16, dtype=F32), buf(GROUPS + 1, 8, dtype=F32), buf(GROUPS + 1, 8, dtype=F32),
        v(ROWS, WIDTH), buf(2, 2, WIDTH),
        buf(2, ROWS), buf(2, ROWS, dtype=F32), buf(2, HALO + ROWS, dtype=F32), v(2, ROWS, 16), v(2, ROWS, 16),
        v(ROWS, 128), v(GROUPS, ROWS, 16), buf(2, 4, 96), buf(2, ROWS), buf(3, 2, 96), buf(96), buf(4, 96), buf(2, 96),
    ]
    for n in (GROUPS + 1, 1):
        one = buf(n, 8, dtype=F32)
        four = buf(4, n, 8, dtype=F32)
        scratch += [one, four, one, one, four]
    scratch += [buf(2, 2, 4, 2, 2, SUB), buf(2, 2, 4, 4, SUB), buf(2, 2, 2, 2, 4, SUB)]
    scratch += [buf(2, 2, 4, 2, 2, 16), buf(2, 2, 4, 4, 16), buf(2, 2, 2, 2, 4, 16)]
    scratch += [buf(3, 3, 4, SUB), buf(3, 3, 4, SUB), buf(3, 3, 2, 2, SUB), buf(9, 3, SUB)]
    scratch += [sem((90,)), sem((90,)), sem((8,)), sem((8,)), sem, sem, sem, sem, sem((9,)), sem((9,)), sem((9,)), sem((9,)),
                sem((9,)), sem((9,)), sem((2, 2)), sem((2, 5)), sem((13,)), pltpu.SemaphoreType.REGULAR]
    names = ("x_conv", "d_x", "x_pre", "cols", "d_cols", "cot_t", "cot_t2", "out_in", "out_in2", "normed_t", "normed_t2", "d_z",
             "d_z2", "state", "d_state")
    return pl.pallas_call(
        backward_kernel,
        out_shape=(sds(3, 96, COLS), sds(96, COLS), sds(GROUPS + 1, 8, COLS), sds(1, 8, COLS), sds(ROWS, WIDTH)),
        in_specs=[hbm] * 19 + [vmem] * 10,
        out_specs=(vmem,) * 5,
        scratch_shapes=scratch,
        compiler_params=pltpu.CompilerParams(collective_id=1, has_side_effects=True, vmem_limit_bytes=63 * 2**20),
        name="backward_between_devices",
    )(w_all, *[r[name] for name in names], w_small, hid, cot, r["pk"], r["d_bc"], r["bc_pre"], r["bc_conv"], taps_bc,
      r["steps"], r["rates"], gain, r["gain_part"], r["skip_part"])
def shards(hidden, grad_out, norm_gain, w_zx, w_bc, w_dt, conv_x, conv_bc, a_log, dt_bias, d_skip, gate_gain, w_out):
    index = lax.axis_index(MP)
    heads = jnp.concatenate([a_log, dt_bias, d_skip, jnp.zeros((COLS - 3 * HEADS,), F32)])[None]
    packed = jnp.concatenate([conv_x, gate_gain[None], heads, jnp.zeros((1, COLS), F32)])
    steps_own = lax.dynamic_update_slice(jnp.zeros((96, 128), BF16), w_dt, (0, index * HEADS))
    taps_bc = jnp.pad(conv_bc, ((0, 3), (0, 0)))
    gain = norm_gain[None]
    w_all, w_small, r = forward(
        jnp.stack([w_zx[:, 1], w_zx[:, 0], w_out.T]), w_bc, steps_own, packed, hidden, grad_out, gain, taps_bc)
    w_all = w_all.reshape(3, GROUPS, WIDTH, COLS)
    w_small = w_small.reshape(WIDTH, COLS)
    owned, small, vector, norm_sum, grad_hidden = backward(w_all, r, w_small, hidden, grad_out, taps_bc, gain)

    def own(flat):
        return lax.dynamic_slice_in_dim(flat, index * HEADS, HEADS, flat.ndim - 1)

    mine = lax.dynamic_index_in_dim(vector, index, 0, keepdims=False)
    return (
        r["result"],
        grad_hidden,
        norm_sum[0, :4].reshape(WIDTH),
        jnp.stack([owned[1], owned[0]], axis=1),
        small[:, :256],
        own(small[:, 256:304]),
        mine[:5],
        vector[GROUPS, :5, :256],
        own(vector[GROUPS, 5, :48]),
        own(vector[GROUPS, 5, 128:176]),
        mine[6].reshape(HEADS, 64).sum(axis=1),
        mine[5],
        owned[2].T,
    )


def solution(mesh):
    finer = Mesh(mesh.devices.reshape(2, 4, 2, 4, 2), DP_MP)
    rows = P(DP_MP, None)
    placed = (rows, rows, P(), P(DP, None, MP), P(DP, None), P(DP, MP), P(None, MP), P(), P(MP), P(MP), P(MP), P(MP),
              P(MP, DP))
    return jax.shard_map(
        shards,
        mesh=finer,
        in_specs=placed,
        out_specs=(rows, rows, P(), P(DP, None, MP), P(DP, None), P(DP, MP), P(None, MP), P(), P(MP), P(MP), P(MP), P(MP),
                   P(MP, DP)),
        check_vma=False,
    )
```

time: 314 us -> 255 us (0.81)
  Pallas kernels: 287 us -> 233 us
    pallas_call x1, Pallas kernels: 126 us -> 91.3 us  [backward(): pl.pallas_call(backward_kernel, out_shape=(sds(3, 96, COLS), sds(96, COLS...]
    pallas_call x1 -> x0, Pallas kernels: 30.4 us -> none  [fourth(): pl.pallas_call(fourth_kernel, grid=(GROUPS,), in_specs=[whole(ROWS, WIDTH...]
    pallas_call x1, Pallas kernels: 131 us -> 142 us  [forward(): pl.pallas_call(forward_kernel, out_shape=(sds(3, 4, 2, 2, 4, 2, 96, COLS,...]
where the time goes in v3:
time: 255 us; the launch traced here: 254 us
  Pallas kernels  233 us (91%)
  local copies, waits for them, and re-layouts  17 us (7%)
  other arithmetic  3 us (1%)
    pallas_call x1, Pallas kernels, forward(): pl.pallas_call(forward_kernel, out_shape=(sds(3, 4, 2, 2, 4, 2, 96, COLS,...  142 us
    pallas_call x1, Pallas kernels, backward(): pl.pallas_call(backward_kernel, out_shape=(sds(3, 96, COLS), sds(96, COLS...  91.3 us

profile of v3, /device:TPU:0, one launch (start us, length us, event | category | flops | bytes accessed | tf_op | source)
XLA Modules:
  0.0 253.7 jit_solution(9451030688844117615)
XLA Ops:
  0.6 0.0 copy-start.8
  0.7 0.0 copy-start.9
  0.7 0.0 copy-start.10
  0.7 0.0 copy-start.7
  0.7 0.0 copy-start.4
  0.7 0.0 copy-start.5
  0.7 0.0 copy-start.6
  0.7 1.3 fusion.2
  2.0 1.6 pad_maximum_fusion.1.w_ref
  3.6 0.8 copy.28
  4.4 0.2 dynamic_update_slice.3.dt_ref
  4.6 0.0 copy-start.3
  4.7 0.0 copy-done.8
  4.7 0.0 copy-done.9
  4.7 0.0 copy-done.10
  4.7 0.1 pad_maximum_fusion.2
  4.8 0.0 copy-done.7
  4.8 0.1 pad.10.clone
  4.9 0.0 copy-done.4
  4.9 0.7 maximum_maximum_fusion.pk_ref
  5.5 0.0 copy-done.5
  5.5 0.6 broadcast_in_dim.23.gain
  6.1 0.0 copy-done.6
  6.1 0.6 pad.4.taps_bc
  6.7 0.0 copy-done.3
  6.7 141.6 %forward_between_devices.1 = (bf16[3,4,2,2,4,2,96,384]{7,6,5,4,3,2,1,0:T(8,128)(2,1)}, bf16[2,4,2,96,384]{4,3,2,1,0:T(8,128)(2,1)}, f32[8,8,384]{2,1,0:T(8,128)}...) custom-call(bf16[3,96,384]{2,1,0:T(8,128)(2,1)} %pad_maximum_fusion., ...), custom_call_target="tpu_custom_call" | custom-call | tf_op jit(solution)/shard_map/forward_between_devices/pallas_call | solution.py:666
  148.4 91.3 %backward_between_devices.1 = (f32[3,96,384]{2,1,0:T(8,128)}, f32[96,384]{1,0:T(8,128)}, f32[9,8,384]{2,1,0:T(8,128)}, f32[1,8,384]{2,1,0:T(8,128)}, f32[256,1536]{1,0:T(8,128)}) custom-call(bf16[3,8,1536,384]{3,2,1,0:T(8,128)(2,1)} %bitcast.26, bf16[8,256,384]{2,1,0:T(8,128)(2,1)} %get-tuple-element.46.x_conv_ref, ...), custom_call_target="tpu_custom_call" | custom-call | tf_op jit(solution)/shard_map/backward_between_devices/pallas_call | solution.py:1143
  239.6 0.0 copy-start.2
  239.6 0.0 copy-start.1
  239.7 0.8 slice.49
  240.4 0.6 reshape_squeeze.6
  241.1 1.7 slice_bitcast_fusion
  242.8 0.9 copy.29
  243.8 0.0 copy-done.2
  243.8 0.6 slice.52
  244.4 0.1 constant_dynamic-slice_fusion.2
  244.5 0.7 copy.30
  245.2 1.3 dynamic-slice_bitcast_fusion
  246.5 1.3 slice_bitcast_fusion.3
  247.8 0.7 fusion.3
  248.5 0.6 fusion
  249.0 0.6 fusion.1
  249.6 1.4 dynamic-slice_reduce_fusion
  251.0 0.1 reshape_squeeze.7
  251.1 0.6 reduce_sum.9
  251.7 0.9 copy.38
  252.6 0.0 copy-done
  252.6 1.1 copy.39
  (9 shorter events, 0.1 us)
Async XLA Ops:
  0.6 4.0 %copy-start.8 = (f32[6]{0:T(128)S(1)}, f32[6]{0:T(128)}, u32[]{:S(2)}) copy-start(f32[6]{0:T(128)} %param.23) | copy-start | bytes 76
  0.7 4.0 %copy-start.9 = (f32[6]{0:T(128)S(1)}, f32[6]{0:T(128)}, u32[]{:S(2)}) copy-start(f32[6]{0:T(128)} %param.22) | copy-start | bytes 76
  0.7 4.0 %copy-start.10 = (f32[6]{0:T(128)S(1)}, f32[6]{0:T(128)}, u32[]{:S(2)}) copy-start(f32[6]{0:T(128)} %param.21) | copy-start | bytes 76
  0.7 4.1 %copy-start.7 = (f32[384]{0:T(512)S(1)}, f32[384]{0:T(512)}, u32[]{:S(2)}) copy-start(f32[384]{0:T(512)} %param.24) | copy-start | bytes 4612
  0.7 4.2 %copy-start.4 = (f32[5,384]{1,0:T(8,128)S(1)}, f32[5,384]{1,0:T(8,128)}, u32[]{:S(2)}) copy-start(f32[5,384]{1,0:T(8,128)} %param.19) | copy-start | bytes 23044
  0.7 4.8 %copy-start.5 = (f32[1536]{0:T(1024)S(1)}, f32[1536]{0:T(1024)}, u32[]{:S(2)}) copy-start(f32[1536]{0:T(1024)} %param.15) | copy-start | bytes 18436
  0.7 5.4 %copy-start.6 = (f32[5,256]{1,0:T(8,128)S(1)}, f32[5,256]{1,0:T(8,128)}, u32[]{:S(2)}) copy-start(f32[5,256]{1,0:T(8,128)} %param.20) | copy-start | bytes 15364
  4.6 2.1 copy-start.3
  239.6 4.1 %copy-start.2 = (f32[96,384]{1,0:T(8,128)S(1)}, f32[96,384]{1,0:T(8,128)}, u32[]{:S(2)}) copy-start(f32[96,384]{1,0:T(8,128)} %get-tuple-element.73) | copy-start | bytes 442372
  239.6 12.1 %copy-start.1 = (bf16[256,1536]{1,0:T(8,128)(2,1)S(1)}, bf16[256,1536]{1,0:T(8,128)(2,1)}, u32[]{:S(2)}) copy-start(bf16[256,1536]{1,0:T(8,128)(2,1)} %get-tuple-element.112) | copy-start | bytes 2359300
  242.8 9.8 %copy-start = (f32[256,1536]{1,0:T(8,128)S(1)}, f32[256,1536]{1,0:T(8,128)}, u32[]{:S(2)}) copy-start(f32[256,1536]{1,0:T(8,128)} %get-tuple-element.113) | copy-start | bytes 4718596

commit v4 on v3

--- a/solution.py
+++ b/solution.py
@@ -162,23 +162,28 @@
     return out
 
 
+PIECES = (((0, 32), (32, 32), (64, 32)),) * 3
+
+
 class Gather:
     def __init__(self, rc, g, w, sems, item, r):
         self.rc, self.g, self.w, self.item, self.r = rc, g, w, item, r
+        self.flying = {}
         self.ts, self.tr, self.cs, self.cr = sems
         self.k = item * 3 + r
+        self.lo, self.n = PIECES[item][r]
         self.me = my_place()
         self.core = lax.axis_index("core")
         self.forwarded = []
 
-    def at(self, pos, lo=0, n=SUB):
+    def at(self, pos, lo=0, n=None):
         z = slice(None) if pos["z"] is None else pos["z"]
         x = slice(None) if pos["x"] is None else pos["x"]
         if pos["y"] is None:
             yh = yl = slice(None)
         else:
             yh, yl = pos["y"] // 2, lax.rem(pos["y"], 2)
-        return self.g.at[self.item, z, yh, yl, x, self.core, pl.ds(self.r * SUB + lo, n)]
+        return self.g.at[z, yh, yl, x, self.core, pl.ds(self.lo + lo, self.n if n is None else n)]
 
     def pos(self, st, d=0):
         p = {a: (None if i < st else self.me[a]) for i, a in enumerate(ORDERS[self.r])}
@@ -186,35 +191,43 @@
         p[a] = lax.rem(self.me[a] + (d + 4), 4)
         return p
 
-    def to_sibling(self, ref, src=None):
-        k = self.k * 10 + len(self.forwarded)
-        self.forwarded.append(self.rc(ref if src is None else src, ref, self.cs.at[k], self.cr.at[k], neighbour("core", 1)))
+    def to_sibling(self, ref):
+        k = self.k * 4 + len(self.forwarded)
+        self.forwarded.append(self.rc(ref, ref, self.cs.at[k], self.cr.at[k], neighbour("core", 1)))
+
+    def push(self, k, src, dst, a, d):
+        s = k % 3 if k < 6 else k % 2
+        if s in self.flying:
+            self.rc.sent(self.flying[s])
+        c = self.rc(src, dst, self.ts.at[3 * self.k + s], self.tr.at[10 * self.k + k], neighbour(a, d))
+        self.flying[s] = c
+        return c
 
     def straight(self, st):
-        ref, t = self.at(self.pos(st)), self.k * 10 + st * 3 - 1
-        src = ref if st else self.w.at[self.item, pl.ds(self.r * SUB, SUB)]
-        self.c = [self.rc(src, ref, self.ts.at[t + d], self.tr.at[t + d], neighbour(ORDERS[self.r][st], d)) for d in (1, 2, 3)]
-        if st == 0:
-            self.to_sibling(ref, src)
+        ref = self.at(self.pos(st))
+        src = ref if st else self.w.at[pl.ds(self.lo, self.n)]
+        self.c = [self.push(3 * st + d - 1, src, ref, ORDERS[self.r][st], d) for d in (1, 2, 3)]
 
     def line(self, st):
-        for d in (1, 2, 3):
-            self.c[d - 1].wait_recv()
-            self.to_sibling(self.at(self.pos(st, -d)))
+        for c in self.c:
+            c.wait_recv()
+        if st == 1:
+            self.to_sibling(self.at(self.pos(2)))
 
     def near(self):
-        a, t = ORDERS[self.r][2], self.k * 10 + 6
         ref = self.at(self.pos(2))
-        self.c = [self.rc(ref, ref, self.ts.at[t + i], self.tr.at[t + i], neighbour(a, d)) for i, d in enumerate((1, -1))]
+        self.c = [self.push(6 + i, ref, ref, ORDERS[self.r][2], d) for i, d in enumerate((1, -1))]
 
     def pass_on(self):
-        a, t = ORDERS[self.r][2], self.k * 10 + 8
         self.f = []
         for i, d in enumerate((1, -1)):
             self.c[i].wait_recv()
             p = self.pos(2, -d)
-            half = self.at(p, 16 * i, 16)
-            self.f.append(self.rc(half, half, self.ts.at[t + i], self.tr.at[t + i], neighbour(a, d)))
+            first = 16 * ((self.n + 16) // 32)
+            lo, n = ((0, first), (first, self.n - first))[i]
+            if n:
+                half = self.at(p, lo, n)
+                self.f.append(self.push(8 + i, half, half, ORDERS[self.r][2], d))
             self.to_sibling(self.at(p))
 
     def last(self):
@@ -226,44 +239,63 @@
         for c in self.forwarded:
             c.wait_recv()
 
-
-def forward_kernel(w_ref, bc_ref, dt_ref, pk_ref, hid, cot_ref, gain, taps_bc, g_ref, gb_ref,
+    def drained(self):
+        for c in [*self.flying.values(), *self.forwarded]:
+            self.rc.sent(c)
+
+
+def forward_kernel(zx_ref, wo_ref, bc_ref, hid, cot_ref, norm_gain, dt_ref, conv_x, taps_bc, log_ref, shift_ref, skip_ref,
+                   gate_ref, g_ref, gb_ref,
                    pk_out, x_pre_out, x_conv_out, d_x_out, normed_t_out, cot_t_out, state_out, bc_pre_out, bc_conv_out,
                    steps_out, rates_out, cols_out, cum_row_out, step_row_out, dec_out, result_out,
                    out_in_out, d_z_out, gain_part_out, skip_part_out, d_cols_out, d_bc_out, d_state_out,
                    normed_t2_out, cot_t2_out, out_in2_out, d_z2_out, *scr):
     (pk, x_pre, x_conv, normed_t, cot_t, state, bc_pre, bc_conv, steps, rates, cols, cum_row, step_row, dec,
      result, out_in, d_z, gain_part, skip_part, d_cols, d_bc, d_state,
-     cot, normed, halo, dts, dt_own, small_all, zb, yb, db, wbuf, gram, d_gram, local, rec_a, out_b, dec_own, square, inner,
-     scales, acc, d_c,
-     ts, tr, cs, cr, bs, br, ps, pr, qs, qr, es, er, fs, fr, gs, gr, ds, dr, hs, hr, lsem, wsem, osem, ysem, xs, xr) = scr
+     cot, normed, halo, dt_own, small_all, zb, yb, uppers, lowers, wx, wo, gram, d_gram, local, rec_a, out_b, dec_own, square,
+     scales, acc, d_c, pk_ref, gain,
+     ts, tr, cs, cr, bs, br, qs, qr, es, er, fs, fr, ds, dr, hs, hr, lsem, wsem, osem, xs, xr) = scr
     rc = Sender()
     me = my_place()
     core = lax.axis_index("core")
     x, ylo = me["x"], lax.axis_index("ylo")
     block = lax.axis_index("z") * 2 + lax.axis_index("yhi")
     arrived = greet()
-    writes = []
+    writes, count = [], [0]
 
     def out(src, dst):
-        c = pltpu.make_async_copy(src, dst, osem.at[len(writes)])
+        c = pltpu.make_async_copy(src, dst, osem.at[count[0]])
         c.start()
+        count[0] += 1
         writes.append(c)
 
     cot_c = pltpu.make_async_copy(cot_ref, cot, lsem.at[3])
     cot_c.start()
-    own_w = pltpu.make_async_copy(w_ref, g_ref.at[:, me["z"], me["y"] // 2, ylo, x, core], lsem.at[0])
-    own_w.start()
+    def spot(ref):
+        return ref.at[me["z"], me["y"] // 2, ylo, x, core]
+
+    own_w = [pltpu.make_async_copy(src, spot(dst), lsem.at[4 + i])
+             for i, (src, dst) in enumerate(((zx_ref.at[1], wx), (zx_ref.at[0], g_ref.at[1]), (wo_ref, wo)))]
+    for c in own_w:
+        c.start()
+    pk_ref[...] = jnp.zeros_like(pk_ref)
+    pk_ref[0:5] = conv_x[...]
+    pk_ref[5] = gate_ref[...]
+    for at, ref in ((6, log_ref), (7, shift_ref), (14, skip_ref)):
+        pk_ref[at, 0:HEADS] = ref[...]
+    pk_ref[8 : 8 + HEADS, 0:96] = dt_ref[...].astype(F32)
+    gain[0] = norm_gain[...]
     arrived()
 
-    gx, gz, go = [[Gather(rc, g_ref, w_ref, (ts, tr, cs, cr), i, r) for r in range(3)] for i in range(3)]
+    gx, gz, go = [[Gather(rc, g, w, (ts, tr, cs, cr), i, r) for r in range(3)]
+                  for i, (g, w) in enumerate(((wx, zx_ref.at[1]), (g_ref.at[1], zx_ref.at[0]), (wo, wo_ref)))]
 
     def each(group, name, *args):
         for c in group:
             getattr(c, name)(*args)
 
     each(gx, "straight", 0)
-    dt_c = to_peers(rc, lambda p: dt_ref, dts, ps, pr, block)
+    pk_c = to_peers(rc, lambda p: pk_ref, pk, qs, qr, block)
 
     def small(lo, n):
         cols = pl.ds(lo, n)
@@ -301,11 +333,6 @@
     bc_y, bc_x, bc_end = small(0, 256)
     dt_y, dt_x, dt_end = small(256, 128)
     bc_s = bc_y(bc_ref)
-    halo_c = rc(hid.at[pl.ds(ROWS - HALO, HALO)], halo, hs, hr, block_device(lax.rem(block + 1, 8)))
-    each(gz, "straight", 0)
-    each(go, "straight", 0)
-    pk_c = to_peers(rc, lambda p: pk_ref, pk, qs, qr, block)
-    dts[block] = dt_ref[...]
     pk[block] = pk_ref[...]
 
     def normalize(part, at):
@@ -314,25 +341,26 @@
         normed[pl.ds(at, part.shape[0])] = (v * r * gain[...]).astype(BF16)
 
     normalize(hid, HALO)
-    own_w.wait()
-    bc_s = bc_x(*bc_s)
     each(gx, "line", 0)
+    for c in own_w:
+        c.wait()
     each(gx, "straight", 1)
-
-    for c in dt_c:
+    halo_c = rc(hid.at[pl.ds(ROWS - HALO, HALO)], halo, hs, hr, block_device(lax.rem(block + 1, 8)))
+
+    for c in pk_c:
         c.wait_recv()
-    total = f32(dts.at[0])
-    for i in range(1, 8):
-        total = total + f32(dts.at[i])
-    dt_own[...] = total.astype(BF16)
+    out(pk, pk_out)
+    columns = jnp.concatenate([pk[m, 8 : 8 + HEADS, 0:128] for m in range(GROUPS)] + [jnp.zeros((80, 128), F32)], axis=0)
+    dt_own[...] = columns.T[:96].astype(BF16)
     dt_s = dt_y(dt_own)
     normed_t[...] = normed[HALO:, :].T.reshape(8, 2, 96, ROWS)
     out(normed_t, normed_t_out)
-    dt_s = dt_x(*dt_s)
     each(gx, "line", 1)
     each(gx, "near")
-    each(gz, "line", 0)
-    each(gz, "straight", 1)
+    bc_s = bc_x(*bc_s)
+    dt_s = dt_x(*dt_s)
+    each(gz, "straight", 0)
+    each(go, "straight", 0)
     cot_c.wait()
     cot_t[...] = cot[...].T.reshape(8, 2, 96, ROWS)
     out(cot_t, cot_t_out)
@@ -343,25 +371,24 @@
     def _():
         normed[pl.ds(0, HALO)] = jnp.zeros((HALO, WIDTH), BF16)
 
-    each(go, "line", 0)
-    for c in pk_c:
-        c.wait_recv()
-    out(pk, pk_out)
+    each(gx, "pass_on")
+    each(gz, "line", 0)
+    each(gz, "straight", 1)
     b_core = bc_end(*bc_s) + dt_end(*dt_s)
     for c in b_core:
         c.wait_recv()
     small_in = pltpu.make_async_copy(gb_ref, small_all, lsem.at[1])
     small_in.start()
-    each(gx, "pass_on")
+    each(go, "line", 0)
     each(go, "straight", 1)
     small_in.wait()
 
-    def row(lo):
-        pieces = [pk[m, 6:7, lo : lo + HEADS] for m in range(GROUPS)]
+    def row(at):
+        pieces = [pk[m, at : at + 1, 0:HEADS] for m in range(GROUPS)]
         return jnp.concatenate(pieces + [jnp.zeros((1, 80), F32)], axis=1)
 
-    rates[0:1] = row(0)
-    rates[1:2] = row(HEADS)
+    rates[0:1] = row(6)
+    rates[1:2] = row(7)
     rates[2:8] = jnp.zeros((6, 128), F32)
     little = dot(normed[...], small_all[...].reshape(WIDTH, COLS))
     bc_pre[...] = little[:, :256]
@@ -391,28 +418,27 @@
     out(cols, cols_out)
     out(cum_row, cum_row_out)
     out(step_row, step_row_out)
+    each(gx, "last")
     each(gz, "line", 1)
     each(gz, "near")
-    each(gx, "last")
     each(gx, "complete")
 
-    g_flat = g_ref.reshape(3, GROUPS, WIDTH, COLS)
-
-    def weights(item, m, buf):
-        return pltpu.make_async_copy(g_flat.at[item, m], wbuf.at[buf, m], wsem.at[buf, m])
-
-    def load(item, buf):
-        for m in range(GROUPS):
-            weights(item, m, buf).start()
-
-    def pairs(item, buf, lo, hi, body):
+    x_flat, o_flat = wx.reshape(GROUPS, WIDTH, COLS), wo.reshape(GROUPS, WIDTH, COLS)
+    g_flat = g_ref.reshape(2, GROUPS, WIDTH, COLS)
+
+    def z_copy(m):
+        return pltpu.make_async_copy(g_flat.at[1, m], x_flat.at[m], wsem.at[m])
+
+    def pairs(buf, lo, hi, body, ready=None):
         @pl.loop(lo, hi)
         def _(i):
-            for k in range(2):
-                weights(item, 2 * i + k, buf).wait()
-            body(i, jnp.concatenate([wbuf[buf, 2 * i], wbuf[buf, 2 * i + 1]], axis=1))
-
-    load(0, 0)
+            if ready is not None:
+                for k in range(2):
+                    ready(2 * i + k).wait()
+            body(i, jnp.concatenate([buf[2 * i], buf[2 * i + 1]], axis=1))
+
+    out(wx, g_ref.at[0])
+    x_written = writes.pop()
 
     def to_owner(m):
         return pltpu.make_async_remote_copy(src_ref=local.at[m], dst_ref=rec_a.at[block], send_sem=es.at[m], recv_sem=er.at[block],
@@ -432,16 +458,13 @@
             local[m] = dot(weighted, bc_conv[:, :128], (0, 0)).astype(BF16)
             pl.when(m != block)(lambda m=m: to_owner(m).start())
 
-    pairs(0, 0, 0, 4, second_pair)
+    pairs(x_flat, 0, 4, second_pair)
+    each(go, "line", 1)
     rec_a[block] = local[block]
     out(x_pre, x_pre_out)
     out(x_conv, x_conv_out)
 
     top, low = slice(0, HALF), slice(HALF, ROWS)
-
-    def decays(cum, rows, h):
-        col, row = cum[:, h : h + 1], rows[h : h + 1, :]
-        return (jnp.exp(jnp.minimum(col[top] - row[:, top], 0.0)), jnp.exp(jnp.minimum(col[low] - row, 0.0)))
 
     def scan_group(m):
         xc = x_conv[m]
@@ -451,17 +474,19 @@
         parts = []
         for h in range(HEADS):
             xh = xc[:, 64 * h : 64 * h + 64]
-            step = step_rows[h : h + 1, :]
-            upper, lower = decays(cum, rows, h)
-            upper = (upper * gram[top, top] * step[:, top]).astype(BF16)
-            lower = (lower * gram[low] * step).astype(BF16)
-            parts.append(jnp.concatenate([dot(upper, xh[top]), dot(lower, xh)], axis=0))
-        yb[m] = jnp.concatenate(parts, axis=1) + spread(pk[m, 6:7, 12:20]) * xc.astype(F32)
-
-    each(go, "line", 1)
+            col, row, step = cum[:, h : h + 1], rows[h : h + 1, :], step_rows[h : h + 1, :]
+            upper = (jnp.exp(jnp.minimum(col[top] - row[:, top], 0.0)) * step[:, top]).astype(BF16)
+            lower = (jnp.exp(jnp.minimum(col[low] - row, 0.0)) * step).astype(BF16)
+            uppers[m, h] = upper
+            lowers[m, h] = lower
+            parts.append(jnp.concatenate([dot((upper.astype(F32) * gram[top, top]).astype(BF16), xh[top]),
+                                          dot((lower.astype(F32) * gram[low]).astype(BF16), xh)], axis=0))
+        yb[m] = jnp.concatenate(parts, axis=1) + spread(pk[m, 14:15, 0:8]) * xc.astype(F32)
+
+    pl.loop(0, 4)(scan_group)
     each(gz, "pass_on")
     each(go, "near")
-    pl.loop(0, GROUPS)(scan_group)
+    pl.loop(4, GROUPS)(scan_group)
     for c in dec_c:
         c.wait_recv()
     out(dec, dec_out)
@@ -485,106 +510,103 @@
     f_c = to_peers(rc, lambda p: out_b.at[p], state, fs, fr, block)
     state[block] = out_b[block]
     each(gz, "last")
-    each(go, "pass_on")
     each(gz, "complete")
-    load(1, 1)
+    x_written.wait()
+    each(gx, "drained")
+    for m in range(GROUPS):
+        z_copy(m).start()
 
     def gate_pair(i, w):
         z = dot(normed[HALO:, :], w)
         for k in range(2):
             zb[2 * i + k] = z[:, COLS * k : COLS * k + COLS]
 
-    pairs(1, 1, 0, 4, gate_pair)
-    each(go, "last")
-    each(go, "complete")
-    load(2, 0)
-
-    def cot_pair(i, w):
-        d = dot(cot[...], w)
-        for k in range(2):
-            db[2 * i + k] = d[:, COLS * k : COLS * k + COLS]
-
-    pairs(2, 0, 0, 4, cot_pair)
+    pairs(x_flat, 0, 4, gate_pair, z_copy)
+    each(go, "pass_on")
     for c in f_c:
         c.wait_recv()
         rc.sent(c)
     out(state, state_out)
     square[...] = jnp.zeros_like(square)
-    inner[...] = jnp.zeros_like(inner)
     c_mat = bc_conv[:, 128:]
 
     @pl.loop(0, GROUPS)
     def _(m):
         carried = dot(c_mat, state[m], (1, 1))
         y = yb[m] + spread(jnp.exp(cols[m][:, :8])) * carried
-        yb[m] = y
         z = zb[m]
-        gated = y * (z * jax.nn.sigmoid(z))
+        sig = jax.nn.sigmoid(z)
+        act = z * sig
+        gated = y * act
+        yb[m] = gated
+        zb[m] = act
+        d_z[m] = (y * sig * (1.0 + z * (1.0 - sig))).astype(BF16)
         sq = gated * gated
-        ip = db[m] * pk[m, 5:6] * gated
         square[...] += sq[:, :128] + sq[:, 128:256] + sq[:, 256:]
-        inner[...] += ip[:, :128] + ip[:, 128:256] + ip[:, 256:]
 
     r2 = lax.rsqrt(jnp.sum(square[...], axis=1, keepdims=True) / INNER + EPS)
-    slope = r2 * r2 * r2 * (jnp.sum(inner[...], axis=1, keepdims=True) / INNER)
-    scales[...] = jnp.concatenate([r2, slope, jnp.zeros((ROWS, 6), F32)], axis=1)
+
+    @pl.loop(0, GROUPS)
+    def _(m):
+        out_in[m] = (yb[m] * r2 * pk[m, 5:6]).astype(BF16)
+
     acc[...] = jnp.zeros_like(acc)
     d_c[...] = jnp.zeros_like(d_c)
     d_gram[...] = jnp.zeros_like(d_gram)
+    each(go, "last")
+    each(go, "complete")
+
+    def result_pair(i, w):
+        acc[...] += dot(jnp.concatenate([out_in[2 * i], out_in[2 * i + 1]], axis=1), w, (1, 1))
+
+    pairs(o_flat, 0, 4, result_pair)
+    total = jnp.sum(cot[...].astype(F32) * acc[...], axis=1, keepdims=True)
+    scales[...] = jnp.concatenate([r2, r2 * r2 * (total / INNER), jnp.zeros((ROWS, 6), F32)], axis=1)
+    result[...] = (hid[...].astype(F32) + acc[...]).astype(BF16)
+    out(result, result_out)
 
     def to_owner_back(m):
-        return pltpu.make_async_remote_copy(src_ref=local.at[m], dst_ref=rec_a.at[block], send_sem=gs.at[m], recv_sem=gr.at[block],
+        return pltpu.make_async_remote_copy(src_ref=local.at[m], dst_ref=rec_a.at[block], send_sem=es.at[m], recv_sem=er.at[block],
                                             device_id=block_device(m), device_id_type=MESHID)
 
-    @pl.loop(0, 4)
-    def _(i):
+    def gate_back(i, w):
         r2, slope = scales[:, 0:1], scales[:, 1:2]
+        both = dot(cot[...], w)
         for k in range(2):
             m = 2 * i + k
-            z, y, d = zb[m], yb[m], db[m]
-            gain_row = pk[m, 5:6]
-            sig = jax.nn.sigmoid(z)
-            act = z * sig
-            gated = y * act
-            unit = gated * r2
-            out_in[m] = (unit * gain_row).astype(BF16)
-            gain_part[m] = jnp.sum(d * unit, axis=0, keepdims=True)
-            d_gated = r2 * (d * gain_row) - gated * slope
-            dy = d_gated * act
-            d_z[m] = (d_gated * y * sig * (1.0 + z * (1.0 - sig))).astype(BF16)
+            d = both[:, COLS * k : COLS * k + COLS]
+            gated = yb[m]
+            gain_part[m] = jnp.sum(d * (gated * r2), axis=0, keepdims=True)
+            d_gated = r2 * (d * pk[m, 5:6]) - gated * slope
+            dy = d_gated * zb[m]
+            d_z[m] = (d_gated * d_z[m].astype(F32)).astype(BF16)
             yb[m] = dy
             skip_part[m] = jnp.sum(dy * x_conv[m].astype(F32), axis=0, keepdims=True)
             grown = spread(jnp.exp(cols[m][:, :8]))
-            dye = (grown * dy).astype(BF16)
+            scaled = grown * dy
+            dye = scaled.astype(BF16)
             d_c[...] += dot(dye, state[m])
             local[m] = dot(dye, c_mat, (0, 0)).astype(BF16)
             pl.when(m != block)(lambda m=m: to_owner_back(m).start())
-            d_cols[m] = jnp.concatenate([gathered_heads(dy * (grown * dot(c_mat, state[m], (1, 1)))), jnp.zeros((ROWS, 8), F32)],
-                                        axis=1)
-        acc[...] += dot(jnp.concatenate([out_in[2 * i], out_in[2 * i + 1]], axis=1),
-                        jnp.concatenate([wbuf[0, 2 * i], wbuf[0, 2 * i + 1]], axis=1), (1, 1))
-
+            d_cols[m] = jnp.concatenate([gathered_heads(scaled * dot(c_mat, state[m], (1, 1))), jnp.zeros((ROWS, 8), F32)], axis=1)
+
+    pairs(o_flat, 0, 4, gate_back)
     rec_a[block] = local[block]
-    result[...] = (hid[...].astype(F32) + acc[...]).astype(BF16)
     across = [rc(src, dst, xs.at[i], xr.at[i], neighbour("core", 1)) for i, (src, dst) in enumerate((
         (cot_t.at[:, 1 - core], cot_t2_out), (out_in, out_in2_out), (normed_t.at[:, 1 - core], normed_t2_out),
         (d_z, d_z2_out)))]
-    out(result, result_out)
     out(out_in, out_in_out)
     out(d_z, d_z_out)
     out(gain_part, gain_part_out)
     out(skip_part, skip_part_out)
 
     def d_x_copy(m):
-        return pltpu.make_async_copy(zb.at[m], d_x_out.at[m], ysem.at[m])
+        return pltpu.make_async_copy(zb.at[m], d_x_out.at[m], wsem.at[m])
 
     def inner_group(m):
         dy = yb[m]
         dyb = dy.astype(BF16)
         xc = x_conv[m]
-        cum = cols[m][:, :8]
-        rows = cum_row[m]
-        step_rows = step_row[m]
         d_cum = d_cols[m][:, :8]
         lane = lax.broadcasted_iota(jnp.int32, (ROWS, 8), 1)
         parts = []
@@ -592,29 +614,27 @@
         for h in range(HEADS):
             xh = xc[:, 64 * h : 64 * h + 64]
             dyh = dyb[:, 64 * h : 64 * h + 64]
-            step = step_rows[h : h + 1, :]
-            upper, lower = decays(cum, rows, h)
-            d_upper = dot(dyh[top], xh[top], (1, 1))
-            d_lower = dot(dyh[low], xh, (1, 1))
-            up, lo = upper * gram[top, top], lower * gram[low]
-            ru, rl = up * d_upper, lo * d_lower
-            col = jnp.sum(rl, axis=0, keepdims=True)
-            sums.append(jnp.concatenate([col[:, top] + jnp.sum(ru, axis=0, keepdims=True), col[:, low]], axis=1))
-            row = jnp.concatenate([jnp.sum(ru * step[:, top], axis=1, keepdims=True),
-                                   jnp.sum(rl * step, axis=1, keepdims=True)], axis=0)
+            upper, lower = uppers[m, h].astype(F32), lowers[m, h].astype(F32)
+            tu = upper * dot(dyh[top], xh[top], (1, 1))
+            tl = lower * dot(dyh[low], xh, (1, 1))
+            d_gram[top, top] += tu
+            d_gram[low] += tl
+            qu, ql = tu * gram[top, top], tl * gram[low]
+            col = jnp.sum(ql, axis=0, keepdims=True)
+            sums.append(jnp.concatenate([col[:, top] + jnp.sum(qu, axis=0, keepdims=True), col[:, low]], axis=1))
+            row = jnp.concatenate([jnp.sum(qu, axis=1, keepdims=True),
+                                   jnp.sum(ql[:, top] + ql[:, low], axis=1, keepdims=True)], axis=0)
             d_cum = jnp.where(lane == h, d_cum + row, d_cum)
-            d_gram[top, top] += upper * d_upper * step[:, top]
-            d_gram[low] += lower * d_lower * step
-            below = dot((lo * step).astype(BF16), dyh[low], (0, 0))
-            parts.append(jnp.concatenate([below[top] + dot((up * step[:, top]).astype(BF16), dyh[top], (0, 0)), below[low]],
-                                         axis=0))
+            below = dot((lower * gram[low]).astype(BF16), dyh[low], (0, 0))
+            above = dot((upper * gram[top, top]).astype(BF16), dyh[top], (0, 0))
+            parts.append(jnp.concatenate([below[top] + above, below[low]], axis=0))
         sums = jnp.concatenate(sums + [jnp.zeros((2, ROWS), F32)], axis=0).T
-        zb[m] = jnp.concatenate(parts, axis=1) + spread(pk[m, 6:7, 12:20]) * dy
+        zb[m] = jnp.concatenate(parts, axis=1) + spread(pk[m, 14:15, 0:8]) * dy
         d_x_copy(m).start()
-        d_cols[m] = jnp.concatenate([d_cum - sums * cols[m][:, 8:], sums], axis=1)
+        d_cols[m] = jnp.concatenate([d_cum - sums, sums], axis=1)
 
     pl.loop(0, 4)(inner_group)
-    exchanged(local, gs, gr)
+    exchanged(local, es, er)
     carry(range(BLOCKS - 1, -1, -1))
     b_c = to_peers(rc, lambda p: out_b.at[p], d_state, fs, fr, block)
     d_state[block] = out_b[block]
@@ -636,7 +656,7 @@
 
 HALF = ROWS // 2
 RESULTS = (
-    ("pk", (GROUPS, 8, COLS), F32), ("x_pre", (GROUPS, HALO + ROWS, COLS), F32), ("x_conv", (GROUPS, ROWS, COLS), BF16),
+    ("pk", (GROUPS, 16, COLS), F32), ("x_pre", (GROUPS, HALO + ROWS, COLS), F32), ("x_conv", (GROUPS, ROWS, COLS), BF16),
     ("d_x", (GROUPS, ROWS, COLS), F32), ("normed_t", (8, 2, 96, ROWS), BF16), ("cot_t", (8, 2, 96, ROWS), BF16),
     ("state", (GROUPS, COLS, 128), BF16), ("bc_pre", (HALO + ROWS, 256), F32), ("bc_conv", (ROWS, 256), BF16),
     ("steps", (ROWS, 128), F32), ("rates", (8, 128), F32), ("cols", (GROUPS, ROWS, 16), F32),
@@ -651,7 +671,7 @@
 )
 
 
-def forward(w3, bc, dt, pk, hid, cot, gain, taps_bc):
+def forward(zx, wo, bc, hid, cot, *params):
     hbm = pl.BlockSpec(memory_space=pl.ANY)
     vmem = pl.BlockSpec(memory_space=pltpu.VMEM)
     sem = pltpu.SemaphoreType.DMA
@@ -665,104 +685,85 @@
     groups = (GROUPS, ROWS, COLS)
     outs = pl.pallas_call(
         forward_kernel,
-        out_shape=(sds(3, 4, 2, 2, 4, 2, 96, COLS, dtype=BF16), sds(2, 4, 2, 96, COLS, dtype=BF16),
+        out_shape=(sds(2, 4, 2, 2, 4, 2, 96, COLS, dtype=BF16), sds(2, 4, 2, 96, COLS, dtype=BF16),
                    *[sds(*shape, dtype=dtype) for _, shape, dtype in RESULTS + SIBLING]),
-        in_specs=[hbm, vmem, vmem, vmem, vmem, hbm, vmem, vmem],
+        in_specs=[hbm, hbm, vmem, vmem, hbm] + [vmem] * 8,
         out_specs=(hbm,) * (2 + len(RESULTS) + len(SIBLING)),
         scratch_shapes=[
             *[pltpu.VMEM(shape, dtype) for name, shape, dtype in RESULTS if name != "d_x"],
-            b(ROWS, WIDTH), b(HALO + ROWS, WIDTH), b(HALO, WIDTH), b(BLOCKS, 96, 128), b(96, 128), b(2, 4, 2, 96, COLS),
-            v(*groups), v(*groups), v(*groups), b(2, GROUPS, WIDTH, COLS), v(ROWS, ROWS), v(ROWS, ROWS),
+            b(ROWS, WIDTH), b(HALO + ROWS, WIDTH), b(HALO, WIDTH), b(96, 128), b(2, 4, 2, 96, COLS),
+            v(*groups), v(*groups), b(GROUPS, HEADS, HALF, HALF), b(GROUPS, HEADS, HALF, ROWS),
+            b(4, 2, 2, 4, 2, 96, COLS), b(4, 2, 2, 4, 2, 96, COLS),
+            v(ROWS, ROWS), v(ROWS, ROWS),
             b(GROUPS, COLS, 128), b(GROUPS, COLS, 128), b(GROUPS, COLS, 128), v(GROUPS, 8, 128),
-            v(ROWS, 128), v(ROWS, 128), v(ROWS, 8), v(ROWS, WIDTH), v(ROWS, 128),
-            sem((90,)), sem((90,)), sem((90,)), sem((90,)), sem((18,)), sem((18,)), sem((8,)), sem((8,)), sem((8,)),
-            sem((8,)), sem((8,)), sem((8,)), sem((8,)), sem((8,)), sem((8,)), sem((8,)), sem((8,)), sem((8,)), sem, sem,
-            sem((4,)), sem((2, GROUPS)), sem((len(RESULTS),)), sem((GROUPS,)), sem((4,)), sem((4,)),
+            v(ROWS, 128), v(ROWS, 8), v(ROWS, WIDTH), v(ROWS, 128), v(16, COLS), v(1, WIDTH),
+            sem((27,)), sem((90,)), sem((36,)), sem((36,)), sem((18,)), sem((18,)), sem((8,)), sem((8,)), sem((8,)), sem((8,)),
+            sem((8,)), sem((8,)), sem((8,)), sem((8,)), sem, sem, sem((7,)), sem((GROUPS,)), sem((len(RESULTS),)), sem((4,)),
+            sem((4,)),
         ],
         compiler_params=pltpu.CompilerParams(collective_id=0, has_side_effects=True, vmem_limit_bytes=62 * 2**20),
         name="forward_between_devices",
-    )(w3, bc, dt, pk, hid, cot, gain, taps_bc)
+    )(zx, wo, bc, hid, cot, *params)
     return outs[0], outs[1], dict(zip([name for name, _, _ in RESULTS + SIBLING], outs[2:]))
 
 
 class Total:
-    def __init__(self, rc, value, core, xs, yl, yh, zs, send, recv):
-        self.rc, self.value, self.core, self.xs, self.yl, self.yh, self.zs = rc, value, core, xs, yl, yh, zs
-        self.send, self.recv, self.at = send, recv, 0
-        self.me = my_place()
-
-    def push(self, dst, device):
-        k = self.at
-        self.at += 1
-        return self.rc(self.value, dst, self.send.at[k], self.recv.at[k], device)
-
-    def done(self):
-        for c in self.flying:
-            c.wait_recv()
-        for c in self.flying:
-            self.rc.sent(c)
+    def __init__(self, rc, value, lines, axes, send, recv):
+        self.rc, self.value, self.lines, self.axes, self.send, self.recv = rc, value, lines, axes, send, recv
+        self.me = dict(my_place(), core=lax.axis_index("core"), ylo=lax.axis_index("ylo"))
 
     def step(self, j):
-        v, me = self.value, self.me
-        if j == 0:
-            self.flying = [self.push(self.core, neighbour("core", 1))]
-        elif j == 1:
-            self.done()
-            v[...] = v[...] + self.core[...]
-            self.xs[me["x"]] = v[...]
-            self.flying = [self.push(self.xs.at[me["x"]], neighbour("x", d)) for d in (1, 2, 3)]
-        elif j == 2:
-            self.done()
-            v[...] = (self.xs[0] + self.xs[1]) + (self.xs[2] + self.xs[3])
-            self.flying = [self.push(self.yl, {"ylo": 1 - lax.axis_index("ylo")})]
-        elif j == 3:
-            self.done()
-            v[...] = v[...] + self.yl[...]
-            self.flying = [self.push(self.yh, {"yhi": 1 - lax.axis_index("yhi")})]
-        elif j == 4:
-            self.done()
-            v[...] = v[...] + self.yh[...]
-            self.zs[me["z"]] = v[...]
-            self.flying = [self.push(self.zs.at[me["z"]], neighbour("z", d)) for d in (1, 2, 3)]
-        elif j == 5:
-            self.done()
-            v[...] = (self.zs[0] + self.zs[1]) + (self.zs[2] + self.zs[3])
+        if j > 0:
+            for c in self.flying:
+                c.wait_recv()
+                self.rc.sent(c)
+            l, i = self.lines, j - 1
+            if self.axes[i] in ("core", "ylo"):
+                self.value[...] = l[i, 0] + l[i, 1]
+            else:
+                self.value[...] = (l[i, 0] + l[i, 1]) + (l[i, 2] + l[i, 3])
+        if j < len(self.axes):
+            a = self.axes[j]
+            mine = self.lines.at[j, self.me[a]]
+            mine[...] = self.value[...]
+            if a in ("core", "ylo"):
+                devices = [{a: 1 - self.me[a]}]
+            else:
+                devices = [neighbour(a, d) for d in (1, 2, 3)]
+            self.flying = [self.rc(mine, mine, self.send.at[d], self.recv.at[3 * j + d], device)
+                           for d, device in enumerate(devices)]
 
 
 class SmallSum:
-    def __init__(self, rc, parts, xs, ys, zs, hs, send, recv):
-        self.rc, self.parts, self.xs, self.ys, self.zs, self.hs = rc, parts, xs, ys, zs, hs
+    def __init__(self, rc, parts, xs, ys, zs, send, recv):
+        self.rc, self.parts, self.xs, self.ys, self.zs = rc, parts, xs, ys, zs
         self.send, self.recv = send, recv
         self.me = my_place()
 
     def step(self, j, out=None):
         rc, me, parts, s, r = self.rc, self.me, self.parts, self.send, self.recv
-        ylo = lax.axis_index("ylo")
+        ylo = lax.rem(me["y"], 2)
         if j == 0:
             self.c = [rc(parts.at[:, lax.rem(me["x"] + d, 4)], self.xs.at[d - 1], s.at[d], r.at[d], neighbour("x", d))
                       for d in (1, 2, 3)]
-        elif j == 1:
-            for c in self.c:
-                c.wait_recv()
+            return
+        for c in self.c:
+            c.wait_recv()
+        if j == 1:
             for yl in range(2):
                 m = parts.at[yl, me["x"]]
                 m[...] = (f32(m) + f32(self.xs.at[0, yl]) + f32(self.xs.at[1, yl]) + f32(self.xs.at[2, yl])).astype(BF16)
-            self.c = [rc(parts.at[1 - ylo, me["x"]], self.ys, s.at[4], r.at[4], {"ylo": 1 - ylo})]
+            self.ys[me["y"]] = parts[ylo, me["x"]]
+            self.c = [rc(parts.at[lax.rem(me["y"] + d, 2), me["x"]], self.ys.at[me["y"]], s.at[3 + d], r.at[3 + d],
+                         neighbour("y", d)) for d in (1, 2, 3)]
         elif j == 2:
-            self.c[0].wait_recv()
-            m = parts.at[ylo, me["x"]]
-            m[...] = (f32(m) + f32(self.ys)).astype(BF16)
-            self.zs[me["z"]] = m[...]
-            self.c = [rc(m, self.zs.at[me["z"]], s.at[4 + d], r.at[4 + d], neighbour("z", d)) for d in (1, 2, 3)]
+            y = self.ys
+            m = self.zs.at[me["z"]]
+            m[...] = ((f32(y.at[0]) + f32(y.at[1])) + (f32(y.at[2]) + f32(y.at[3]))).astype(BF16)
+            self.c = [rc(m, m, s.at[6 + d], r.at[6 + d], neighbour("z", d)) for d in (1, 2, 3)]
         elif j == 3:
-            for c in self.c:
-                c.wait_recv()
-            z, hs = self.zs, self.hs
-            hs[0] = ((f32(z.at[0]) + f32(z.at[1])) + (f32(z.at[2]) + f32(z.at[3]))).astype(BF16)
-            self.c = [rc(hs.at[0], hs.at[1], s.at[8], r.at[8], {"yhi": 1 - lax.axis_index("yhi")})]
-        elif j == 4:
-            self.c[0].wait_recv()
-            out[...] = f32(self.hs.at[0]) + f32(self.hs.at[1])
+            z = self.zs
+            return (f32(z.at[0]) + f32(z.at[1])) + (f32(z.at[2]) + f32(z.at[3]))
 
 
 def part_of(ref, item, pos, lo, n):
@@ -782,8 +783,10 @@
         self.full, self.half = full[r].at[wide], half[r].at[wide]
         self.direct = {1: second[r].at[slot], 2: third.at[slot * 3 + r]}
         self.send, self.recv = sems
-        self.base = (slot * 3 + r) * 10
+        self.number = slot * 3 + r
+        self.base = self.number * 10
         self.me = my_place()
+        self.flying = {}
 
     def slab(self, st, d, lo=0, n=SUB):
         p = {a: (self.me[a] if i < st else None) for i, a in enumerate(ORDERS[self.r])}
@@ -813,8 +816,12 @@
                         body((i // 2, lax.rem(i, 2), k))
 
     def push(self, k, src, dst, st, d):
-        t = self.base + k
-        return self.rc(src, dst, self.send.at[t], self.recv.at[t], neighbour(ORDERS[self.r][st], d))
+        s = k % 2 if k < 4 else (k - 4) % 3
+        if s in self.flying:
+            self.rc.sent(self.flying[s])
+        c = self.rc(src, dst, self.send.at[3 * self.number + s], self.recv.at[self.base + k], neighbour(ORDERS[self.r][st], d))
+        self.flying[s] = c
+        return c
 
     def far(self):
         self.far_c = [self.push(i, self.slab(0, 2, 16 * i, 16), self.half.at[i], 0, d) for i, d in enumerate((1, -1))]
@@ -869,19 +876,21 @@
                 self.loop(1, add)
                 self.straight(2)
             else:
-                self.out[self.item, pl.ds(self.r * SUB, SUB)] = total(())
+                self.out(pl.ds(self.r * SUB, SUB))[...] = total(())
 
 
 def backward_kernel(g_ref, x_conv_ref, d_x_ref, x_pre_ref, cols_ref, d_cols_ref, cot_t_ref, cot_t2_ref, out_in_ref, out_in2_ref,
                     normed_t_ref, normed_t2_ref, d_z_ref, d_z2_ref, state_ref, d_state_ref, w_small_ref, hid_ref, cot_ref,
-                    taps, d_bc_in, bc_pre, bc_conv, taps_bc, shifted, rates, gain, gain_part, skip_part,
-                    out_ref, sout_ref, vout_ref, nout_ref, grad_hidden, *scr):
+                    taps, d_bc_in, bc_pre, bc_conv, taps_bc, norm_gain, shifted, rates, gain_part, skip_part,
+                    zx_out, wo_out, wbc_out, wdt_out, taps_out, taps_bc_out, log_out, shift_out, skip_out, gate_out, norm_out,
+                    grad_hidden, *scr):
     (own, l_c, l_c2, l_n, l_n2, rhs_o, rhs_z, rhs_x, state, d_state, w_small, hid, cot, tails, halo_src, halo_dst, acc, wbuf,
-     bxc, bdx, bxp, bcols, bdc, d_b, d_all, parts, small2, s_xs, s_ys, s_zs, s_hs,
-     v_core, v_xs, v_yl, v_yh, v_zs, n_core, n_xs, n_yl, n_yh, n_zs) = scr[:41]
-    bufs = [scr[41:44], scr[44:47], scr[47:50], scr[50]]
-    (t_s, t_r, x_s, x_r, h_s, h_r, m_s, m_r, ss, sr, vs, vr, ns, nr, wsem, lsem, isem, freed) = scr[51:]
+     bxc, bdx, bxp, bcols, bdc, d_b, d_all, parts, small2, s_xs, s_ys, s_zs,
+     v_all, v_in, v_sum, v_lines, n_all, n_lines, gain) = scr[:37]
+    bufs = [scr[37:40], scr[40:43], scr[43:46], scr[46]]
+    (t_s, t_r, x_s, x_r, h_s, h_r, m_s, m_r, ss, sr, vms, vmr, vs, vr, ns, nr, wsem, lsem, isem, freed) = scr[47:]
     rc = Sender()
+    gain[0] = norm_gain[...]
     core = lax.axis_index("core")
     block = lax.axis_index("z") * 2 + lax.axis_index("yhi")
     arrived = greet()
@@ -903,8 +912,10 @@
     load_in("z", (normed_t_ref.at[:, core], l_n), (normed_t2_ref, l_n2), (d_z_ref, rhs_z.at[0]), (d_z2_ref, rhs_z.at[1]))
     load_in("s", (state_ref, state), (d_state_ref, d_state))
 
+    outs = (lambda at: zx_out.at[at, 1], lambda at: zx_out.at[at, 0], lambda at: wo_out.at[at])
+
     def chunks(item, slot, wide):
-        return [Chunk(rc, own, out_ref, bufs, (t_s, t_r), item, slot, wide, r) for r in range(3)]
+        return [Chunk(rc, own, outs[item], bufs, (t_s, t_r), item, slot, wide, r) for r in range(3)]
 
     def steps(cs, j):
         for c in cs:
@@ -913,8 +924,10 @@
     def both_tokens(own_t, other_t):
         return jnp.concatenate([own_t[...].reshape(768, ROWS), other_t[...].reshape(768, ROWS)], axis=1)
 
-    def gradient(left, left2, rhs, slot):
+    def gradient(left, left2, rhs, slot, ready=None):
         def one(m):
+            if ready is not None:
+                ready(m)
             v = dot(both_tokens(left, left2), jnp.concatenate([rhs[0, m], rhs[1, m]], axis=0))
             own[slot, m // 2, lax.rem(m, 2)] = v.astype(BF16).reshape(2, 4, 96, COLS)
 
@@ -971,13 +984,13 @@
         row = lax.broadcasted_iota(jnp.int32, (ROWS, 8), 0)
         d_cum = bdc[k][:, :8] - both
         d_cum = jnp.where(row == ROWS - 1, d_cum + d_last, d_cum)
-        d_all[m] = jnp.concatenate([d_cum, bdc[k][:, 8:] + tail * d_weights], axis=1)
+        d_all[m] = jnp.concatenate([d_cum, bdc[k][:, 8:] + both], axis=1)
         ext = bxp[k]
         tap = taps[m]
         pre = conv_pre(ext, tap)
         sig = jax.nn.sigmoid(pre)
         dp = dx * (sig * (1.0 + pre * (1.0 - sig)))
-        vout_ref[m] = conv_grads(dp, ext, gain_part[m], skip_part[m])
+        v_all[m, 0:8] = conv_grads(dp, ext, gain_part[m], skip_part[m])
         whole_dx = conv_transposed(jnp.concatenate([dp, jnp.zeros((8, COLS), F32)], axis=0), tap)
         rhs_x[0, m] = whole_dx.astype(BF16)
         tails[m] = whole_dx[ROWS - 16 :]
@@ -1006,13 +1019,18 @@
     d_decay = dot(triangle(True).astype(F32), d_cum, precision=lax.Precision.HIGHEST)
     rate = -jnp.exp(rates[0:1])
     v = shifted[...]
-    d_dt = (d_step + rate * d_decay) * jax.nn.sigmoid(v)
+    sig = jax.nn.sigmoid(v)
+    far = v < -16.0
+    ratio = jnp.where(far, 1.0, sig / jnp.where(far, 1.0, softplus(v)))
+    d_dt = d_step * ratio + rate * d_decay * sig
     log_grad = jnp.sum(d_decay * (softplus(v) * rate), axis=0, keepdims=True)
     shift_grad = jnp.sum(d_dt, axis=0, keepdims=True)
     bc_rows = conv_grads(dp_bc, ext, jnp.concatenate([log_grad, shift_grad], axis=1), zero8)
-    vout_ref[GROUPS] = jnp.concatenate([bc_rows, jnp.zeros((8, 128), F32)], axis=1)
-    vec = Total(rc, vout_ref, v_core, v_xs, v_yl, v_yh, v_zs, vs, vr)
-    vec.step(0)
+    bc_rows = jnp.concatenate([bc_rows, jnp.zeros((8, 128), F32)], axis=1)
+    for m in range(GROUPS):
+        v_all[m, 8:16] = bc_rows
+    vec_c = to_peers(rc, lambda p: v_all.at[p], v_in, vms, vmr, block)
+    v_in[block] = v_all[block]
 
     halo.wait_recv()
     inside = block < 7
@@ -1033,7 +1051,6 @@
     d_bc = conv_transposed(jnp.concatenate([dp_bc, below(GROUPS)[:, :256]], axis=0), taps_bc[...])
     small2[0] = jnp.concatenate([d_bc, d_dt], axis=1).astype(BF16)
     small_c = rc(small2.at[0], small2.at[1], m_s, m_r, neighbour("core", 1))
-    vec.step(1)
 
     def weights(m):
         k = lax.rem(m, 2)
@@ -1041,16 +1058,15 @@
 
     for c in weights(0):
         c.start()
-    for m in range(GROUPS):
-        across(m).wait()
-    gradient(l_n, l_n2, rhs_x, 2)
+    small_c.wait_recv()
+    parts[...] = dot(both_tokens(l_n, l_n2), small2[...].reshape(2 * ROWS, COLS)).astype(BF16).reshape(2, 4, 96, COLS)
+    sums = SmallSum(rc, parts, s_xs, s_ys, s_zs, ss, sr)
+    sums.step(0)
+    gradient(l_n, l_n2, rhs_x, 2, lambda m: across(m).wait())
     pl.semaphore_wait(freed, 6)
     steps(xc_, 0)
-    small_c.wait_recv()
-    parts[...] = dot(both_tokens(l_n, l_n2), small2[...].reshape(2 * ROWS, COLS)).astype(BF16).reshape(2, 4, 96, COLS)
     ready("end")
     acc[...] = dot(small2[0], w_small[...], (1, 1))
-
     def input_group(m):
         k = lax.rem(m, 2)
 
@@ -1066,10 +1082,15 @@
         acc[...] += dot(lhs, rhs, (1, 1))
 
     pl.loop(0, 4)(input_group)
-    vec.step(2)
     steps(xc_, 1)
-    sums = SmallSum(rc, parts, s_xs, s_ys, s_zs, s_hs, ss, sr)
-    sums.step(0)
+    for c in vec_c:
+        c.wait_recv()
+    t = v_in[0]
+    for i in range(1, BLOCKS):
+        t = t + v_in[i]
+    v_sum[...] = t
+    vec = Total(rc, v_sum, v_lines, ("core", "x", "ylo"), vs, vr)
+    vec.step(0)
     pl.loop(4, GROUPS)(input_group)
     v = hid[...].astype(F32)
     r = lax.rsqrt(jnp.mean(v * v, axis=1, keepdims=True) + EPS)
@@ -1077,36 +1098,52 @@
     dn = acc[...]
     gain_grad = jnp.sum(dn * unit, axis=0, keepdims=True)
     for i in range(4):
-        nout_ref[0, pl.ds(i, 1)] = gain_grad[:, COLS * i : COLS * i + COLS]
-    nout_ref[0, pl.ds(4, 4)] = jnp.zeros((4, COLS), F32)
-    nvec = Total(rc, nout_ref, n_core, n_xs, n_yl, n_yh, n_zs, ns, nr)
+        n_all[pl.ds(i, 1)] = gain_grad[:, COLS * i : COLS * i + COLS]
+    n_all[pl.ds(4, 4)] = jnp.zeros((4, COLS), F32)
+    nvec = Total(rc, n_all, n_lines, ("core", "x", "y", "z"), ns, nr)
     nvec.step(0)
-    vec.step(3)
+    sums.step(1)
+    vec.step(1)
     d_in = dn * gain[...]
     grad_hidden[...] = r * (d_in - unit * jnp.mean(d_in * unit, axis=1, keepdims=True)) + cot[...].astype(F32)
     nvec.step(1)
+    steps(xc_, 2)
     steps(zc, 2)
     steps(oc, 3)
-    vec.step(4)
+    sums.step(2)
     nvec.step(2)
-    steps(xc_, 2)
-    sums.step(1)
+    vec.step(2)
+    steps(xc_, 3)
     nvec.step(3)
-    vec.step(5)
-    sums.step(2)
+    vec.step(3)
+    steps(zc, 3)
+    steps(oc, 4)
+
+    pick = lax.broadcasted_iota(jnp.int32, (8, 128), 0) + block * HEADS
+    pick = (pick == lax.broadcasted_iota(jnp.int32, (8, 128), 1)).astype(F32)
+
+    def own_heads(row):
+        return dot(row, pick, (1, 1), precision=lax.Precision.HIGHEST)
+
+    mine = v_sum[...]
+    taps_out[...] = mine[:5]
+    gate_out[...] = mine[5]
+    skip_out[...] = gathered_heads(mine[6:7])[0, :HEADS]
+    taps_bc_out[...] = mine[8:13, :256]
+    log_out[...] = own_heads(mine[13:14, :128])[0, :HEADS]
+    shift_out[...] = own_heads(mine[13:14, 128:256])[0, :HEADS]
+    steps(xc_, 4)
+    steps(zc, 4)
+    little = sums.step(3)
+    wbc_out[...] = little[:, :256]
+    wdt_out[...] = dot(pick, little[:, 256:], (1, 1), precision=lax.Precision.HIGHEST)[:HEADS]
     nvec.step(4)
-    steps(oc, 4)
-    steps(zc, 3)
-    steps(xc_, 3)
-    sums.step(3)
-    nvec.step(5)
-    steps(zc, 4)
-    sums.step(4, sout_ref)
-    steps(xc_, 4)
+    for i in range(4):
+        norm_out[pl.ds(COLS * i, COLS)] = n_all[i]
     rc.all_sent()
 
 
-def backward(w_all, r, w_small, hid, cot, taps_bc, gain):
+def backward(w_all, r, w_small, hid, cot, norm_gain, conv_bc):
     hbm = pl.BlockSpec(memory_space=pl.ANY)
     vmem = pl.BlockSpec(memory_space=pltpu.VMEM)
     sem = pltpu.SemaphoreType.DMA
@@ -1127,61 +1164,36 @@
         buf(GROUPS, 16, dtype=F32), buf(GROUPS + 1, 8, dtype=F32), buf(GROUPS + 1, 8, dtype=F32),
         v(ROWS, WIDTH), buf(2, 2, WIDTH),
         buf(2, ROWS), buf(2, ROWS, dtype=F32), buf(2, HALO + ROWS, dtype=F32), v(2, ROWS, 16), v(2, ROWS, 16),
-        v(ROWS, 128), v(GROUPS, ROWS, 16), buf(2, 4, 96), buf(2, ROWS), buf(3, 2, 96), buf(96), buf(4, 96), buf(2, 96),
+        v(ROWS, 128), v(GROUPS, ROWS, 16), buf(2, 4, 96), buf(2, ROWS), buf(3, 2, 96), buf(4, 96), buf(4, 96),
     ]
-    for n in (GROUPS + 1, 1):
-        one = buf(n, 8, dtype=F32)
-        four = buf(4, n, 8, dtype=F32)
-        scratch += [one, four, one, one, four]
+    scratch += [buf(GROUPS, 16, dtype=F32), buf(GROUPS, 16, dtype=F32), buf(16, dtype=F32), buf(3, 4, 16, dtype=F32)]
+    scratch += [buf(8, dtype=F32), buf(4, 4, 8, dtype=F32), v(1, WIDTH)]
     scratch += [buf(2, 2, 4, 2, 2, SUB), buf(2, 2, 4, 4, SUB), buf(2, 2, 2, 2, 4, SUB)]
     scratch += [buf(2, 2, 4, 2, 2, 16), buf(2, 2, 4, 4, 16), buf(2, 2, 2, 2, 4, 16)]
     scratch += [buf(3, 3, 4, SUB), buf(3, 3, 4, SUB), buf(3, 3, 2, 2, SUB), buf(9, 3, SUB)]
-    scratch += [sem((90,)), sem((90,)), sem((8,)), sem((8,)), sem, sem, sem, sem, sem((9,)), sem((9,)), sem((9,)), sem((9,)),
-                sem((9,)), sem((9,)), sem((2, 2)), sem((2, 5)), sem((13,)), pltpu.SemaphoreType.REGULAR]
+    scratch += [sem((27,)), sem((90,)), sem((8,)), sem((8,)), sem, sem, sem, sem, sem((10,)), sem((10,)), sem((8,)), sem((8,)),
+                sem((3,)), sem((9,)), sem((3,)), sem((12,)), sem((2, 2)), sem((2, 5)), sem((13,)), pltpu.SemaphoreType.REGULAR]
     names = ("x_conv", "d_x", "x_pre", "cols", "d_cols", "cot_t", "cot_t2", "out_in", "out_in2", "normed_t", "normed_t2", "d_z",
              "d_z2", "state", "d_state")
     return pl.pallas_call(
         backward_kernel,
-        out_shape=(sds(3, 96, COLS), sds(96, COLS), sds(GROUPS + 1, 8, COLS), sds(1, 8, COLS), sds(ROWS, WIDTH)),
+        out_shape=(sds(96, 2, COLS), sds(96, COLS), sds(96, 256), sds(HEADS, 96), sds(5, COLS), sds(5, 256), sds(HEADS), sds(HEADS),
+                   sds(HEADS), sds(COLS), sds(WIDTH), sds(ROWS, WIDTH)),
         in_specs=[hbm] * 19 + [vmem] * 10,
-        out_specs=(vmem,) * 5,
+        out_specs=(vmem,) * 12,
         scratch_shapes=scratch,
         compiler_params=pltpu.CompilerParams(collective_id=1, has_side_effects=True, vmem_limit_bytes=63 * 2**20),
         name="backward_between_devices",
-    )(w_all, *[r[name] for name in names], w_small, hid, cot, r["pk"], r["d_bc"], r["bc_pre"], r["bc_conv"], taps_bc,
-      r["steps"], r["rates"], gain, r["gain_part"], r["skip_part"])
+    )(w_all, *[r[name] for name in names], w_small, hid, cot, r["pk"], r["d_bc"], r["bc_pre"], r["bc_conv"], conv_bc, norm_gain,
+      r["steps"], r["rates"], r["gain_part"], r["skip_part"])
 def shards(hidden, grad_out, norm_gain, w_zx, w_bc, w_dt, conv_x, conv_bc, a_log, dt_bias, d_skip, gate_gain, w_out):
-    index = lax.axis_index(MP)
-    heads = jnp.concatenate([a_log, dt_bias, d_skip, jnp.zeros((COLS - 3 * HEADS,), F32)])[None]
-    packed = jnp.concatenate([conv_x, gate_gain[None], heads, jnp.zeros((1, COLS), F32)])
-    steps_own = lax.dynamic_update_slice(jnp.zeros((96, 128), BF16), w_dt, (0, index * HEADS))
-    taps_bc = jnp.pad(conv_bc, ((0, 3), (0, 0)))
-    gain = norm_gain[None]
-    w_all, w_small, r = forward(
-        jnp.stack([w_zx[:, 1], w_zx[:, 0], w_out.T]), w_bc, steps_own, packed, hidden, grad_out, gain, taps_bc)
-    w_all = w_all.reshape(3, GROUPS, WIDTH, COLS)
+    w_all, w_small, r = forward(jnp.moveaxis(w_zx, 1, 0), w_out.T, w_bc, hidden, grad_out, norm_gain, w_dt.T, conv_x, conv_bc,
+                                a_log, dt_bias, d_skip, gate_gain)
+    w_all = w_all.reshape(2, GROUPS, WIDTH, COLS)
     w_small = w_small.reshape(WIDTH, COLS)
-    owned, small, vector, norm_sum, grad_hidden = backward(w_all, r, w_small, hidden, grad_out, taps_bc, gain)
-
-    def own(flat):
-        return lax.dynamic_slice_in_dim(flat, index * HEADS, HEADS, flat.ndim - 1)
-
-    mine = lax.dynamic_index_in_dim(vector, index, 0, keepdims=False)
-    return (
-        r["result"],
-        grad_hidden,
-        norm_sum[0, :4].reshape(WIDTH),
-        jnp.stack([owned[1], owned[0]], axis=1),
-        small[:, :256],
-        own(small[:, 256:304]),
-        mine[:5],
-        vector[GROUPS, :5, :256],
-        own(vector[GROUPS, 5, :48]),
-        own(vector[GROUPS, 5, 128:176]),
-        mine[6].reshape(HEADS, 64).sum(axis=1),
-        mine[5],
-        owned[2].T,
-    )
+    zx, wo, wbc, wdt, grad_taps, grad_taps_bc, log_rate, shift, skip, gate, norm, grad_hidden = backward(
+        w_all, r, w_small, hidden, grad_out, norm_gain, conv_bc)
+    return (r["result"], grad_hidden, norm, zx, wbc, wdt.T, grad_taps, grad_taps_bc, log_rate, shift, skip, gate, wo.T)
 
 
 def solution(mesh):

time: 255 us -> 231 us (0.906)
  Pallas kernels: 233 us -> 219 us
  local copies, waits for them, and re-layouts: 17 us -> 11 us
  other arithmetic: 3 us -> 0 us
    pallas_call x2, Pallas kernels: 233 us -> 219 us  [the longest x1 133 us: forward(): pl.pallas_call(forward_kernel, out_shape=(sds(2, 4, 2, 2, 4, 2, 96, COLS,...]
    unnamed x27 -> x40, local copies, waits for them, and re-layouts: 4.49 us -> 11 us
    slice x7 -> x0, local copies, waits for them, and re-layouts: 6.09 us -> none  [the longest x1 1.38 us: shards(): mine[5]]
where the time goes in v4:
time: 231 us
  Pallas kernels  219 us (95%)
  local copies, waits for them, and re-layouts  11 us (5%)
    pallas_call x1, Pallas kernels, forward(): pl.pallas_call(forward_kernel, out_shape=(sds(2, 4, 2, 2, 4, 2, 96, COLS,...  133 us
    pallas_call x1, Pallas kernels, backward(): pl.pallas_call(backward_kernel, out_shape=(sds(96, 2, COLS), sds(96, COLS...  85.9 us
    unnamed x40, local copies, waits for them, and re-layouts  11 us

profile of v4, /device:TPU:0, one launch (start us, length us, event | category | flops | bytes accessed | tf_op | source)
XLA Modules:
  0.0 230.6 jit_solution(5028481095479150416)
XLA Ops:
  0.6 1.6 copy.28
  2.2 133.0 %forward_between_devices.1 = (bf16[2,4,2,2,4,2,96,384]{7,6,5,4,3,2,1,0:T(8,128)(2,1)}, bf16[2,4,2,96,384]{4,3,2,1,0:T(8,128)(2,1)}, f32[8,16,384]{2,1,0:T(8,128)...) custom-call(bf16[2,96,384]{2,1,0:T(8,128)(2,1)} %bitcast.11, ...), custom_call_target="tpu_custom_call" | custom-call | tf_op jit(solution)/shard_map/forward_between_devices/pallas_call | solution.py:686
  135.2 0.0 copy-start.1
  135.2 85.9 %backward_between_devices.1 = (f32[96,2,384]{2,1,0:T(2,128)}, f32[96,384]{1,0:T(8,128)}, f32[96,256]{1,0:T(8,128)}, f32[6,96]{1,0:T(8,128)}, f32[5,384]{1,0:T(8,...) custom-call(bf16[2,8,1536,384]{3,2,1,0:T(8,128)(2,1)} %bitcast.9, ...), custom_call_target="tpu_custom_call" | custom-call | tf_op jit(solution)/shard_map/backward_between_devices/pallas_call | solution.py:1178
  221.2 0.0 copy-start
  221.2 0.0 copy-done.1
  221.2 0.9 copy.42
  222.1 0.8 copy-done
  222.9 0.0 copy-start.7
  222.9 0.0 copy-start.2
  222.9 0.0 copy-start.4
  222.9 0.0 copy-start.8
  222.9 0.0 copy-start.5
  222.9 0.0 copy-start.6
  222.9 0.0 copy-start.12
  222.9 0.0 copy-start.11
  222.9 0.0 copy-start.10
  222.9 0.0 copy-start.9
  222.9 0.0 copy-start.3
  222.9 1.1 copy.43
  224.1 0.0 copy-done.7
  224.1 0.6 copy.44
  224.7 0.0 copy-done.2
  224.7 0.7 copy.45
  225.4 0.0 copy-done.4
  225.4 0.6 copy.46
  226.1 0.0 copy-done.8
  226.1 0.6 copy.47
  226.6 0.0 copy-done.5
  226.7 0.6 copy.48
  227.3 0.0 copy-done.6
  227.3 0.6 copy.49
  227.9 0.0 copy-done.12
  227.9 0.5 copy.50
  228.4 0.0 copy-done.11
  228.4 0.5 copy.51
  228.9 0.0 copy-done.10
  228.9 0.5 copy.52
  229.4 0.0 copy-done.9
  229.4 0.6 copy.53
  230.0 0.0 copy-done.3
  230.0 0.7 copy.54
Async XLA Ops:
  135.2 86.0 %copy-start.1 = (bf16[256,1536]{1,0:T(8,128)(2,1)S(1)}, bf16[256,1536]{1,0:T(8,128)(2,1)}, u32[]{:S(2)}) copy-start(bf16[256,1536]{1,0:T(8,128)(2,1)} %get-tuple-element.102) | copy-start | bytes 2359300
  221.2 1.7 copy-start
  222.9 1.2 copy-start.7
  222.9 1.8 copy-start.2
  222.9 2.5 %copy-start.4 = (f32[96,256]{1,0:T(8,128)S(1)}, f32[96,256]{1,0:T(8,128)}, u32[]{:S(2)}) copy-start(f32[96,256]{1,0:T(8,128)} %get-tuple-element.106) | copy-start | bytes 294916
  222.9 3.2 %copy-start.8 = (f32[6,96]{1,0:T(8,128)S(1)}, f32[6,96]{1,0:T(8,128)}, u32[]{:S(2)}) copy-start(f32[6,96]{1,0:T(8,128)} %get-tuple-element.81) | copy-start | bytes 6916
  222.9 3.8 %copy-start.5 = (f32[5,384]{1,0:T(8,128)S(1)}, f32[5,384]{1,0:T(8,128)}, u32[]{:S(2)}) copy-start(f32[5,384]{1,0:T(8,128)} %get-tuple-element.108) | copy-start | bytes 23044
  222.9 4.4 %copy-start.6 = (f32[5,256]{1,0:T(8,128)S(1)}, f32[5,256]{1,0:T(8,128)}, u32[]{:S(2)}) copy-start(f32[5,256]{1,0:T(8,128)} %get-tuple-element.109) | copy-start | bytes 15364
  222.9 5.0 %copy-start.12 = (f32[6]{0:T(128)S(1)}, f32[6]{0:T(128)}, u32[]{:S(2)}) copy-start(f32[6]{0:T(128)} %get-tuple-element.110) | copy-start | bytes 76
  222.9 5.5 %copy-start.11 = (f32[6]{0:T(128)S(1)}, f32[6]{0:T(128)}, u32[]{:S(2)}) copy-start(f32[6]{0:T(128)} %get-tuple-element.111) | copy-start | bytes 76
  222.9 6.0 %copy-start.10 = (f32[6]{0:T(128)S(1)}, f32[6]{0:T(128)}, u32[]{:S(2)}) copy-start(f32[6]{0:T(128)} %get-tuple-element.112) | copy-start | bytes 76
  222.9 6.5 %copy-start.9 = (f32[384]{0:T(512)S(1)}, f32[384]{0:T(512)}, u32[]{:S(2)}) copy-start(f32[384]{0:T(512)} %get-tuple-element.113) | copy-start | bytes 4612
  222.9 7.0 %copy-start.3 = (f32[96,384]{1,0:T(8,128)S(1)}, f32[96,384]{1,0:T(8,128)}, u32[]{:S(2)}) copy-start(f32[96,384]{1,0:T(8,128)} %get-tuple-element.88) | copy-start | bytes 442372

commit v5 on v4

--- a/solution.py
+++ b/solution.py
@@ -251,7 +251,7 @@
                    out_in_out, d_z_out, gain_part_out, skip_part_out, d_cols_out, d_bc_out, d_state_out,
                    normed_t2_out, cot_t2_out, out_in2_out, d_z2_out, *scr):
     (pk, x_pre, x_conv, normed_t, cot_t, state, bc_pre, bc_conv, steps, rates, cols, cum_row, step_row, dec,
-     result, out_in, d_z, gain_part, skip_part, d_cols, d_bc, d_state,
+     result, out_in, d_z, gain_part, skip_part, d_cols, d_bc,
      cot, normed, halo, dt_own, small_all, zb, yb, uppers, lowers, wx, wo, gram, d_gram, local, rec_a, out_b, dec_own, square,
      scales, acc, d_c, pk_ref, gain,
      ts, tr, cs, cr, bs, br, qs, qr, es, er, fs, fr, ds, dr, hs, hr, lsem, wsem, osem, xs, xr) = scr
@@ -582,12 +582,11 @@
             d_z[m] = (d_gated * d_z[m].astype(F32)).astype(BF16)
             yb[m] = dy
             skip_part[m] = jnp.sum(dy * x_conv[m].astype(F32), axis=0, keepdims=True)
-            grown = spread(jnp.exp(cols[m][:, :8]))
-            scaled = grown * dy
+            scaled = spread(jnp.exp(cols[m][:, :8])) * dy
             dye = scaled.astype(BF16)
-            d_c[...] += dot(dye, state[m])
             local[m] = dot(dye, c_mat, (0, 0)).astype(BF16)
             pl.when(m != block)(lambda m=m: to_owner_back(m).start())
+            d_c[...] += dot(dye, state[m])
             d_cols[m] = jnp.concatenate([gathered_heads(scaled * dot(c_mat, state[m], (1, 1))), jnp.zeros((ROWS, 8), F32)], axis=1)
 
     pairs(o_flat, 0, 4, gate_back)
@@ -598,7 +597,6 @@
     out(out_in, out_in_out)
     out(d_z, d_z_out)
     out(gain_part, gain_part_out)
-    out(skip_part, skip_part_out)
 
     def d_x_copy(m):
         return pltpu.make_async_copy(zb.at[m], d_x_out.at[m], wsem.at[m])
@@ -606,6 +604,7 @@
     def inner_group(m):
         dy = yb[m]
         dyb = dy.astype(BF16)
+        dy_t = dyb.T
         xc = x_conv[m]
         d_cum = d_cols[m][:, :8]
         lane = lax.broadcasted_iota(jnp.int32, (ROWS, 8), 1)
@@ -625,28 +624,27 @@
             row = jnp.concatenate([jnp.sum(qu, axis=1, keepdims=True),
                                    jnp.sum(ql[:, top] + ql[:, low], axis=1, keepdims=True)], axis=0)
             d_cum = jnp.where(lane == h, d_cum + row, d_cum)
-            below = dot((lower * gram[low]).astype(BF16), dyh[low], (0, 0))
-            above = dot((upper * gram[top, top]).astype(BF16), dyh[top], (0, 0))
-            parts.append(jnp.concatenate([below[top] + above, below[low]], axis=0))
+            dyt = dy_t[64 * h : 64 * h + 64]
+            below = dot(dyt[:, low], (lower * gram[low]).astype(BF16))
+            above = dot(dyt[:, top], (upper * gram[top, top]).astype(BF16))
+            parts.append(jnp.concatenate([below[:, top] + above, below[:, low]], axis=1))
         sums = jnp.concatenate(sums + [jnp.zeros((2, ROWS), F32)], axis=0).T
-        zb[m] = jnp.concatenate(parts, axis=1) + spread(pk[m, 14:15, 0:8]) * dy
+        zb[m] = jnp.concatenate(parts, axis=0).T + spread(pk[m, 14:15, 0:8]) * dy
         d_x_copy(m).start()
         d_cols[m] = jnp.concatenate([d_cum - sums, sums], axis=1)
 
-    pl.loop(0, 4)(inner_group)
-    exchanged(local, es, er)
-    carry(range(BLOCKS - 1, -1, -1))
-    b_c = to_peers(rc, lambda p: out_b.at[p], d_state, fs, fr, block)
-    d_state[block] = out_b[block]
-    pl.loop(4, GROUPS)(inner_group)
+    pl.loop(0, GROUPS)(inner_group)
+    out(skip_part, skip_part_out)
     out(d_cols, d_cols_out)
     dg = jnp.where(triangle(False), d_gram[...], 0.0).astype(BF16)
     d_bc[:, :128] = dot(dg, c_mat, (0, 0))
     d_bc[:, 128:] = d_c[...] + dot(dg, bc_conv[:, :128])
     out(d_bc, d_bc_out)
-    for c in b_c + across:
+    exchanged(local, es, er)
+    carry(range(BLOCKS - 1, -1, -1))
+    out(out_b, d_state_out)
+    for c in across:
         c.wait_recv()
-    out(d_state, d_state_out)
     for c in writes:
         c.wait()
     for m in range(GROUPS):
@@ -690,7 +688,7 @@
         in_specs=[hbm, hbm, vmem, vmem, hbm] + [vmem] * 8,
         out_specs=(hbm,) * (2 + len(RESULTS) + len(SIBLING)),
         scratch_shapes=[
-            *[pltpu.VMEM(shape, dtype) for name, shape, dtype in RESULTS if name != "d_x"],
+            *[pltpu.VMEM(shape, dtype) for name, shape, dtype in RESULTS if name not in ("d_x", "d_state")],
             b(ROWS, WIDTH), b(HALO + ROWS, WIDTH), b(HALO, WIDTH), b(96, 128), b(2, 4, 2, 96, COLS),
             v(*groups), v(*groups), b(GROUPS, HEADS, HALF, HALF), b(GROUPS, HEADS, HALF, ROWS),
             b(4, 2, 2, 4, 2, 96, COLS), b(4, 2, 2, 4, 2, 96, COLS),
@@ -888,7 +886,7 @@
      bxc, bdx, bxp, bcols, bdc, d_b, d_all, parts, small2, s_xs, s_ys, s_zs,
      v_all, v_in, v_sum, v_lines, n_all, n_lines, gain) = scr[:37]
     bufs = [scr[37:40], scr[40:43], scr[43:46], scr[46]]
-    (t_s, t_r, x_s, x_r, h_s, h_r, m_s, m_r, ss, sr, vms, vmr, vs, vr, ns, nr, wsem, lsem, isem, freed) = scr[47:]
+    (t_s, t_r, e_s, e_r, x_s, x_r, h_s, h_r, m_s, m_r, ss, sr, vms, vmr, vs, vr, ns, nr, wsem, lsem, isem, freed) = scr[47:]
     rc = Sender()
     gain[0] = norm_gain[...]
     core = lax.axis_index("core")
@@ -910,7 +908,7 @@
 
     load_in("o", (cot_t_ref.at[:, core], l_c), (cot_t2_ref, l_c2), (out_in_ref, rhs_o.at[0]), (out_in2_ref, rhs_o.at[1]))
     load_in("z", (normed_t_ref.at[:, core], l_n), (normed_t2_ref, l_n2), (d_z_ref, rhs_z.at[0]), (d_z2_ref, rhs_z.at[1]))
-    load_in("s", (state_ref, state), (d_state_ref, d_state))
+    load_in("s", (state_ref, state), (d_state_ref.at[block], d_state.at[block]))
 
     outs = (lambda at: zx_out.at[at, 1], lambda at: zx_out.at[at, 0], lambda at: wo_out.at[at])
 
@@ -925,18 +923,22 @@
         return jnp.concatenate([own_t[...].reshape(768, ROWS), other_t[...].reshape(768, ROWS)], axis=1)
 
     def gradient(left, left2, rhs, slot, ready=None):
-        def one(m):
+        def one(i):
             if ready is not None:
-                ready(m)
-            v = dot(both_tokens(left, left2), jnp.concatenate([rhs[0, m], rhs[1, m]], axis=0))
-            own[slot, m // 2, lax.rem(m, 2)] = v.astype(BF16).reshape(2, 4, 96, COLS)
-
-        pl.loop(0, GROUPS)(one)
+                ready(2 * i)
+                ready(2 * i + 1)
+            right = jnp.concatenate([jnp.concatenate([rhs[0, 2 * i + k], rhs[1, 2 * i + k]], axis=0) for k in range(2)], axis=1)
+            v = dot(both_tokens(left, left2), right).astype(BF16)
+            for k in range(2):
+                own[slot, i, k] = v[:, COLS * k : COLS * k + COLS].reshape(2, 4, 96, COLS)
+
+        pl.loop(0, GROUPS // 2)(one)
 
     oc, zc, xc_ = chunks(2, 0, 0), chunks(1, 1, 1), chunks(0, 2, 0)
+    arrived()
+    back = to_peers(rc, lambda p: d_state_ref.at[p], d_state, e_s, e_r, block)
     ready("o")
     gradient(l_c, l_c2, rhs_o, 0)
-    arrived()
     steps(oc, 0)
     ready("z")
 
@@ -951,6 +953,8 @@
     gradient(l_n, l_n2, rhs_z, 1)
     steps(zc, 0)
     ready("s")
+    for c in back:
+        c.wait_recv()
     load_in("end", (w_small_ref, w_small), (hid_ref, hid), (cot_ref, cot))
 
     def fifth_group(m):
@@ -997,9 +1001,9 @@
         halo_src[m] = dp[:8]
 
     d_b[...] = jnp.zeros_like(d_b)
-    pl.loop(0, 2)(fifth_group)
+    pl.loop(0, 1)(fifth_group)
     steps(oc, 1)
-    pl.loop(2, GROUPS)(fifth_group)
+    pl.loop(1, GROUPS)(fifth_group)
 
     d_bc = jnp.concatenate([d_bc_in[:, :128] + d_b[...], d_bc_in[:, 128:]], axis=1)
     ext = bc_pre[...]
@@ -1008,8 +1012,8 @@
     dp_bc = d_bc * (sig * (1.0 + pre * (1.0 - sig)))
     halo_src[GROUPS] = jnp.concatenate([dp_bc[:8], jnp.zeros((8, 128), F32)], axis=1)
     halo = rc(halo_src, halo_dst, h_s, h_r, block_device(lax.rem(block + 7, 8)))
+    steps(oc, 2)
     steps(zc, 1)
-    steps(oc, 2)
     for a in "xyz":
         for s in (1, -1):
             pl.semaphore_signal(freed, inc=1, device_id=neighbour(a, s), device_id_type=MESHID)
@@ -1047,10 +1051,10 @@
         rhs_x[0, m, pl.ds(ROWS - 16, 16)] = (tails[m] + conv_transposed(ext, taps[m], 16)).astype(BF16)
         across(m).start()
 
-    pl.loop(0, GROUPS)(fix)
     d_bc = conv_transposed(jnp.concatenate([dp_bc, below(GROUPS)[:, :256]], axis=0), taps_bc[...])
     small2[0] = jnp.concatenate([d_bc, d_dt], axis=1).astype(BF16)
     small_c = rc(small2.at[0], small2.at[1], m_s, m_r, neighbour("core", 1))
+    pl.loop(0, GROUPS)(fix)
 
     def weights(m):
         k = lax.rem(m, 2)
@@ -1058,13 +1062,12 @@
 
     for c in weights(0):
         c.start()
+    gradient(l_n, l_n2, rhs_x, 2, lambda m: across(m).wait())
+    pl.semaphore_wait(freed, 6)
+    steps(xc_, 0)
     small_c.wait_recv()
     parts[...] = dot(both_tokens(l_n, l_n2), small2[...].reshape(2 * ROWS, COLS)).astype(BF16).reshape(2, 4, 96, COLS)
     sums = SmallSum(rc, parts, s_xs, s_ys, s_zs, ss, sr)
-    sums.step(0)
-    gradient(l_n, l_n2, rhs_x, 2, lambda m: across(m).wait())
-    pl.semaphore_wait(freed, 6)
-    steps(xc_, 0)
     ready("end")
     acc[...] = dot(small2[0], w_small[...], (1, 1))
     def input_group(m):
@@ -1081,8 +1084,11 @@
         rhs = jnp.concatenate([wbuf[k, 0], wbuf[k, 1]], axis=1)
         acc[...] += dot(lhs, rhs, (1, 1))
 
-    pl.loop(0, 4)(input_group)
-    steps(xc_, 1)
+    pl.loop(0, 2)(input_group)
+    sums.step(0)
+    steps(oc, 3)
+    steps(zc, 2)
+    pl.loop(2, 4)(input_group)
     for c in vec_c:
         c.wait_recv()
     t = v_in[0]
@@ -1091,6 +1097,7 @@
     v_sum[...] = t
     vec = Total(rc, v_sum, v_lines, ("core", "x", "ylo"), vs, vr)
     vec.step(0)
+    steps(xc_, 1)
     pl.loop(4, GROUPS)(input_group)
     v = hid[...].astype(F32)
     r = lax.rsqrt(jnp.mean(v * v, axis=1, keepdims=True) + EPS)
@@ -1104,20 +1111,19 @@
     nvec.step(0)
     sums.step(1)
     vec.step(1)
+    steps(oc, 4)
+    steps(zc, 3)
     d_in = dn * gain[...]
     grad_hidden[...] = r * (d_in - unit * jnp.mean(d_in * unit, axis=1, keepdims=True)) + cot[...].astype(F32)
     nvec.step(1)
     steps(xc_, 2)
-    steps(zc, 2)
-    steps(oc, 3)
     sums.step(2)
+    vec.step(2)
     nvec.step(2)
-    vec.step(2)
+    steps(zc, 4)
     steps(xc_, 3)
+    vec.step(3)
     nvec.step(3)
-    vec.step(3)
-    steps(zc, 3)
-    steps(oc, 4)
 
     pick = lax.broadcasted_iota(jnp.int32, (8, 128), 0) + block * HEADS
     pick = (pick == lax.broadcasted_iota(jnp.int32, (8, 128), 1)).astype(F32)
@@ -1133,7 +1139,6 @@
     log_out[...] = own_heads(mine[13:14, :128])[0, :HEADS]
     shift_out[...] = own_heads(mine[13:14, 128:256])[0, :HEADS]
     steps(xc_, 4)
-    steps(zc, 4)
     little = sums.step(3)
     wbc_out[...] = little[:, :256]
     wdt_out[...] = dot(pick, little[:, 256:], (1, 1), precision=lax.Precision.HIGHEST)[:HEADS]
@@ -1171,7 +1176,7 @@
     scratch += [buf(2, 2, 4, 2, 2, SUB), buf(2, 2, 4, 4, SUB), buf(2, 2, 2, 2, 4, SUB)]
     scratch += [buf(2, 2, 4, 2, 2, 16), buf(2, 2, 4, 4, 16), buf(2, 2, 2, 2, 4, 16)]
     scratch += [buf(3, 3, 4, SUB), buf(3, 3, 4, SUB), buf(3, 3, 2, 2, SUB), buf(9, 3, SUB)]
-    scratch += [sem((27,)), sem((90,)), sem((8,)), sem((8,)), sem, sem, sem, sem, sem((10,)), sem((10,)), sem((8,)), sem((8,)),
+    scratch += [sem((27,)), sem((90,)), sem((8,)), sem((8,)), sem((8,)), sem((8,)), sem, sem, sem, sem, sem((10,)), sem((10,)), sem((8,)), sem((8,)),
                 sem((3,)), sem((9,)), sem((3,)), sem((12,)), sem((2, 2)), sem((2, 5)), sem((13,)), pltpu.SemaphoreType.REGULAR]
     names = ("x_conv", "d_x", "x_pre", "cols", "d_cols", "cot_t", "cot_t2", "out_in", "out_in2", "normed_t", "normed_t2", "d_z",
              "d_z2", "state", "d_state")
@@ -1186,6 +1191,32 @@
         name="backward_between_devices",
     )(w_all, *[r[name] for name in names], w_small, hid, cot, r["pk"], r["d_bc"], r["bc_pre"], r["bc_conv"], conv_bc, norm_gain,
       r["steps"], r["rates"], r["gain_part"], r["skip_part"])
+def results_kernel(*refs):
+    n = (len(refs) - 2) // 3
+    sems = refs[-2:]
+    into = [pltpu.make_async_copy(refs[i], refs[2 * n + i], sems[0].at[i]) for i in range(n)]
+    back = [pltpu.make_async_copy(refs[2 * n + i], refs[n + i], sems[1].at[i]) for i in range(n)]
+    for c in into:
+        c.start()
+    for c, d in zip(into, back):
+        c.wait()
+        d.start()
+    for d in back:
+        d.wait()
+
+
+def as_results(*arrays):
+    hbm = pl.BlockSpec(memory_space=pl.ANY)
+    return pl.pallas_call(
+        results_kernel,
+        out_shape=tuple(jax.ShapeDtypeStruct(a.shape, a.dtype) for a in arrays),
+        in_specs=[hbm] * len(arrays),
+        out_specs=(hbm,) * len(arrays),
+        scratch_shapes=[*[pltpu.VMEM(a.shape, a.dtype) for a in arrays], *[pltpu.SemaphoreType.DMA((len(arrays),))] * 2],
+        name="results",
+    )(*arrays)
+
+
 def shards(hidden, grad_out, norm_gain, w_zx, w_bc, w_dt, conv_x, conv_bc, a_log, dt_bias, d_skip, gate_gain, w_out):
     w_all, w_small, r = forward(jnp.moveaxis(w_zx, 1, 0), w_out.T, w_bc, hidden, grad_out, norm_gain, w_dt.T, conv_x, conv_bc,
                                 a_log, dt_bias, d_skip, gate_gain)
@@ -1193,7 +1224,9 @@
     w_small = w_small.reshape(WIDTH, COLS)
     zx, wo, wbc, wdt, grad_taps, grad_taps_bc, log_rate, shift, skip, gate, norm, grad_hidden = backward(
         w_all, r, w_small, hidden, grad_out, norm_gain, conv_bc)
-    return (r["result"], grad_hidden, norm, zx, wbc, wdt.T, grad_taps, grad_taps_bc, log_rate, shift, skip, gate, wo.T)
+    result, grad_hidden, norm, zx, wbc, wdt, grad_taps, grad_taps_bc, log_rate, shift, skip, gate, wo = as_results(
+        r["result"], grad_hidden, norm, zx, wbc, wdt, grad_taps, grad_taps_bc, log_rate, shift, skip, gate, wo)
+    return (result, grad_hidden, norm, zx, wbc, wdt.T, grad_taps, grad_taps_bc, log_rate, shift, skip, gate, wo.T)
 
 
 def solution(mesh):

time: 231 us -> 219 us (0.948)
  local copies, waits for them, and re-layouts: 11 us -> 1.59 us
    pallas_call x1, Pallas kernels: 133 us -> 122 us  [forward(): pl.pallas_call(forward_kernel, out_shape=(sds(2, 4, 2, 2, 4, 2, 96, COLS,...]
    unnamed x40 -> x1, local copies, waits for them, and re-layouts: 11 us -> 1.59 us
    pallas_call x1, Pallas kernels: 85.9 us -> 91.3 us  [backward(): pl.pallas_call(backward_kernel, out_shape=(sds(96, 2, COLS), sds(96, COLS...]
    pallas_call x0 -> x1, Pallas kernels: none -> 3.23 us  [as_results(): pl.pallas_call(results_kernel, out_shape=tuple((jax.ShapeDtypeStruct(a.sh...]
where the time goes in v5:
time: 219 us
  Pallas kernels  217 us (99%)
    pallas_call x1, Pallas kernels, forward(): pl.pallas_call(forward_kernel, out_shape=(sds(2, 4, 2, 2, 4, 2, 96, COLS,...  122 us
    pallas_call x1, Pallas kernels, backward(): pl.pallas_call(backward_kernel, out_shape=(sds(96, 2, COLS), sds(96, COLS...  91.3 us

profile of v5, /device:TPU:0, one launch (start us, length us, event | category | flops | bytes accessed | tf_op | source)
XLA Modules:
  0.0 219.1 jit_solution(4736944589072383347)
XLA Ops:
  0.6 1.6 copy.28
  2.2 122.1 %forward_between_devices.1 = (bf16[2,4,2,2,4,2,96,384]{7,6,5,4,3,2,1,0:T(8,128)(2,1)}, bf16[2,4,2,96,384]{4,3,2,1,0:T(8,128)(2,1)}, f32[8,16,384]{2,1,0:T(8,128)...) custom-call(bf16[2,96,384]{2,1,0:T(8,128)(2,1)} %bitcast.11, ...), custom_call_target="tpu_custom_call" | custom-call | tf_op jit(solution)/shard_map/forward_between_devices/pallas_call | solution.py:684
  124.4 91.3 %backward_between_devices.1 = (f32[96,2,384]{2,1,0:T(2,128)}, f32[96,384]{1,0:T(8,128)}, f32[96,256]{1,0:T(8,128)}, f32[6,96]{1,0:T(8,128)}, f32[5,384]{1,0:T(8,...) custom-call(bf16[2,8,1536,384]{3,2,1,0:T(8,128)(2,1)} %bitcast.9, ...), custom_call_target="tpu_custom_call" | custom-call | tf_op jit(solution)/shard_map/backward_between_devices/pallas_call | solution.py:1183
  215.7 3.2 %results.1 = (bf16[256,1536]{1,0:T(8,128)(2,1)}, f32[256,1536]{1,0:T(8,128)}, f32[1536]{0:T(1024)}, f32[96,2,384]{2,1,0:T(2,128)}, f32[96,256]{1,0:T(8,128)}, /*...) custom-call(bf16[256,1536]{1,0:T(8,128)(2,1)} %get-tuple-element.64., ...), custom_call_target="tpu_custom_call" | custom-call | tf_op jit(solution)/shard_map/results/pallas_call | solution.py:1210

commit v6 on v5

--- a/solution.py
+++ b/solution.py
@@ -162,7 +162,7 @@
     return out
 
 
-PIECES = (((0, 32), (32, 32), (64, 32)),) * 3
+PIECES = (((0, 32), (32, 32), (64, 32)), ((0, 16), (16, 48), (64, 32)), ((0, 32), (32, 32), (64, 32)))
 
 
 class Gather:
@@ -248,12 +248,12 @@
                    gate_ref, g_ref, gb_ref,
                    pk_out, x_pre_out, x_conv_out, d_x_out, normed_t_out, cot_t_out, state_out, bc_pre_out, bc_conv_out,
                    steps_out, rates_out, cols_out, cum_row_out, step_row_out, dec_out, result_out,
-                   out_in_out, d_z_out, gain_part_out, skip_part_out, d_cols_out, d_bc_out, d_state_out,
+                   out_in_out, d_z_out, gain_part_out, skip_part_out, d_cols_out, d_bc_out, conv_slope_out, d_state_out,
                    normed_t2_out, cot_t2_out, out_in2_out, d_z2_out, *scr):
     (pk, x_pre, x_conv, normed_t, cot_t, state, bc_pre, bc_conv, steps, rates, cols, cum_row, step_row, dec,
-     result, out_in, d_z, gain_part, skip_part, d_cols, d_bc,
+     result, out_in, d_z, gain_part, skip_part, d_cols, d_bc, conv_slope,
      cot, normed, halo, dt_own, small_all, zb, yb, uppers, lowers, wx, wo, gram, d_gram, local, rec_a, out_b, dec_own, square,
-     scales, acc, d_c, pk_ref, gain,
+     scales, acc, d_c, pk_ref, gain, zx,
      ts, tr, cs, cr, bs, br, qs, qr, es, er, fs, fr, ds, dr, hs, hr, lsem, wsem, osem, xs, xr) = scr
     rc = Sender()
     me = my_place()
@@ -274,8 +274,11 @@
     def spot(ref):
         return ref.at[me["z"], me["y"] // 2, ylo, x, core]
 
+    split = zx_ref[...].astype(F32)
+    for i in range(2):
+        zx[i] = split[:, i, :].astype(BF16)
     own_w = [pltpu.make_async_copy(src, spot(dst), lsem.at[4 + i])
-             for i, (src, dst) in enumerate(((zx_ref.at[1], wx), (zx_ref.at[0], g_ref.at[1]), (wo_ref, wo)))]
+             for i, (src, dst) in enumerate(((zx.at[1], wx), (zx.at[0], g_ref.at[1]), (wo_ref, wo)))]
     for c in own_w:
         c.start()
     pk_ref[...] = jnp.zeros_like(pk_ref)
@@ -288,7 +291,7 @@
     arrived()
 
     gx, gz, go = [[Gather(rc, g, w, (ts, tr, cs, cr), i, r) for r in range(3)]
-                  for i, (g, w) in enumerate(((wx, zx_ref.at[1]), (g_ref.at[1], zx_ref.at[0]), (wo, wo_ref)))]
+                  for i, (g, w) in enumerate(((wx, zx.at[1]), (g_ref.at[1], zx.at[0]), (wo, wo_ref)))]
 
     def each(group, name, *args):
         for c in group:
@@ -345,7 +348,9 @@
     for c in own_w:
         c.wait()
     each(gx, "straight", 1)
+    each(gz, "straight", 0)
     halo_c = rc(hid.at[pl.ds(ROWS - HALO, HALO)], halo, hs, hr, block_device(lax.rem(block + 1, 8)))
+    each(go, "straight", 0)
 
     for c in pk_c:
         c.wait_recv()
@@ -359,8 +364,6 @@
     each(gx, "near")
     bc_s = bc_x(*bc_s)
     dt_s = dt_x(*dt_s)
-    each(gz, "straight", 0)
-    each(go, "straight", 0)
     cot_c.wait()
     cot_t[...] = cot[...].T.reshape(8, 2, 96, ROWS)
     out(cot_t, cot_t_out)
@@ -401,6 +404,8 @@
     cum = dot(triangle(False).astype(F32), decay, precision=lax.Precision.HIGHEST)
     cum_t = cum.T
     step_t = step.T
+    each(gz, "line", 1)
+    each(gz, "near")
     lasts = jnp.broadcast_to(jnp.exp(cum_t[:, ROWS - 1 : ROWS]), (128, 128))
     for m in range(GROUPS):
         at = slice(HEADS * m, HEADS * m + 8)
@@ -419,8 +424,6 @@
     out(cum_row, cum_row_out)
     out(step_row, step_row_out)
     each(gx, "last")
-    each(gz, "line", 1)
-    each(gz, "near")
     each(gx, "complete")
 
     x_flat, o_flat = wx.reshape(GROUPS, WIDTH, COLS), wo.reshape(GROUPS, WIDTH, COLS)
@@ -509,6 +512,14 @@
     carry(range(BLOCKS))
     f_c = to_peers(rc, lambda p: out_b.at[p], state, fs, fr, block)
     state[block] = out_b[block]
+
+    @pl.loop(0, GROUPS)
+    def _(m):
+        pre = conv_pre(x_pre[m], pk[m])
+        sig = jax.nn.sigmoid(pre)
+        conv_slope[m] = (sig * (1.0 + pre * (1.0 - sig))).astype(BF16)
+
+    out(conv_slope, conv_slope_out)
     each(gz, "last")
     each(gz, "complete")
     x_written.wait()
@@ -661,7 +672,7 @@
     ("cum_row", (GROUPS, 8, ROWS), F32), ("step_row", (GROUPS, 8, ROWS), F32), ("dec", (BLOCKS, 8, 128), F32),
     ("result", (ROWS, WIDTH), BF16), ("out_in", (GROUPS, ROWS, COLS), BF16), ("d_z", (GROUPS, ROWS, COLS), BF16),
     ("gain_part", (GROUPS, 1, COLS), F32), ("skip_part", (GROUPS, 1, COLS), F32), ("d_cols", (GROUPS, ROWS, 16), F32),
-    ("d_bc", (ROWS, 256), F32), ("d_state", (GROUPS, COLS, 128), BF16),
+    ("d_bc", (ROWS, 256), F32), ("conv_slope", (GROUPS, ROWS, COLS), BF16), ("d_state", (GROUPS, COLS, 128), BF16),
 )
 SIBLING = (
     ("normed_t2", (8, 96, ROWS), BF16), ("cot_t2", (8, 96, ROWS), BF16), ("out_in2", (GROUPS, ROWS, COLS), BF16),
@@ -685,7 +696,7 @@
         forward_kernel,
         out_shape=(sds(2, 4, 2, 2, 4, 2, 96, COLS, dtype=BF16), sds(2, 4, 2, 96, COLS, dtype=BF16),
                    *[sds(*shape, dtype=dtype) for _, shape, dtype in RESULTS + SIBLING]),
-        in_specs=[hbm, hbm, vmem, vmem, hbm] + [vmem] * 8,
+        in_specs=[vmem, hbm, vmem, vmem, hbm] + [vmem] * 8,
         out_specs=(hbm,) * (2 + len(RESULTS) + len(SIBLING)),
         scratch_shapes=[
             *[pltpu.VMEM(shape, dtype) for name, shape, dtype in RESULTS if name not in ("d_x", "d_state")],
@@ -694,7 +705,7 @@
             b(4, 2, 2, 4, 2, 96, COLS), b(4, 2, 2, 4, 2, 96, COLS),
             v(ROWS, ROWS), v(ROWS, ROWS),
             b(GROUPS, COLS, 128), b(GROUPS, COLS, 128), b(GROUPS, COLS, 128), v(GROUPS, 8, 128),
-            v(ROWS, 128), v(ROWS, 8), v(ROWS, WIDTH), v(ROWS, 128), v(16, COLS), v(1, WIDTH),
+            v(ROWS, 128), v(ROWS, 8), v(ROWS, WIDTH), v(ROWS, 128), v(16, COLS), v(1, WIDTH), b(2, 96, COLS),
             sem((27,)), sem((90,)), sem((36,)), sem((36,)), sem((18,)), sem((18,)), sem((8,)), sem((8,)), sem((8,)), sem((8,)),
             sem((8,)), sem((8,)), sem((8,)), sem((8,)), sem, sem, sem((7,)), sem((GROUPS,)), sem((len(RESULTS),)), sem((4,)),
             sem((4,)),
@@ -877,16 +888,16 @@
                 self.out(pl.ds(self.r * SUB, SUB))[...] = total(())
 
 
-def backward_kernel(g_ref, x_conv_ref, d_x_ref, x_pre_ref, cols_ref, d_cols_ref, cot_t_ref, cot_t2_ref, out_in_ref, out_in2_ref,
+def backward_kernel(g_ref, x_conv_ref, d_x_ref, x_pre_ref, cols_ref, d_cols_ref, slope_ref, cot_t_ref, cot_t2_ref, out_in_ref, out_in2_ref,
                     normed_t_ref, normed_t2_ref, d_z_ref, d_z2_ref, state_ref, d_state_ref, w_small_ref, hid_ref, cot_ref,
                     taps, d_bc_in, bc_pre, bc_conv, taps_bc, norm_gain, shifted, rates, gain_part, skip_part,
                     zx_out, wo_out, wbc_out, wdt_out, taps_out, taps_bc_out, log_out, shift_out, skip_out, gate_out, norm_out,
                     grad_hidden, *scr):
     (own, l_c, l_c2, l_n, l_n2, rhs_o, rhs_z, rhs_x, state, d_state, w_small, hid, cot, tails, halo_src, halo_dst, acc, wbuf,
-     bxc, bdx, bxp, bcols, bdc, d_b, d_all, parts, small2, s_xs, s_ys, s_zs,
-     v_all, v_in, v_sum, v_lines, n_all, n_lines, gain) = scr[:37]
-    bufs = [scr[37:40], scr[40:43], scr[43:46], scr[46]]
-    (t_s, t_r, e_s, e_r, x_s, x_r, h_s, h_r, m_s, m_r, ss, sr, vms, vmr, vs, vr, ns, nr, wsem, lsem, isem, freed) = scr[47:]
+     bxc, bdx, bxp, bcols, bdc, bslope, d_b, d_all, parts, small2, s_xs, s_ys, s_zs,
+     v_all, v_in, v_sum, v_lines, n_all, n_lines, gain) = scr[:38]
+    bufs = [scr[38:41], scr[41:44], scr[44:47], scr[47]]
+    (t_s, t_r, e_s, e_r, x_s, x_r, h_s, h_r, m_s, m_r, ss, sr, vms, vmr, vs, vr, ns, nr, wsem, lsem, isem, freed) = scr[48:]
     rc = Sender()
     gain[0] = norm_gain[...]
     core = lax.axis_index("core")
@@ -942,7 +953,7 @@
     steps(oc, 0)
     ready("z")
 
-    streams = ((x_conv_ref, bxc), (d_x_ref, bdx), (x_pre_ref, bxp), (cols_ref, bcols), (d_cols_ref, bdc))
+    streams = ((x_conv_ref, bxc), (d_x_ref, bdx), (x_pre_ref, bxp), (cols_ref, bcols), (d_cols_ref, bdc), (slope_ref, bslope))
 
     def load(m):
         k = lax.rem(m, 2)
@@ -991,9 +1002,7 @@
         d_all[m] = jnp.concatenate([d_cum, bdc[k][:, 8:] + both], axis=1)
         ext = bxp[k]
         tap = taps[m]
-        pre = conv_pre(ext, tap)
-        sig = jax.nn.sigmoid(pre)
-        dp = dx * (sig * (1.0 + pre * (1.0 - sig)))
+        dp = dx * bslope[k].astype(F32)
         v_all[m, 0:8] = conv_grads(dp, ext, gain_part[m], skip_part[m])
         whole_dx = conv_transposed(jnp.concatenate([dp, jnp.zeros((8, COLS), F32)], axis=0), tap)
         rhs_x[0, m] = whole_dx.astype(BF16)
@@ -1001,9 +1010,9 @@
         halo_src[m] = dp[:8]
 
     d_b[...] = jnp.zeros_like(d_b)
-    pl.loop(0, 1)(fifth_group)
+    pl.loop(0, 3)(fifth_group)
     steps(oc, 1)
-    pl.loop(1, GROUPS)(fifth_group)
+    pl.loop(3, GROUPS)(fifth_group)
 
     d_bc = jnp.concatenate([d_bc_in[:, :128] + d_b[...], d_bc_in[:, 128:]], axis=1)
     ext = bc_pre[...]
@@ -1012,11 +1021,7 @@
     dp_bc = d_bc * (sig * (1.0 + pre * (1.0 - sig)))
     halo_src[GROUPS] = jnp.concatenate([dp_bc[:8], jnp.zeros((8, 128), F32)], axis=1)
     halo = rc(halo_src, halo_dst, h_s, h_r, block_device(lax.rem(block + 7, 8)))
-    steps(oc, 2)
     steps(zc, 1)
-    for a in "xyz":
-        for s in (1, -1):
-            pl.semaphore_signal(freed, inc=1, device_id=neighbour(a, s), device_id_type=MESHID)
     zero8 = jnp.zeros((1, 256), F32)
     d_cum = jnp.concatenate([d_all[m][:, :HEADS] for m in range(GROUPS)] + [jnp.zeros((ROWS, 80), F32)], axis=1)
     d_step = jnp.concatenate([d_all[m][:, 8 : 8 + HEADS] for m in range(GROUPS)] + [jnp.zeros((ROWS, 80), F32)], axis=1)
@@ -1062,6 +1067,10 @@
 
     for c in weights(0):
         c.start()
+    steps(oc, 2)
+    for a in "xyz":
+        for s in (1, -1):
+            pl.semaphore_signal(freed, inc=1, device_id=neighbour(a, s), device_id_type=MESHID)
     gradient(l_n, l_n2, rhs_x, 2, lambda m: across(m).wait())
     pl.semaphore_wait(freed, 6)
     steps(xc_, 0)
@@ -1086,9 +1095,8 @@
 
     pl.loop(0, 2)(input_group)
     sums.step(0)
-    steps(oc, 3)
+    pl.loop(2, 4)(input_group)
     steps(zc, 2)
-    pl.loop(2, 4)(input_group)
     for c in vec_c:
         c.wait_recv()
     t = v_in[0]
@@ -1099,6 +1107,7 @@
     vec.step(0)
     steps(xc_, 1)
     pl.loop(4, GROUPS)(input_group)
+    steps(oc, 3)
     v = hid[...].astype(F32)
     r = lax.rsqrt(jnp.mean(v * v, axis=1, keepdims=True) + EPS)
     unit = v * r
@@ -1111,7 +1120,6 @@
     nvec.step(0)
     sums.step(1)
     vec.step(1)
-    steps(oc, 4)
     steps(zc, 3)
     d_in = dn * gain[...]
     grad_hidden[...] = r * (d_in - unit * jnp.mean(d_in * unit, axis=1, keepdims=True)) + cot[...].astype(F32)
@@ -1120,6 +1128,7 @@
     sums.step(2)
     vec.step(2)
     nvec.step(2)
+    steps(oc, 4)
     steps(zc, 4)
     steps(xc_, 3)
     vec.step(3)
@@ -1169,6 +1178,7 @@
         buf(GROUPS, 16, dtype=F32), buf(GROUPS + 1, 8, dtype=F32), buf(GROUPS + 1, 8, dtype=F32),
         v(ROWS, WIDTH), buf(2, 2, WIDTH),
         buf(2, ROWS), buf(2, ROWS, dtype=F32), buf(2, HALO + ROWS, dtype=F32), v(2, ROWS, 16), v(2, ROWS, 16),
+        buf(2, ROWS),
         v(ROWS, 128), v(GROUPS, ROWS, 16), buf(2, 4, 96), buf(2, ROWS), buf(3, 2, 96), buf(4, 96), buf(4, 96),
     ]
     scratch += [buf(GROUPS, 16, dtype=F32), buf(GROUPS, 16, dtype=F32), buf(16, dtype=F32), buf(3, 4, 16, dtype=F32)]
@@ -1177,14 +1187,14 @@
     scratch += [buf(2, 2, 4, 2, 2, 16), buf(2, 2, 4, 4, 16), buf(2, 2, 2, 2, 4, 16)]
     scratch += [buf(3, 3, 4, SUB), buf(3, 3, 4, SUB), buf(3, 3, 2, 2, SUB), buf(9, 3, SUB)]
     scratch += [sem((27,)), sem((90,)), sem((8,)), sem((8,)), sem((8,)), sem((8,)), sem, sem, sem, sem, sem((10,)), sem((10,)), sem((8,)), sem((8,)),
-                sem((3,)), sem((9,)), sem((3,)), sem((12,)), sem((2, 2)), sem((2, 5)), sem((13,)), pltpu.SemaphoreType.REGULAR]
-    names = ("x_conv", "d_x", "x_pre", "cols", "d_cols", "cot_t", "cot_t2", "out_in", "out_in2", "normed_t", "normed_t2", "d_z",
+                sem((3,)), sem((9,)), sem((3,)), sem((12,)), sem((2, 2)), sem((2, 6)), sem((13,)), pltpu.SemaphoreType.REGULAR]
+    names = ("x_conv", "d_x", "x_pre", "cols", "d_cols", "conv_slope", "cot_t", "cot_t2", "out_in", "out_in2", "normed_t", "normed_t2", "d_z",
              "d_z2", "state", "d_state")
     return pl.pallas_call(
         backward_kernel,
         out_shape=(sds(96, 2, COLS), sds(96, COLS), sds(96, 256), sds(HEADS, 96), sds(5, COLS), sds(5, 256), sds(HEADS), sds(HEADS),
                    sds(HEADS), sds(COLS), sds(WIDTH), sds(ROWS, WIDTH)),
-        in_specs=[hbm] * 19 + [vmem] * 10,
+        in_specs=[hbm] * 20 + [vmem] * 10,
         out_specs=(vmem,) * 12,
         scratch_shapes=scratch,
         compiler_params=pltpu.CompilerParams(collective_id=1, has_side_effects=True, vmem_limit_bytes=63 * 2**20),
@@ -1218,7 +1228,7 @@
 
 
 def shards(hidden, grad_out, norm_gain, w_zx, w_bc, w_dt, conv_x, conv_bc, a_log, dt_bias, d_skip, gate_gain, w_out):
-    w_all, w_small, r = forward(jnp.moveaxis(w_zx, 1, 0), w_out.T, w_bc, hidden, grad_out, norm_gain, w_dt.T, conv_x, conv_bc,
+    w_all, w_small, r = forward(w_zx, w_out.T, w_bc, hidden, grad_out, norm_gain, w_dt.T, conv_x, conv_bc,
                                 a_log, dt_bias, d_skip, gate_gain)
     w_all = w_all.reshape(2, GROUPS, WIDTH, COLS)
     w_small = w_small.reshape(WIDTH, COLS)

time: 219 us -> 211 us (0.963)
  Pallas kernels: 217 us -> 210 us
    pallas_call x1, Pallas kernels: 91.3 us -> 87.3 us  [backward(): pl.pallas_call(backward_kernel, out_shape=(sds(96, 2, COLS), sds(96, COLS...]
    pallas_call x1, Pallas kernels: 122 us -> 119 us  [forward(): pl.pallas_call(forward_kernel, out_shape=(sds(2, 4, 2, 2, 4, 2, 96, COLS,...]
where the time goes in v6:
time: 211 us; the launch traced here: 210 us
  Pallas kernels  210 us (100%)
    pallas_call x1, Pallas kernels, forward(): pl.pallas_call(forward_kernel, out_shape=(sds(2, 4, 2, 2, 4, 2, 96, COLS,...  119 us
    pallas_call x1, Pallas kernels, backward(): pl.pallas_call(backward_kernel, out_shape=(sds(96, 2, COLS), sds(96, COLS...  87.3 us

profile of v6, /device:TPU:0, one launch (start us, length us, event | category | flops | bytes accessed | tf_op | source)
XLA Modules:
  0.0 210.4 jit_solution(1451107830588120478)
XLA Ops:
  0.6 119.1 %forward_between_devices.1 = (bf16[2,4,2,2,4,2,96,384]{7,6,5,4,3,2,1,0:T(8,128)(2,1)}, bf16[2,4,2,96,384]{4,3,2,1,0:T(8,128)(2,1)}, f32[8,16,384]{2,1,0:T(8,128)...) custom-call(bf16[96,2,384]{2,1,0:T(2,128)(2,1)} %zx_ref.1, ...), custom_call_target="tpu_custom_call" | custom-call | tf_op jit(solution)/shard_map/forward_between_devices/pallas_call | solution.py:695
  119.8 87.3 %backward_between_devices.1 = (f32[96,2,384]{2,1,0:T(2,128)}, f32[96,384]{1,0:T(8,128)}, f32[96,256]{1,0:T(8,128)}, f32[6,96]{1,0:T(8,128)}, f32[5,384]{1,0:T(8,...) custom-call(bf16[2,8,1536,384]{3,2,1,0:T(8,128)(2,1)} %bitcast.6, ...), custom_call_target="tpu_custom_call" | custom-call | tf_op jit(solution)/shard_map/backward_between_devices/pallas_call | solution.py:1193
  207.0 3.2 %results.1 = (bf16[256,1536]{1,0:T(8,128)(2,1)}, f32[256,1536]{1,0:T(8,128)}, f32[1536]{0:T(1024)}, f32[96,2,384]{2,1,0:T(2,128)}, f32[96,256]{1,0:T(8,128)}, /*...) custom-call(bf16[256,1536]{1,0:T(8,128)(2,1)} %get-tuple-element.65., ...), custom_call_target="tpu_custom_call" | custom-call | tf_op jit(solution)/shard_map/results/pallas_call | solution.py:1220

commit v7 on v6

--- a/solution.py
+++ b/solution.py
@@ -248,12 +248,12 @@
                    gate_ref, g_ref, gb_ref,
                    pk_out, x_pre_out, x_conv_out, d_x_out, normed_t_out, cot_t_out, state_out, bc_pre_out, bc_conv_out,
                    steps_out, rates_out, cols_out, cum_row_out, step_row_out, dec_out, result_out,
-                   out_in_out, d_z_out, gain_part_out, skip_part_out, d_cols_out, d_bc_out, conv_slope_out, d_state_out,
+                   out_in_out, d_z_out, gain_part_out, skip_part_out, d_cols_out, d_bc_out, conv_slope_out, leaving_out, d_state_out,
                    normed_t2_out, cot_t2_out, out_in2_out, d_z2_out, *scr):
     (pk, x_pre, x_conv, normed_t, cot_t, state, bc_pre, bc_conv, steps, rates, cols, cum_row, step_row, dec,
-     result, out_in, d_z, gain_part, skip_part, d_cols, d_bc, conv_slope,
+     result, out_in, d_z, gain_part, skip_part, d_cols, d_bc, conv_slope, leaving,
      cot, normed, halo, dt_own, small_all, zb, yb, uppers, lowers, wx, wo, gram, d_gram, local, rec_a, out_b, dec_own, square,
-     scales, acc, d_c, pk_ref, gain, zx,
+     scales, acc, d_c, pk_ref, gain, zx, grown, entered,
      ts, tr, cs, cr, bs, br, qs, qr, es, er, fs, fr, ds, dr, hs, hr, lsem, wsem, osem, xs, xr) = scr
     rc = Sender()
     me = my_place()
@@ -404,6 +404,7 @@
     cum = dot(triangle(False).astype(F32), decay, precision=lax.Precision.HIGHEST)
     cum_t = cum.T
     step_t = step.T
+    each(gx, "last")
     each(gz, "line", 1)
     each(gz, "near")
     lasts = jnp.broadcast_to(jnp.exp(cum_t[:, ROWS - 1 : ROWS]), (128, 128))
@@ -423,7 +424,6 @@
     out(cols, cols_out)
     out(cum_row, cum_row_out)
     out(step_row, step_row_out)
-    each(gx, "last")
     each(gx, "complete")
 
     x_flat, o_flat = wx.reshape(GROUPS, WIDTH, COLS), wo.reshape(GROUPS, WIDTH, COLS)
@@ -457,7 +457,9 @@
             xc = (pre * jax.nn.sigmoid(pre)).astype(BF16)
             x_conv[m] = xc
             cum, step = cols[m][:, :8], cols[m][:, 8:]
-            weighted = (xc.astype(F32) * spread(step * jnp.exp(cum[ROWS - 1 : ROWS] - cum))).astype(BF16)
+            wide = spread(step * jnp.exp(cum[ROWS - 1 : ROWS] - cum))
+            leaving[m] = wide.astype(BF16)
+            weighted = (xc.astype(F32) * wide).astype(BF16)
             local[m] = dot(weighted, bc_conv[:, :128], (0, 0)).astype(BF16)
             pl.when(m != block)(lambda m=m: to_owner(m).start())
 
@@ -466,6 +468,7 @@
     rec_a[block] = local[block]
     out(x_pre, x_pre_out)
     out(x_conv, x_conv_out)
+    out(leaving, leaving_out)
 
     top, low = slice(0, HALF), slice(HALF, ROWS)
 
@@ -530,7 +533,10 @@
     def gate_pair(i, w):
         z = dot(normed[HALO:, :], w)
         for k in range(2):
-            zb[2 * i + k] = z[:, COLS * k : COLS * k + COLS]
+            part = z[:, COLS * k : COLS * k + COLS]
+            sig = jax.nn.sigmoid(part)
+            zb[2 * i + k] = part * sig
+            d_z[2 * i + k] = (sig * (1.0 + part * (1.0 - sig))).astype(BF16)
 
     pairs(x_flat, 0, 4, gate_pair, z_copy)
     each(go, "pass_on")
@@ -543,18 +549,18 @@
 
     @pl.loop(0, GROUPS)
     def _(m):
-        carried = dot(c_mat, state[m], (1, 1))
-        y = yb[m] + spread(jnp.exp(cols[m][:, :8])) * carried
-        z = zb[m]
-        sig = jax.nn.sigmoid(z)
-        act = z * sig
-        gated = y * act
+        wide = spread(jnp.exp(cols[m][:, :8]))
+        carried = wide * dot(c_mat, state[m], (1, 1))
+        grown[m] = wide
+        entered[m] = carried
+        y = yb[m] + carried
+        gated = y * zb[m]
         yb[m] = gated
-        zb[m] = act
-        d_z[m] = (y * sig * (1.0 + z * (1.0 - sig))).astype(BF16)
+        d_z[m] = (y * d_z[m].astype(F32)).astype(BF16)
         sq = gated * gated
         square[...] += sq[:, :128] + sq[:, 128:256] + sq[:, 256:]
 
+    each(go, "last")
     r2 = lax.rsqrt(jnp.sum(square[...], axis=1, keepdims=True) / INNER + EPS)
 
     @pl.loop(0, GROUPS)
@@ -564,7 +570,6 @@
     acc[...] = jnp.zeros_like(acc)
     d_c[...] = jnp.zeros_like(d_c)
     d_gram[...] = jnp.zeros_like(d_gram)
-    each(go, "last")
     each(go, "complete")
 
     def result_pair(i, w):
@@ -593,12 +598,11 @@
             d_z[m] = (d_gated * d_z[m].astype(F32)).astype(BF16)
             yb[m] = dy
             skip_part[m] = jnp.sum(dy * x_conv[m].astype(F32), axis=0, keepdims=True)
-            scaled = spread(jnp.exp(cols[m][:, :8])) * dy
-            dye = scaled.astype(BF16)
+            dye = (grown[m] * dy).astype(BF16)
             local[m] = dot(dye, c_mat, (0, 0)).astype(BF16)
             pl.when(m != block)(lambda m=m: to_owner_back(m).start())
             d_c[...] += dot(dye, state[m])
-            d_cols[m] = jnp.concatenate([gathered_heads(scaled * dot(c_mat, state[m], (1, 1))), jnp.zeros((ROWS, 8), F32)], axis=1)
+            d_cols[m] = jnp.concatenate([gathered_heads(dy * entered[m]), jnp.zeros((ROWS, 8), F32)], axis=1)
 
     pairs(o_flat, 0, 4, gate_back)
     rec_a[block] = local[block]
@@ -672,7 +676,8 @@
     ("cum_row", (GROUPS, 8, ROWS), F32), ("step_row", (GROUPS, 8, ROWS), F32), ("dec", (BLOCKS, 8, 128), F32),
     ("result", (ROWS, WIDTH), BF16), ("out_in", (GROUPS, ROWS, COLS), BF16), ("d_z", (GROUPS, ROWS, COLS), BF16),
     ("gain_part", (GROUPS, 1, COLS), F32), ("skip_part", (GROUPS, 1, COLS), F32), ("d_cols", (GROUPS, ROWS, 16), F32),
-    ("d_bc", (ROWS, 256), F32), ("conv_slope", (GROUPS, ROWS, COLS), BF16), ("d_state", (GROUPS, COLS, 128), BF16),
+    ("d_bc", (ROWS, 256), F32), ("conv_slope", (GROUPS, ROWS, COLS), BF16), ("leaving", (GROUPS, ROWS, COLS), BF16),
+    ("d_state", (GROUPS, COLS, 128), BF16),
 )
 SIBLING = (
     ("normed_t2", (8, 96, ROWS), BF16), ("cot_t2", (8, 96, ROWS), BF16), ("out_in2", (GROUPS, ROWS, COLS), BF16),
@@ -705,12 +710,12 @@
             b(4, 2, 2, 4, 2, 96, COLS), b(4, 2, 2, 4, 2, 96, COLS),
             v(ROWS, ROWS), v(ROWS, ROWS),
             b(GROUPS, COLS, 128), b(GROUPS, COLS, 128), b(GROUPS, COLS, 128), v(GROUPS, 8, 128),
-            v(ROWS, 128), v(ROWS, 8), v(ROWS, WIDTH), v(ROWS, 128), v(16, COLS), v(1, WIDTH), b(2, 96, COLS),
+            v(ROWS, 128), v(ROWS, 8), v(ROWS, WIDTH), v(ROWS, 128), v(16, COLS), v(1, WIDTH), b(2, 96, COLS), v(*groups), v(*groups),
             sem((27,)), sem((90,)), sem((36,)), sem((36,)), sem((18,)), sem((18,)), sem((8,)), sem((8,)), sem((8,)), sem((8,)),
             sem((8,)), sem((8,)), sem((8,)), sem((8,)), sem, sem, sem((7,)), sem((GROUPS,)), sem((len(RESULTS),)), sem((4,)),
             sem((4,)),
         ],
-        compiler_params=pltpu.CompilerParams(collective_id=0, has_side_effects=True, vmem_limit_bytes=62 * 2**20),
+        compiler_params=pltpu.CompilerParams(collective_id=0, has_side_effects=True, vmem_limit_bytes=63 * 2**20),
         name="forward_between_devices",
     )(zx, wo, bc, hid, cot, *params)
     return outs[0], outs[1], dict(zip([name for name, _, _ in RESULTS + SIBLING], outs[2:]))
@@ -888,16 +893,16 @@
                 self.out(pl.ds(self.r * SUB, SUB))[...] = total(())
 
 
-def backward_kernel(g_ref, x_conv_ref, d_x_ref, x_pre_ref, cols_ref, d_cols_ref, slope_ref, cot_t_ref, cot_t2_ref, out_in_ref, out_in2_ref,
+def backward_kernel(g_ref, x_conv_ref, d_x_ref, x_pre_ref, cols_ref, d_cols_ref, slope_ref, leaving_ref, cot_t_ref, cot_t2_ref, out_in_ref, out_in2_ref,
                     normed_t_ref, normed_t2_ref, d_z_ref, d_z2_ref, state_ref, d_state_ref, w_small_ref, hid_ref, cot_ref,
                     taps, d_bc_in, bc_pre, bc_conv, taps_bc, norm_gain, shifted, rates, gain_part, skip_part,
                     zx_out, wo_out, wbc_out, wdt_out, taps_out, taps_bc_out, log_out, shift_out, skip_out, gate_out, norm_out,
                     grad_hidden, *scr):
-    (own, l_c, l_c2, l_n, l_n2, rhs_o, rhs_z, rhs_x, state, d_state, w_small, hid, cot, tails, halo_src, halo_dst, acc, wbuf,
-     bxc, bdx, bxp, bcols, bdc, bslope, d_b, d_all, parts, small2, s_xs, s_ys, s_zs,
-     v_all, v_in, v_sum, v_lines, n_all, n_lines, gain) = scr[:38]
-    bufs = [scr[38:41], scr[41:44], scr[44:47], scr[47]]
-    (t_s, t_r, e_s, e_r, x_s, x_r, h_s, h_r, m_s, m_r, ss, sr, vms, vmr, vs, vr, ns, nr, wsem, lsem, isem, freed) = scr[48:]
+    (own, l_c, l_c2, l_n, l_n2, rhs_o, rhs_z, rhs_x, state, d_state, w_small, hid, cot, tails, halo_src, halo_dst, halo_x, halo_x_in, halo_bc, halo_bc_in, acc, wbuf,
+     bxc, bdx, bxp, bcols, bdc, bslope, bleave, d_b, d_all, parts, small2, s_xs, s_ys, s_zs,
+     v_all, v_in, v_sum, v_lines, n_all, n_lines, gain) = scr[:43]
+    bufs = [scr[43:46], scr[46:49], scr[49:52], scr[52]]
+    (t_s, t_r, e_s, e_r, x_s, x_r, h_s, h_r, m_s, m_r, ss, sr, vms, vmr, vs, vr, ns, nr, wsem, lsem, isem, freed) = scr[53:]
     rc = Sender()
     gain[0] = norm_gain[...]
     core = lax.axis_index("core")
@@ -953,27 +958,26 @@
     steps(oc, 0)
     ready("z")
 
-    streams = ((x_conv_ref, bxc), (d_x_ref, bdx), (x_pre_ref, bxp), (cols_ref, bcols), (d_cols_ref, bdc), (slope_ref, bslope))
+    streams = ((x_conv_ref, bxc), (d_x_ref, bdx), (x_pre_ref, bxp), (cols_ref, bcols), (d_cols_ref, bdc), (slope_ref, bslope), (leaving_ref, bleave))
 
     def load(m):
-        k = lax.rem(m, 2)
+        k = lax.rem(m, 3)
         return [pltpu.make_async_copy(src.at[m], dst.at[k], lsem.at[k, i]) for i, (src, dst) in enumerate(streams)]
 
-    for c in load(0):
+    for c in load(0) + load(1):
         c.start()
     gradient(l_n, l_n2, rhs_z, 1)
     steps(zc, 0)
     ready("s")
     for c in back:
         c.wait_recv()
-    load_in("end", (w_small_ref, w_small), (hid_ref, hid), (cot_ref, cot))
 
     def fifth_group(m):
-        k = lax.rem(m, 2)
-
-        @pl.when(m < GROUPS - 1)
+        k = lax.rem(m, 3)
+
+        @pl.when(m < GROUPS - 2)
         def _():
-            for c in load(m + 1):
+            for c in load(m + 2):
                 c.start()
 
         for c in load(m):
@@ -984,7 +988,7 @@
         last = cum[ROWS - 1 : ROWS]
         tail = jnp.exp(last - cum)
         weights = step * tail
-        wide = spread(weights)
+        wide = bleave[k].astype(F32)
         d_weighted = dot(bc_conv[:, :128], ds, (1, 1))
         d_b[...] += dot((xf * wide).astype(BF16), ds)
         dx = bdx[k] + wide * d_weighted
@@ -1014,13 +1018,19 @@
     steps(oc, 1)
     pl.loop(3, GROUPS)(fifth_group)
 
+    load_in("end", (w_small_ref, w_small), (hid_ref, hid), (cot_ref, cot))
+    for m in range(GROUPS):
+        halo_x[3 * m : 3 * m + 3] = halo_src[m, 0:3]
+    before = block_device(lax.rem(block + 7, 8))
+    halo = [rc(halo_x, halo_x_in, h_s.at[0], h_r.at[0], before)]
+
     d_bc = jnp.concatenate([d_bc_in[:, :128] + d_b[...], d_bc_in[:, 128:]], axis=1)
     ext = bc_pre[...]
     pre = conv_pre(ext, taps_bc[...])
     sig = jax.nn.sigmoid(pre)
     dp_bc = d_bc * (sig * (1.0 + pre * (1.0 - sig)))
-    halo_src[GROUPS] = jnp.concatenate([dp_bc[:8], jnp.zeros((8, 128), F32)], axis=1)
-    halo = rc(halo_src, halo_dst, h_s, h_r, block_device(lax.rem(block + 7, 8)))
+    halo_bc[...] = dp_bc[:8]
+    halo.append(rc(halo_bc, halo_bc_in, h_s.at[1], h_r.at[1], before))
     steps(zc, 1)
     zero8 = jnp.zeros((1, 256), F32)
     d_cum = jnp.concatenate([d_all[m][:, :HEADS] for m in range(GROUPS)] + [jnp.zeros((ROWS, 80), F32)], axis=1)
@@ -1041,11 +1051,15 @@
     vec_c = to_peers(rc, lambda p: v_all.at[p], v_in, vms, vmr, block)
     v_in[block] = v_all[block]
 
-    halo.wait_recv()
+    for c in halo:
+        c.wait_recv()
     inside = block < 7
+    halo_dst[...] = jnp.zeros_like(halo_dst)
+    for m in range(GROUPS):
+        halo_dst[m, 0:3] = jnp.where(inside, halo_x_in[3 * m : 3 * m + 3], 0.0)
 
     def below(k):
-        return jnp.where(inside, halo_dst[k], 0.0)
+        return halo_dst[k]
 
     def across(m):
         return pltpu.make_async_remote_copy(src_ref=rhs_x.at[0, m], dst_ref=rhs_x.at[1, m], send_sem=x_s.at[m],
@@ -1056,7 +1070,7 @@
         rhs_x[0, m, pl.ds(ROWS - 16, 16)] = (tails[m] + conv_transposed(ext, taps[m], 16)).astype(BF16)
         across(m).start()
 
-    d_bc = conv_transposed(jnp.concatenate([dp_bc, below(GROUPS)[:, :256]], axis=0), taps_bc[...])
+    d_bc = conv_transposed(jnp.concatenate([dp_bc, jnp.where(inside, halo_bc_in[...], 0.0)], axis=0), taps_bc[...])
     small2[0] = jnp.concatenate([d_bc, d_dt], axis=1).astype(BF16)
     small_c = rc(small2.at[0], small2.at[1], m_s, m_r, neighbour("core", 1))
     pl.loop(0, GROUPS)(fix)
@@ -1175,10 +1189,11 @@
         buf(3, 4, 2, 2, 4, 96), b(8, 96, ROWS), b(8, 96, ROWS), b(8, 96, ROWS), b(8, 96, ROWS),
         buf(2, GROUPS, ROWS), buf(2, GROUPS, ROWS), buf(2, GROUPS, ROWS), b(GROUPS, COLS, 128), b(GROUPS, COLS, 128),
         buf(WIDTH), b(ROWS, WIDTH), b(ROWS, WIDTH),
-        buf(GROUPS, 16, dtype=F32), buf(GROUPS + 1, 8, dtype=F32), buf(GROUPS + 1, 8, dtype=F32),
+        buf(GROUPS, 16, dtype=F32), buf(GROUPS, 8, dtype=F32), buf(GROUPS, 8, dtype=F32),
+        buf(24, dtype=F32), buf(24, dtype=F32), v(8, 256), v(8, 256),
         v(ROWS, WIDTH), buf(2, 2, WIDTH),
-        buf(2, ROWS), buf(2, ROWS, dtype=F32), buf(2, HALO + ROWS, dtype=F32), v(2, ROWS, 16), v(2, ROWS, 16),
-        buf(2, ROWS),
+        buf(3, ROWS), buf(3, ROWS, dtype=F32), buf(3, HALO + ROWS, dtype=F32), v(3, ROWS, 16), v(3, ROWS, 16),
+        buf(3, ROWS), buf(3, ROWS),
         v(ROWS, 128), v(GROUPS, ROWS, 16), buf(2, 4, 96), buf(2, ROWS), buf(3, 2, 96), buf(4, 96), buf(4, 96),
     ]
     scratch += [buf(GROUPS, 16, dtype=F32), buf(GROUPS, 16, dtype=F32), buf(16, dtype=F32), buf(3, 4, 16, dtype=F32)]
@@ -1186,15 +1201,15 @@
     scratch += [buf(2, 2, 4, 2, 2, SUB), buf(2, 2, 4, 4, SUB), buf(2, 2, 2, 2, 4, SUB)]
     scratch += [buf(2, 2, 4, 2, 2, 16), buf(2, 2, 4, 4, 16), buf(2, 2, 2, 2, 4, 16)]
     scratch += [buf(3, 3, 4, SUB), buf(3, 3, 4, SUB), buf(3, 3, 2, 2, SUB), buf(9, 3, SUB)]
-    scratch += [sem((27,)), sem((90,)), sem((8,)), sem((8,)), sem((8,)), sem((8,)), sem, sem, sem, sem, sem((10,)), sem((10,)), sem((8,)), sem((8,)),
-                sem((3,)), sem((9,)), sem((3,)), sem((12,)), sem((2, 2)), sem((2, 6)), sem((13,)), pltpu.SemaphoreType.REGULAR]
-    names = ("x_conv", "d_x", "x_pre", "cols", "d_cols", "conv_slope", "cot_t", "cot_t2", "out_in", "out_in2", "normed_t", "normed_t2", "d_z",
+    scratch += [sem((27,)), sem((90,)), sem((8,)), sem((8,)), sem((8,)), sem((8,)), sem((2,)), sem((2,)), sem, sem, sem((10,)), sem((10,)), sem((8,)), sem((8,)),
+                sem((3,)), sem((9,)), sem((3,)), sem((12,)), sem((2, 2)), sem((3, 7)), sem((13,)), pltpu.SemaphoreType.REGULAR]
+    names = ("x_conv", "d_x", "x_pre", "cols", "d_cols", "conv_slope", "leaving", "cot_t", "cot_t2", "out_in", "out_in2", "normed_t", "normed_t2", "d_z",
              "d_z2", "state", "d_state")
     return pl.pallas_call(
         backward_kernel,
         out_shape=(sds(96, 2, COLS), sds(96, COLS), sds(96, 256), sds(HEADS, 96), sds(5, COLS), sds(5, 256), sds(HEADS), sds(HEADS),
                    sds(HEADS), sds(COLS), sds(WIDTH), sds(ROWS, WIDTH)),
-        in_specs=[hbm] * 20 + [vmem] * 10,
+        in_specs=[hbm] * 21 + [vmem] * 10,
         out_specs=(vmem,) * 12,
         scratch_shapes=scratch,
         compiler_params=pltpu.CompilerParams(collective_id=1, has_side_effects=True, vmem_limit_bytes=63 * 2**20),

time: 211 us -> 207 us (0.981)
  Pallas kernels: 210 us -> 206 us
    pallas_call x1, Pallas kernels: 119 us -> 116 us  [forward(): pl.pallas_call(forward_kernel, out_shape=(sds(2, 4, 2, 2, 4, 2, 96, COLS,...]
where the time goes in v7:
time: 207 us
  Pallas kernels  206 us (100%)
    pallas_call x1, Pallas kernels, forward(): pl.pallas_call(forward_kernel, out_shape=(sds(2, 4, 2, 2, 4, 2, 96, COLS,...  116 us
    pallas_call x1, Pallas kernels, backward(): pl.pallas_call(backward_kernel, out_shape=(sds(96, 2, COLS), sds(96, COLS...  87 us

profile of v7, /device:TPU:0, one launch (start us, length us, event | category | flops | bytes accessed | tf_op | source)
XLA Modules:
  0.0 207.0 jit_solution(5273286205896398430)
XLA Ops:
  0.6 115.9 %forward_between_devices.1 = (bf16[2,4,2,2,4,2,96,384]{7,6,5,4,3,2,1,0:T(8,128)(2,1)}, bf16[2,4,2,96,384]{4,3,2,1,0:T(8,128)(2,1)}, f32[8,16,384]{2,1,0:T(8,128)...) custom-call(bf16[96,2,384]{2,1,0:T(2,128)(2,1)} %zx_ref.1, ...), custom_call_target="tpu_custom_call" | custom-call | tf_op jit(solution)/shard_map/forward_between_devices/pallas_call | solution.py:700
  116.5 87.0 %backward_between_devices.1 = (f32[96,2,384]{2,1,0:T(2,128)}, f32[96,384]{1,0:T(8,128)}, f32[96,256]{1,0:T(8,128)}, f32[6,96]{1,0:T(8,128)}, f32[5,384]{1,0:T(8,...) custom-call(bf16[2,8,1536,384]{3,2,1,0:T(8,128)(2,1)} %bitcast.6, ...), custom_call_target="tpu_custom_call" | custom-call | tf_op jit(solution)/shard_map/backward_between_devices/pallas_call | solution.py:1208
  203.5 3.2 %results.1 = (bf16[256,1536]{1,0:T(8,128)(2,1)}, f32[256,1536]{1,0:T(8,128)}, f32[1536]{0:T(1024)}, f32[96,2,384]{2,1,0:T(2,128)}, f32[96,256]{1,0:T(8,128)}, /*...) custom-call(bf16[256,1536]{1,0:T(8,128)(2,1)} %get-tuple-element.66., ...), custom_call_target="tpu_custom_call" | custom-call | tf_op jit(solution)/shard_map/results/pallas_call | solution.py:1235

commit v8 on v7

--- a/solution.py
+++ b/solution.py
@@ -254,7 +254,7 @@
      result, out_in, d_z, gain_part, skip_part, d_cols, d_bc, conv_slope, leaving,
      cot, normed, halo, dt_own, small_all, zb, yb, uppers, lowers, wx, wo, gram, d_gram, local, rec_a, out_b, dec_own, square,
      scales, acc, d_c, pk_ref, gain, zx, grown, entered,
-     ts, tr, cs, cr, bs, br, qs, qr, es, er, fs, fr, ds, dr, hs, hr, lsem, wsem, osem, xs, xr) = scr
+     ts, tr, cs, cr, bs, br, qs, qr, es, er, fs, fr, ds, dr, hs, hr, lsem, wsem, osem, dsem, xs, xr) = scr
     rc = Sender()
     me = my_place()
     core = lax.axis_index("core")
@@ -613,6 +613,9 @@
     out(d_z, d_z_out)
     out(gain_part, gain_part_out)
 
+    def d_cols_copy(m):
+        return pltpu.make_async_copy(d_cols.at[m], d_cols_out.at[m], dsem.at[m])
+
     def d_x_copy(m):
         return pltpu.make_async_copy(zb.at[m], d_x_out.at[m], wsem.at[m])
 
@@ -647,23 +650,25 @@
         zb[m] = jnp.concatenate(parts, axis=0).T + spread(pk[m, 14:15, 0:8]) * dy
         d_x_copy(m).start()
         d_cols[m] = jnp.concatenate([d_cum - sums, sums], axis=1)
-
-    pl.loop(0, GROUPS)(inner_group)
+        d_cols_copy(m).start()
+
     out(skip_part, skip_part_out)
-    out(d_cols, d_cols_out)
+    pl.loop(0, GROUPS - 1)(inner_group)
+    exchanged(local, es, er)
+    carry(range(BLOCKS - 1, -1, -1))
+    out(out_b, d_state_out)
+    pl.loop(GROUPS - 1, GROUPS)(inner_group)
     dg = jnp.where(triangle(False), d_gram[...], 0.0).astype(BF16)
     d_bc[:, :128] = dot(dg, c_mat, (0, 0))
     d_bc[:, 128:] = d_c[...] + dot(dg, bc_conv[:, :128])
     out(d_bc, d_bc_out)
-    exchanged(local, es, er)
-    carry(range(BLOCKS - 1, -1, -1))
-    out(out_b, d_state_out)
     for c in across:
         c.wait_recv()
     for c in writes:
         c.wait()
     for m in range(GROUPS):
         d_x_copy(m).wait()
+        d_cols_copy(m).wait()
     rc.all_sent()
 
 
@@ -712,7 +717,7 @@
             b(GROUPS, COLS, 128), b(GROUPS, COLS, 128), b(GROUPS, COLS, 128), v(GROUPS, 8, 128),
             v(ROWS, 128), v(ROWS, 8), v(ROWS, WIDTH), v(ROWS, 128), v(16, COLS), v(1, WIDTH), b(2, 96, COLS), v(*groups), v(*groups),
             sem((27,)), sem((90,)), sem((36,)), sem((36,)), sem((18,)), sem((18,)), sem((8,)), sem((8,)), sem((8,)), sem((8,)),
-            sem((8,)), sem((8,)), sem((8,)), sem((8,)), sem, sem, sem((7,)), sem((GROUPS,)), sem((len(RESULTS),)), sem((4,)),
+            sem((8,)), sem((8,)), sem((8,)), sem((8,)), sem, sem, sem((7,)), sem((GROUPS,)), sem((len(RESULTS),)), sem((GROUPS,)), sem((4,)),
             sem((4,)),
         ],
         compiler_params=pltpu.CompilerParams(collective_id=0, has_side_effects=True, vmem_limit_bytes=63 * 2**20),

time: 207 us -> 208 us (level)
  no operation moved by 1% of the time
where the time goes in v8:
time: 208 us
  Pallas kernels  207 us (100%)
    pallas_call x1, Pallas kernels, forward(): pl.pallas_call(forward_kernel, out_shape=(sds(2, 4, 2, 2, 4, 2, 96, COLS,...  116 us
    pallas_call x1, Pallas kernels, backward(): pl.pallas_call(backward_kernel, out_shape=(sds(96, 2, COLS), sds(96, COLS...  88 us

profile of v8, /device:TPU:0, one launch (start us, length us, event | category | flops | bytes accessed | tf_op | source)
XLA Modules:
  0.0 207.8 jit_solution(2240625225938087692)
XLA Ops:
  0.6 115.7 %forward_between_devices.1 = (bf16[2,4,2,2,4,2,96,384]{7,6,5,4,3,2,1,0:T(8,128)(2,1)}, bf16[2,4,2,96,384]{4,3,2,1,0:T(8,128)(2,1)}, f32[8,16,384]{2,1,0:T(8,128)...) custom-call(bf16[96,2,384]{2,1,0:T(2,128)(2,1)} %zx_ref.1, ...), custom_call_target="tpu_custom_call" | custom-call | tf_op jit(solution)/shard_map/forward_between_devices/pallas_call | solution.py:705
  116.3 88.0 %backward_between_devices.1 = (f32[96,2,384]{2,1,0:T(2,128)}, f32[96,384]{1,0:T(8,128)}, f32[96,256]{1,0:T(8,128)}, f32[6,96]{1,0:T(8,128)}, f32[5,384]{1,0:T(8,...) custom-call(bf16[2,8,1536,384]{3,2,1,0:T(8,128)(2,1)} %bitcast.6, ...), custom_call_target="tpu_custom_call" | custom-call | tf_op jit(solution)/shard_map/backward_between_devices/pallas_call | solution.py:1213
  204.3 3.2 %results.1 = (bf16[256,1536]{1,0:T(8,128)(2,1)}, f32[256,1536]{1,0:T(8,128)}, f32[1536]{0:T(1024)}, f32[96,2,384]{2,1,0:T(2,128)}, f32[96,256]{1,0:T(8,128)}, /*...) custom-call(bf16[256,1536]{1,0:T(8,128)(2,1)} %get-tuple-element.66., ...), custom_call_target="tpu_custom_call" | custom-call | tf_op jit(solution)/shard_map/results/pallas_call | solution.py:1240
